TPU v7x, 32 devices: a whole 2x2x4 slice. The times are simulated.
32 devices in a mesh: row: 8 (over z, y), col: 4 (over x, core).
Axes of the slice: x: 2, y: 2, z: 4, core: 2. Of those that a mesh axis runs over, the one named last changes fastest.
Arguments:
- queries: bfloat16 [768, 8192], P('col', 'row'), may hold values from -16 to 16
- key_rows: bfloat16 [768, 8192], P('col', 'row'), may hold values from -16 to 16
- values: bfloat16 [768, 8192], P('col', 'row'), may hold values from -6 to 6
- block_lists: int32 [32, 16], P('row'), may hold values from 0 to 31, as said below
- counts: int32 [32], P('row'), may hold values from 1 to 16, as said below
- out_proj: bfloat16 [768, 768], P('col'), may hold values from -0.21875 to 0.21875
- stream: bfloat16 [8192, 768], P('row'), may hold values from -6 to 6
- norm_gain: float32 [768], replicated, may hold values from 0.1 to 1.9
- head_proj: bfloat16 [96, 768], replicated, may hold values from -0.21875 to 0.21875
- patches: float32 [8192, 48], P('row'), may hold values from -6 to 6
- token_order: int32 [8192], P('row'), may hold values from 0 to 8191, as said below
- cotangent: float32 [8192, 48], P('row'), may hold values from -6 to 6
Outputs:
- latent_out: float32 [8192, 48], P('row')
- grad_queries: bfloat16 [768, 8192], P('col', 'row')
- grad_keys: bfloat16 [768, 8192], P('col', 'row')
- grad_values: bfloat16 [768, 8192], P('col', 'row')
Inputs may be any that keep to these rules, and one draw needn't show every extreme that they name: `block_lists`: entry 0 of row b is b; entries 1 to counts[b] - 1 are distinct blocks from b - 15 to b - 1; later entries equal b. counts[b] is at most b + 1; every block whose index is 31 modulo 32 has 16. A permutation; token_order[t] lies in block 31 - t // 256.
All inputs are finite; a program needn't handle non-finite values.
Results may differ from a plain program's by a relative error of at most 0.012.
The roundings to bfloat16 on the way count: a program that leaves them out, or rounds other values in their place, can miss the bound.
Values may be sent and summed in bfloat16 or wider, within the bound.
No kernel may reach another device: no remote copies, remote signals or barrier semaphores. Data moves between devices by JAX's collectives and lax.ppermute only.
A program may use at most 128 MiB of HBM per device.

v0:
```python
import functools

import jax
import jax.numpy as jnp
from jax import lax
from jax.experimental import pallas as pl
from jax.experimental.pallas import tpu as pltpu
from jax.sharding import PartitionSpec as P

HEAD_DIM = 64
BLOCK = 256
LIST = 16
REACH = 4

NEG = -1e30
EPS = 1e-05
SCALE = HEAD_DIM ** (-0.5)
F32 = jnp.float32
BF16 = jnp.bfloat16


def dot(a, b, ca=1, cb=0):
    return lax.dot_general(a, b, (((ca,), (cb,)), ((), ())), preferred_element_type=F32)


def vmem(count):
    return [pl.BlockSpec(memory_space=pltpu.VMEM)] * count


def smem(count):
    return [pl.BlockSpec(memory_space=pltpu.SMEM)] * count


def hop(array, by):
    size = lax.axis_size("row")
    pairs = [(i, i + by) for i in range(size) if 0 <= i + by < size]
    return lax.ppermute(array, "row", pairs)


def mate(array):
    return lax.ppermute(array, "row", [(i, i ^ 1) for i in range(lax.axis_size("row"))])


def upward(array):
    return lax.ppermute(array, "row", [(i, i + 1) for i in range(0, lax.axis_size("row"), 2)])


def downward(array):
    return lax.ppermute(array, "row", [(i + 1, i) for i in range(0, lax.axis_size("row"), 2)])


def mirror(array):
    size = lax.axis_size("row")
    return lax.ppermute(array, "row", [(i, size - 1 - i) for i in range(size)])


def across(array, bits):
    return lax.ppermute(array, "col", [(i, i ^ bits) for i in range(lax.axis_size("col"))])


def split3(x):
    hi = x.astype(BF16)
    rest = x - hi.astype(F32)
    mid = rest.astype(BF16)
    low = (rest - mid.astype(F32)).astype(BF16)
    return hi, mid, low


def picked(place_ref, order_ref, blocks):
    cols = pl.ds(pl.multiple_of((blocks - 1 - place_ref[1]) * BLOCK, BLOCK), BLOCK)
    rows = lax.broadcasted_iota(jnp.int32, (BLOCK, BLOCK), 0)
    return (rows == lax.rem(order_ref[:, cols], BLOCK)).astype(BF16), cols


def scatter_kernel(place_ref, order_ref, x_ref, o_ref):
    pick, cols = picked(place_ref, order_ref, x_ref.shape[1] // BLOCK)
    hi, mid, low = split3(x_ref[:, cols])
    o_ref[...] = (dot(hi, pick, 1, 1) + dot(mid, pick, 1, 1)) + dot(low, pick, 1, 1)


def gather_kernel(place_ref, order_ref, x_ref, o_ref):
    pick, _ = picked(place_ref, order_ref, order_ref.shape[1] // BLOCK)
    hi, mid, low = split3(x_ref[...])
    o_ref[...] = (dot(hi, pick) + dot(mid, pick)) + dot(low, pick)


def permuted(kernel, place, order, x):
    return pl.pallas_call(
        kernel,
        out_shape=jax.ShapeDtypeStruct((x.shape[0], BLOCK), F32),
        in_specs=smem(1) + vmem(2),
        out_specs=vmem(1)[0],
    )(place, order, x)


def assemble_kernel(place_ref, p0, p1, p2, p3, o_ref):
    blocks = o_ref.shape[1] // BLOCK
    for k, ref in enumerate((p0, p1, p2, p3)):
        at = (blocks - 1 - jnp.bitwise_xor(place_ref[1], k)) * BLOCK
        o_ref[:, pl.ds(pl.multiple_of(at, BLOCK), BLOCK)] = ref[...]


def assembled(place, pieces, tokens):
    return pl.pallas_call(
        assemble_kernel,
        out_shape=jax.ShapeDtypeStruct((pieces[0].shape[0], tokens), F32),
        in_specs=smem(1) + vmem(4),
        out_specs=vmem(1)[0],
    )(place, *pieces)


def live_slots(lists_ref, counts_ref, place_ref, regions, blocks, first, items_ref):
    row = place_ref[0]
    odd = lax.rem(row, 2)
    wanted = [jnp.where(odd == 1, region[1], region[0]) for region in regions]
    found = []
    for b in range(blocks):

        def look(j, count, b=b):
            block = lists_ref[b, j]
            distance = row - lax.div(block, blocks)
            slot, hit = 0, 0
            for r, want in enumerate(wanted):
                here = (distance == want).astype(jnp.int32)
                slot = slot + here * r * blocks
                hit = hit + here
            items_ref[b * LIST + count] = slot + lax.rem(block, blocks)
            return count + hit

        found.append(lax.fori_loop(first, counts_ref[b], look, 0))
    return found


def staged(place_ref, regions, refs, copy):
    odd = lax.rem(place_ref[0], 2)
    at = 0
    for r, region in enumerate(regions):
        if region[2] == "both":
            copy(r, refs[at])
            at += 1
            continue
        for parity in (0, 1):
            if region[parity] >= 0:
                pl.when(odd == parity)(lambda r=r, ref=refs[at]: copy(r, ref))
                at += 1


def region_inputs(regions):
    return sum(1 if region[2] == "both" else (region[0] >= 0) + (region[1] >= 0)
               for region in regions)


def causal():
    return (lax.broadcasted_iota(jnp.int32, (BLOCK, BLOCK), 0)
            <= lax.broadcasted_iota(jnp.int32, (BLOCK, BLOCK), 1))


def head_rows(h):
    return slice(h * HEAD_DIM, (h + 1) * HEAD_DIM)


def forward_kernel(regions, opening, closing, lists_ref, counts_ref, place_ref, q_ref, *refs):
    heads = q_ref.shape[0] // HEAD_DIM
    blocks = q_ref.shape[1] // BLOCK
    refs = list(refs)
    slabs = [refs.pop(0) for _ in range(region_inputs(regions))]
    if not opening:
        acc_in, stat_in = refs.pop(0), refs.pop(0)
    if closing:
        att_ref, lse_ref = refs.pop(0), refs.pop(0)
        key_rows, value_cols, items, acc_ref = refs
    else:
        acc_ref, stat_ref = refs.pop(0), refs.pop(0)
        key_rows, value_cols, items = refs

    def copy(r, ref):
        for b in range(blocks):
            slot, cols = r * blocks + b, slice(b * BLOCK, (b + 1) * BLOCK)
            value_cols[slot] = ref[1, :, cols]
            for h in range(heads):
                key_rows[slot, h] = ref[0, head_rows(h), cols].T

    staged(place_ref, regions, slabs, copy)
    found = live_slots(
        lists_ref, counts_ref, place_ref, regions, blocks, 1 if opening else 0, items)
    acc_ref[...] = jnp.zeros_like(acc_ref) if opening else acc_in[...]
    keep = causal()

    for b in range(blocks):
        cols = slice(b * BLOCK, (b + 1) * BLOCK)
        queries = [q_ref[head_rows(h), cols] * BF16(SCALE) for h in range(heads)]

        def entry(slot, state, masked, cols=cols, queries=queries):
            out = []
            for h in range(heads):
                rows = head_rows(h)
                top, total = state[2 * h], state[2 * h + 1]
                scores = dot(key_rows[slot, h], queries[h])
                if masked:
                    scores = jnp.where(keep, scores, NEG)
                newest = jnp.maximum(top, jnp.max(scores, axis=0, keepdims=True))
                weights = jnp.exp(scores - newest)
                fade = jnp.exp(top - newest)
                total = total * fade + jnp.sum(weights, axis=0, keepdims=True)
                acc_ref[rows, cols] = acc_ref[rows, cols] * fade + dot(
                    value_cols[slot, rows], weights.astype(BF16))
                out += [newest, total]
            return tuple(out)

        if opening:
            state = (jnp.full((1, BLOCK), NEG, F32), jnp.zeros((1, BLOCK), F32)) * heads
            state = entry(b, state, True)
        else:
            state = tuple(stat_in[i, :, cols] for i in range(2 * heads))
        state = lax.fori_loop(
            0, found[b], lambda i, s: entry(items[b * LIST + i], s, False), state)
        for h in range(heads):
            if closing:
                att_ref[head_rows(h), cols] = (
                    acc_ref[head_rows(h), cols] / state[2 * h + 1]).astype(BF16)
                lse_ref[h, :, cols] = state[2 * h] + jnp.log(state[2 * h + 1])
            else:
                stat_ref[2 * h, :, cols] = state[2 * h]
                stat_ref[2 * h + 1, :, cols] = state[2 * h + 1]


def forward(tables, queries, regions, slabs, state=None, closing=False, pairs=1):
    width, tokens = queries.shape
    heads = width // HEAD_DIM
    slots = len(regions) * (tokens // BLOCK)
    running = (jax.ShapeDtypeStruct((width, tokens), F32),
               jax.ShapeDtypeStruct((2 * heads, 1, tokens), F32))
    result = (jax.ShapeDtypeStruct((width, tokens), BF16),
              jax.ShapeDtypeStruct((heads, 1, tokens), F32))
    state = () if state is None else state
    return pl.pallas_call(
        functools.partial(forward_kernel, regions, not state, closing),
        out_shape=result if closing else running,
        in_specs=smem(3) + vmem(1 + len(slabs) + len(state)),
        out_specs=tuple(vmem(2)),
        scratch_shapes=[
            pltpu.VMEM((slots, heads, BLOCK, HEAD_DIM), BF16),
            pltpu.VMEM((slots, width, BLOCK), BF16),
            pltpu.SMEM((tokens // BLOCK * LIST,), jnp.int32),
        ] + [pltpu.VMEM((width, tokens), F32)] * closing,
        compiler_params=pltpu.CompilerParams(vmem_limit_bytes=48 << 20),
        cost_estimate=pl.CostEstimate(
            flops=pairs * 10 ** 9, bytes_accessed=6 << 20, transcendentals=pairs * 10 ** 5),
    )(*tables, queries, *slabs, *state)


def flow_kernel(place_ref, a0, a1, a2, a3, w0, w1, w2, w3, stream_ref, gain_ref, head_ref,
                patch_ref, grad_ref, latent_ref, g0, g1, g2, g3, wide, weights):
    width = a0.shape[0]
    channels = patch_ref.shape[0]
    cols = pl.ds(pl.multiple_of(place_ref[1] * BLOCK, BLOCK), BLOCK)
    for k, (part, weight) in enumerate(zip((a0, a1, a2, a3), (w0, w1, w2, w3))):
        wide[k * width:(k + 1) * width] = part[...]
        weights[k * width:(k + 1) * width] = weight[...]
    hidden = stream_ref[cols].astype(F32) + dot(wide[...], weights[...], 0, 0)
    inverse = lax.rsqrt(jnp.mean(hidden * hidden, axis=-1, keepdims=True) + EPS)
    gain = gain_ref[...]
    normed = (hidden * inverse * gain).astype(BF16)
    params = dot(head_ref[...], normed, 1, 1)
    factor = jnp.exp(-params[channels:])
    latent = (patch_ref[:, cols] - params[:channels]) * factor
    latent_ref[...] = latent
    grad = grad_ref[...]
    grad_params = jnp.concatenate([-grad * factor, -grad * latent - 1.0], axis=0).astype(BF16)
    gained = dot(grad_params, head_ref[...], 0, 0) * gain
    grad_hidden = (
        inverse * gained
        - hidden * inverse ** 3 * jnp.mean(hidden * gained, axis=-1, keepdims=True)
    ).astype(BF16)
    wide[...] = dot(weights[...], grad_hidden, 1, 1).astype(BF16)
    for k, ref in enumerate((g0, g1, g2, g3)):
        ref[...] = wide[k * width:(k + 1) * width]


def flow(place, parts, weights, stream, gain, head_proj, patches, grad):
    width = parts[0].shape[0]
    return pl.pallas_call(
        flow_kernel,
        out_shape=(jax.ShapeDtypeStruct(grad.shape, F32),)
        + (jax.ShapeDtypeStruct((width, BLOCK), BF16),) * 4,
        in_specs=smem(1) + vmem(13),
        out_specs=tuple(vmem(5)),
        scratch_shapes=[
            pltpu.VMEM((4 * width, BLOCK), BF16), pltpu.VMEM((4 * width, stream.shape[1]), BF16)],
        compiler_params=pltpu.CompilerParams(vmem_limit_bytes=48 << 20),
    )(place, *parts, *weights, stream, gain, head_proj, patches, grad)


def backward_kernel(regions, diagonal, last, lists_ref, counts_ref, place_ref, q_ref, att_ref,
                    lse_ref, g0, g1, g2, g3, *refs):
    heads = q_ref.shape[0] // HEAD_DIM
    blocks = q_ref.shape[1] // BLOCK
    refs = list(refs)
    slabs = [refs.pop(0) for _ in range(region_inputs(regions))]
    dq_in = None if len(refs) < 10 + len(regions) else refs.pop(0)
    dq_ref = refs.pop(0)
    outs = [refs.pop(0) for _ in regions]
    key_rows, value_rows, key_cols, grad_cols, grad_keys, grad_values, items, acc_ref = refs
    me = place_ref[1]
    for k, ref in enumerate((g0, g1, g2, g3)):
        grad_cols[jnp.bitwise_xor(me, k)] = ref[...]

    def copy(r, ref):
        for b in range(blocks):
            slot, cols = r * blocks + b, slice(b * BLOCK, (b + 1) * BLOCK)
            key_cols[slot] = ref[0, :, cols]
            for h in range(heads):
                key_rows[slot, h] = ref[0, head_rows(h), cols].T
                value_rows[slot, h] = ref[1, head_rows(h), cols].T

    staged(place_ref, regions, slabs, copy)
    grad_keys[...] = jnp.zeros_like(grad_keys)
    grad_values[...] = jnp.zeros_like(grad_values)
    found = live_slots(
        lists_ref, counts_ref, place_ref, regions, blocks, 1 if diagonal else 0, items)
    acc_ref[...] = jnp.zeros_like(acc_ref) if dq_in is None else dq_in[...]
    keep = causal()

    for b in range(blocks):
        cols = slice(b * BLOCK, (b + 1) * BLOCK)
        queries, grads, sums, tops = [], [], [], []
        for h in range(heads):
            rows = head_rows(h)
            queries.append(q_ref[rows, cols] * BF16(SCALE))
            grads.append(grad_cols[b, rows])
            sums.append(jnp.sum(grads[h].astype(F32) * att_ref[rows, cols].astype(F32),
                                axis=0, keepdims=True))
            tops.append(lse_ref[h, :, cols])

        def entry(slot, masked, cols=cols, queries=queries, grads=grads, sums=sums, tops=tops):
            for h in range(heads):
                rows = head_rows(h)
                scores = dot(key_rows[slot, h], queries[h])
                if masked:
                    scores = jnp.where(keep, scores, NEG)
                probs = jnp.exp(scores - tops[h])
                grad_scores = (
                    probs * (dot(value_rows[slot, h], grads[h]) - sums[h])).astype(BF16)
                acc_ref[rows, cols] += dot(key_cols[slot, rows], grad_scores)
                grad_keys[slot, rows] += dot(queries[h], grad_scores, 1, 1)
                grad_values[slot, rows] += dot(grads[h], probs.astype(BF16), 1, 1)

        if diagonal:
            entry(b, True)

        @pl.loop(0, found[b])
        def _(i, b=b, entry=entry):
            entry(items[b * LIST + i], False)

    if last:
        dq_ref[...] = (acc_ref[...] * SCALE).astype(BF16)
    else:
        dq_ref[...] = acc_ref[...]
    for r, ref in enumerate(outs):
        for b in range(blocks):
            cols = slice(b * BLOCK, (b + 1) * BLOCK)
            ref[0, :, cols] = grad_keys[r * blocks + b].astype(ref.dtype)
            ref[1, :, cols] = grad_values[r * blocks + b].astype(ref.dtype)


def backward(tables, queries, attended, lse, grads, regions, slabs, dq=None, last=False, pairs=1):
    width, tokens = queries.shape
    heads, blocks = width // HEAD_DIM, tokens // BLOCK
    slots = len(regions) * blocks
    diagonal = regions[0][0] == 0
    given = () if dq is None else (dq,)
    return pl.pallas_call(
        functools.partial(backward_kernel, regions, diagonal, last),
        out_shape=(jax.ShapeDtypeStruct((width, tokens), BF16 if last else F32),)
        + (jax.ShapeDtypeStruct((2, width, tokens), F32 if diagonal else BF16),) * len(regions),
        in_specs=smem(3) + vmem(7 + len(slabs) + len(given)),
        out_specs=tuple(vmem(1 + len(regions))),
        scratch_shapes=[
            pltpu.VMEM((slots, heads, BLOCK, HEAD_DIM), BF16),
            pltpu.VMEM((slots, heads, BLOCK, HEAD_DIM), BF16),
            pltpu.VMEM((slots, width, BLOCK), BF16),
            pltpu.VMEM((blocks, width, BLOCK), BF16),
            pltpu.VMEM((slots, width, BLOCK), F32),
            pltpu.VMEM((slots, width, BLOCK), F32),
            pltpu.SMEM((blocks * LIST,), jnp.int32),
            pltpu.VMEM((width, tokens), F32),
        ],
        compiler_params=pltpu.CompilerParams(vmem_limit_bytes=48 << 20),
        cost_estimate=pl.CostEstimate(
            flops=pairs * 10 ** 9, bytes_accessed=8 << 20, transcendentals=pairs * 10 ** 5),
    )(*tables, queries, attended, lse, *grads, *slabs, *given)


def on_device(queries, key_rows, values, block_lists, counts, out_proj, stream, norm_gain,
              head_proj, patches, token_order, cotangent):
    width, tokens = queries.shape
    cols = lax.axis_size("col")
    row, col = lax.axis_index("row"), lax.axis_index("col")
    odd = row % 2 == 1
    place = jnp.stack([row, col]).astype(jnp.int32)

    tables = (block_lists, counts, place)
    own = jnp.stack([key_rows, values])
    slab2 = hop(own, 2)
    state = forward(tables, queries, [(0, 0, "both")], [own], pairs=1)
    *state, slab2, out_proj = lax.optimization_barrier([*state, slab2, out_proj])
    up1 = upward(own)
    slab4 = hop(slab2, 2)
    up2 = upward(slab2)
    down1 = downward(slab2)

    order = token_order.reshape(1, tokens)
    grad_latent = mirror(permuted(scatter_kernel, place, order, cotangent.T))
    weights = [out_proj] + [across(out_proj, k) for k in range(1, cols)]

    state = forward(tables, queries, [(2, 2, "both")], [slab2], tuple(state), pairs=1)
    *state, slab4 = lax.optimization_barrier([*state, slab4])
    down2 = downward(slab4)
    state = forward(tables, queries, [(1, 1, "each")], [down1, up1], tuple(state), pairs=1)
    state = forward(tables, queries, [(4, 4, "both"), (-1, 3, "one")], [slab4, up2], state,
                    pairs=1)
    attended, lse = forward(tables, queries, [(3, -1, "one")], [down2], state, True, pairs=1)

    def block_of(array, b):
        return lax.dynamic_slice_in_dim(array, b * BLOCK, BLOCK, 1)

    parts = [block_of(attended, col)] + [
        across(block_of(attended, jnp.bitwise_xor(col, k)), k) for k in range(1, cols)]
    latent, *grads = flow(
        place, parts, weights, stream, norm_gain.reshape(1, -1), head_proj, patches.T,
        grad_latent)
    *grads, mirrored = lax.optimization_barrier(
        [grads[0]] + [across(grads[k], k) for k in range(1, cols)] + [mirror(latent)])

    shared = (tables, queries, attended, lse, grads)
    grad_queries, part3, part4 = backward(
        *shared, [(3, 3, "each"), (4, 4, "both")], [down2, up2, slab4], pairs=1)
    from3 = mate(part3)
    reordered = permuted(gather_kernel, place, order, mirrored)
    grad_queries, reordered = lax.optimization_barrier((grad_queries, reordered))
    pieces = [reordered] + [across(reordered, k) for k in range(1, cols)]
    grad_queries, part1 = backward(
        *shared, [(1, 1, "each")], [down1, up1], grad_queries, pairs=1)
    from1 = mate(part1)
    zero = jnp.zeros_like(part1)
    far = part4 + jnp.where(odd, from3, zero)
    grad_queries, far, *pieces = lax.optimization_barrier([grad_queries, far] + pieces)
    far = hop(far, -2)
    latent_out = assembled(place, pieces, tokens).T
    grad_queries, part2 = backward(*shared, [(2, 2, "both")], [slab2], grad_queries, pairs=1)
    near = part2 + jnp.where(odd, from1, from3) + far
    grad_queries, near = lax.optimization_barrier((grad_queries, near))
    near = hop(near, -2)
    grad_queries, own_grad = backward(
        *shared, [(0, 0, "both")], [own], grad_queries, True, pairs=1)
    own_grad = own_grad + jnp.where(odd, zero, from1).astype(F32) + near.astype(F32)
    own_grad = own_grad.astype(BF16)
    return (latent_out, grad_queries, own_grad[0], own_grad[1])


def solution(mesh):
    return jax.shard_map(
        on_device,
        mesh=mesh,
        in_specs=(
            P("col", "row"),
            P("col", "row"),
            P("col", "row"),
            P("row", None),
            P("row"),
            P("col", None),
            P("row", None),
            P(),
            P(),
            P("row", None),
            P("row"),
            P("row", None),
        ),
        out_specs=(P("row", None), P("col", "row"), P("col", "row"), P("col", "row")),
        check_vma=False,
    )
```

profile of v0, /device:TPU:8, one launch (start us, length us, event | category | flops | bytes accessed | tf_op | source)
XLA Modules:
  0.0 224.3 jit_solution(17508494212941439032)
XLA Ops:
  0.7 1.2 pad_maximum_fusion.refs_0_
  1.9 3.5 %collective-permute-start = (bf16[2,192,1024]{2,1,0:T(8,128)(2,1)S(1)}, bf16[2,192,1024]{2,1,0:T(8,128)(2,1)S(1)}, u32[]{:S(2)}, u32[]{:S(2)}) collective-permute-start(bf16[2,192,1024]{2,1,0:T(8,128)(2,1)S(1)} %pad_maximum_fusion.refs_0_), channel_id=1, source_target_pairs={{0,8},{4,12},{8,16},{12,20},{16,24},{20,28},{1,9},{5,13},{9,17},{1... | collective-permute-start | bytes 2359304 | tf_op jit(solution)/shard_map/ppermute | solution.py:37
  5.4 0.1 pad_add_fusion.place_ref
  5.5 10.2 %shard_map.147 = (f32[192,1024]{1,0:T(8,128)S(1)}, f32[6,1,1024]{2,1,0:T(1,128)S(1)}) custom-call(s32[4,16]{1,0:T(4,128)S(1)} %copy-done.14, s32[4]{0:T(128)S(1)} %copy-done.15, s32[2]{0:T(128)S(1)} %pad_add_fusion.place_ref, bf16[192,1024]{1,0:T(8,128)(2,1)S(1)} %copy-done.9, bf16[2,192,1024]{2,1,0:T(8,128)(2,1)S(1)} %pad_maximum_fusion.refs_0_), custom_call_target="tpu_custom_call" | custom-call | flops 1000000000 | bytes 6291456 | tf_op jit(solution)/shard_map/pallas_call | solution.py:236
  15.7 7.3 %collective-permute-done.refs_0_ = bf16[2,192,1024]{2,1,0:T(8,128)(2,1)S(1)} collective-permute-done((bf16[2,192,1024]{2,1,0:T(8,128)(2,1)S(1)}, bf16[2,192,1024]{2,1,0:T(8,128)(2,1)S(1)}, u32[]{:S(2)}, u32[]{:S(2)}) %collective-permute-start) | collective-permute-done | bytes 786464 | tf_op jit(solution)/shard_map/ppermute | solution.py:37
  23.1 3.6 %collective-permute-start.1 = (bf16[2,192,1024]{2,1,0:T(8,128)(2,1)S(1)}, bf16[2,192,1024]{2,1,0:T(8,128)(2,1)}, u32[]{:S(2)}, u32[]{:S(2)}) collective-permute-start(bf16[2,192,1024]{2,1,0:T(8,128)(2,1)S(1)} %collective-permute-done.refs_0_), channel_id=1, source_target_pairs={{0,8},{4,12},{8,16},{12,20},{16,24},{20,28},{1,9},{5,13},{9,17},{1... | collective-permute-start | bytes 2359304 | tf_op jit(solution)/shard_map/ppermute | solution.py:37
  26.7 4.3 %collective-permute-start.5 = (bf16[2,192,1024]{2,1,0:T(8,128)(2,1)S(1)}, bf16[2,192,1024]{2,1,0:T(8,128)(2,1)}, u32[]{:S(2)}, u32[]{:S(2)}) collective-permute-start(bf16[2,192,1024]{2,1,0:T(8,128)(2,1)S(1)} %pad_maximum_fusion.refs_0_), channel_id=1, source_target_pairs={{0,4},{8,12},{16,20},{24,28},{1,5},{9,13},{17,21},{25,29},{2,6},{1... | collective-permute-start | bytes 2359304 | tf_op jit(solution)/shard_map/ppermute | solution.py:45
  31.0 1.3 collective-permute-start.4
  32.3 6.4 %collective-permute-start.3 = (bf16[2,192,1024]{2,1,0:T(8,128)(2,1)S(1)}, bf16[2,192,1024]{2,1,0:T(8,128)(2,1)}, u32[]{:S(2)}, u32[]{:S(2)}) collective-permute-start(bf16[2,192,1024]{2,1,0:T(8,128)(2,1)S(1)} %collective-permute-done.refs_0_), channel_id=1, source_target_pairs={{0,4},{8,12},{16,20},{24,28},{1,5},{9,13},{17,21},{25,29},{2,6},{1... | collective-permute-start | bytes 2359304 | tf_op jit(solution)/shard_map/ppermute | solution.py:45
  38.7 15.3 %shard_map.148 = (f32[192,1024]{1,0:T(8,128)S(1)}, f32[6,1,1024]{2,1,0:T(1,128)S(1)}) custom-call(s32[4,16]{1,0:T(4,128)S(1)} %copy-done.14, s32[4]{0:T(128)S(1)} %copy-done.15, s32[2]{0:T(128)S(1)} %pad_add_fusion.place_ref, bf16[192,1024]{1,0:T(8,128)(2,1)S(1)} %copy-done.9, bf16[2,192,1024]{2,1,0:T(8,128)(2,1)S(1)} %collective-permute-done.refs_0_, ...), custom_call_target="tpu_custom_call" | custom-call | flops 1000000000 | bytes 6291456 | tf_op jit(solution)/shard_map/pallas_call | solution.py:236
  54.0 0.9 copy-done.18
  54.9 1.3 collective-permute-start.2
  56.2 1.8 shard_map.152
  58.1 0.1 collective-permute-start.11
  58.2 1.6 collective-permute-start.10
  59.7 0.6 copy-done.5
  60.3 1.1 copy-done.19
  61.5 16.2 %shard_map.149 = (f32[192,1024]{1,0:T(8,128)S(1)}, f32[6,1,1024]{2,1,0:T(1,128)S(1)}) custom-call(s32[4,16]{1,0:T(4,128)S(1)} %copy-done.14, s32[4]{0:T(128)S(1)} %copy-done.15, s32[2]{0:T(128)S(1)} %copy-done.5, bf16[192,1024]{1,0:T(8,128)(2,1)S(1)} %copy-done.9, bf16[2,192,1024]{2,1,0:T(8,128)(2,1)} %collective-permute-done.4.refs_0_, ...), custom_call_target="tpu_custom_call" | custom-call | flops 1000000000 | bytes 6291456 | tf_op jit(solution)/shard_map/pallas_call | solution.py:236
  77.6 0.3 collective-permute-start.9
  78.0 2.3 %shard_map.150 = (f32[192,1024]{1,0:T(8,128)S(1)}, f32[6,1,1024]{2,1,0:T(1,128)S(1)}) custom-call(s32[4,16]{1,0:T(4,128)S(1)} %copy-done.14, s32[4]{0:T(128)S(1)} %copy-done.15, s32[2]{0:T(128)S(1)} %copy-done.5, bf16[192,1024]{1,0:T(8,128)(2,1)S(1)} %copy-done.9, bf16[2,192,1024]{2,1,0:T(8,128)(2,1)} %collective-permute-done.1.refs_0_.refs_2_, ...), custom_call_target="tpu_custom_call" | custom-call | flops 1000000000 | bytes 6291456 | tf_op jit(solution)/shard_map/pallas_call | solution.py:236
  80.3 0.0 copy-start.28
  80.3 0.0 copy-start
  80.3 0.0 copy-start.2
  80.3 0.0 copy-start.3
  80.4 2.4 %shard_map.151 = (bf16[192,1024]{1,0:T(8,128)(2,1)S(1)}, f32[3,1,1024]{2,1,0:T(1,128)S(1)}) custom-call(s32[4,16]{1,0:T(4,128)S(1)} %copy-done.14, s32[4]{0:T(128)S(1)} %copy-done.15, s32[2]{0:T(128)S(1)} %copy-done.5, bf16[192,1024]{1,0:T(8,128)(2,1)S(1)} %copy-done.9, bf16[2,192,1024]{2,1,0:T(8,128)(2,1)} %collective-permute-done.2.refs_0_, ...), custom_call_target="tpu_custom_call" | custom-call | flops 1000000000 | bytes 6291456 | tf_op jit(solution)/shard_map/pallas_call | solution.py:236
  82.8 0.1 constant_dynamic-slice_fusion
  82.9 1.2 collective-permute-start.8
  84.0 0.7 collective-permute-start.7
  84.8 2.9 %collective-permute-done.8.a3 = bf16[192,256]{1,0:T(8,128)(2,1)S(1)} collective-permute-done((bf16[192,256]{1,0:T(8,128)(2,1)S(1)}, bf16[192,256]{1,0:T(8,128)(2,1)S(1)}, u32[]{:S(2)}, u32[]{:S(2)}) %collective-permute-start.8) | collective-permute-done | bytes 98336 | tf_op jit(solution)/shard_map/ppermute | solution.py:58
  87.7 2.4 %collective-permute-done.7.a2 = bf16[192,256]{1,0:T(8,128)(2,1)S(1)} collective-permute-done((bf16[192,256]{1,0:T(8,128)(2,1)S(1)}, bf16[192,256]{1,0:T(8,128)(2,1)S(1)}, u32[]{:S(2)}, u32[]{:S(2)}) %collective-permute-start.7) | collective-permute-done | bytes 98336 | tf_op jit(solution)/shard_map/ppermute | solution.py:58
  90.2 2.5 %shard_map.153 = (f32[48,256]{1,0:T(8,128)S(1)}, bf16[192,256]{1,0:T(8,128)(2,1)S(1)}, bf16[192,256]{1,0:T(8,128)(2,1)S(1)}, bf16[192,256]{1,0:T(8,128)(2,1)S(1)}, bf16[192,256]{1,0:T(8,128)(2,1)S(1)}) custom-call(s32[2]{0:T(128)S(1)} %copy-done.6, bf16[192,256]{1,0:T(8,128)(2,1)S(1)} %get-tuple-element.101.a0, ...), custom_call_target="tpu_custom_call" | custom-call | tf_op jit(solution)/shard_map/pallas_call | solution.py:282
  92.6 0.1 collective-permute-start.13
  92.7 1.6 collective-permute-start.14
  94.3 0.3 collective-permute-start.15
  94.6 5.0 %collective-permute-done.16.x_ref = f32[48,256]{1,0:T(8,128)S(1)} collective-permute-done((f32[48,256]{1,0:T(8,128)S(1)}, f32[48,256]{1,0:T(8,128)S(1)}, u32[]{:S(2)}, u32[]{:S(2)}) %collective-permute-start.16) | collective-permute-done | bytes 49184 | tf_op jit(solution)/shard_map/ppermute | solution.py:54
  99.6 0.0 copy-start.10
  99.6 0.6 copy-done.27
  100.2 4.6 %shard_map.154 = (f32[192,1024]{1,0:T(8,128)S(1)}, bf16[2,192,1024]{2,1,0:T(8,128)(2,1)}, bf16[2,192,1024]{2,1,0:T(8,128)(2,1)S(1)}) custom-call(s32[4,16]{1,0:T(4,128)S(1)} %copy-done.14, s32[4]{0:T(128)S(1)} %copy-done.15, s32[2]{0:T(128)S(1)} %copy-done.6, bf16[192,1024]{1,0:T(8,128)(2,1)S(1)} %copy-done.9, ...), custom_call_target="tpu_custom_call" | custom-call | flops 1000000000 | bytes 8388608 | tf_op jit(solution)/shard_map/pallas_call | solution.py:372
  104.8 0.9 copy-done.16
  105.7 33.4 %collective-permute-start.17 = (bf16[2,192,1024]{2,1,0:T(8,128)(2,1)}, bf16[2,192,1024]{2,1,0:T(8,128)(2,1)}, u32[]{:S(2)}, u32[]{:S(2)}) collective-permute-start(bf16[2,192,1024]{2,1,0:T(8,128)(2,1)} %get-tuple-element.81), channel_id=1, source_target_pairs={{0,4},{4,0},{8,12},{12,8},{16,20},{20,16},{24,28},{28,24},{1,5},{5... | collective-permute-start | bytes 2359304 | tf_op jit(solution)/shard_map/ppermute | solution.py:41
  139.1 1.7 shard_map.155.p0
  140.8 0.5 collective-permute-start.20
  141.3 1.0 collective-permute-start.19
  142.3 0.3 collective-permute-start.18
  142.7 0.9 copy-done.11
  143.5 1.1 copy-done.17
  144.7 19.4 %shard_map.156 = (f32[192,1024]{1,0:T(8,128)S(1)}, bf16[2,192,1024]{2,1,0:T(8,128)(2,1)S(1)}) custom-call(s32[4,16]{1,0:T(4,128)S(1)} %copy-done.14, s32[4]{0:T(128)S(1)} %copy-done.15, s32[2]{0:T(128)S(1)} %copy-done.7, bf16[192,1024]{1,0:T(8,128)(2,1)S(1)} %copy-done.9, bf16[192,1024]{1,0:T(8,128)(2,1)S(1)} %get-tuple-element.64.att_ref, ...), custom_call_target="tpu_custom_call" | custom-call | flops 1000000000 | bytes 8388608 | tf_op jit(solution)/shard_map/pallas_call | solution.py:372
  164.1 0.0 copy-start.12
  164.1 0.1 collective-permute-start.21
  164.2 0.1 select_add_fusion
  164.3 0.0 copy-start.26
  164.3 0.6 copy-done.25
  164.9 0.0 copy-done.26
  165.0 1.9 collective-permute-start.22
  166.9 18.3 %shard_map.158 = (f32[192,1024]{1,0:T(8,128)S(1)}, bf16[2,192,1024]{2,1,0:T(8,128)(2,1)S(1)}) custom-call(s32[4,16]{1,0:T(4,128)S(1)} %copy-done.14, s32[4]{0:T(128)S(1)} %copy-done.15, s32[2]{0:T(128)S(1)} %copy-done.7, bf16[192,1024]{1,0:T(8,128)(2,1)S(1)} %copy-done.9, bf16[192,1024]{1,0:T(8,128)(2,1)S(1)} %get-tuple-element.64.att_ref, ...), custom_call_target="tpu_custom_call" | custom-call | flops 1000000000 | bytes 8388608 | tf_op jit(solution)/shard_map/pallas_call | solution.py:372
  185.3 1.2 collective-permute-done.22
  186.5 2.3 %add_add_fusion = bf16[2,192,1024]{2,1,0:T(8,128)(2,1)} fusion(bf16[2,192,1024]{2,1,0:T(8,128)(2,1)S(1)} %collective-permute-done.22, bf16[2,192,1024]{2,1,0:T(8,128)(2,1)S(1)} %get-tuple-element.89, bf16[2,192,1024]{2,1,0:T(8,128)(2,1)S(1)} %collective-permute-done.21, bf16[2,192,1024]{2,1,0:T(8,128)(2,1)} %collective-permute-done.17, pred[]{:T(512)S(6)} %eq.5), kind=kLoop, calls=%fused_computation.2 | loop fusion | flops 1179648 | bytes 3932161 | tf_op jit(solution)/shard_map/add | solution.py:451
  188.7 2.2 collective-permute-start.23
  190.9 1.6 shard_map.157
  192.5 1.1 copy-done.21
  193.7 12.6 %shard_map.159 = (bf16[192,1024]{1,0:T(8,128)(2,1)}, f32[2,192,1024]{2,1,0:T(8,128)S(1)}) custom-call(s32[4,16]{1,0:T(4,128)S(1)} %copy-done.14, s32[4]{0:T(128)S(1)} %copy-done.15, s32[2]{0:T(128)S(1)} %copy-done.8, bf16[192,1024]{1,0:T(8,128)(2,1)S(1)} %copy-done.9, bf16[192,1024]{1,0:T(8,128)(2,1)S(1)} %get-tuple-element.64.att_ref, ...), custom_call_target="tpu_custom_call" | custom-call | flops 1000000000 | bytes 8388608 | tf_op jit(solution)/shard_map/pallas_call | solution.py:372
  206.3 15.6 %collective-permute-done.23 = bf16[2,192,1024]{2,1,0:T(8,128)(2,1)} collective-permute-done((bf16[2,192,1024]{2,1,0:T(8,128)(2,1)}, bf16[2,192,1024]{2,1,0:T(8,128)(2,1)}, u32[]{:S(2)}, u32[]{:S(2)}) %collective-permute-start.23) | collective-permute-done | bytes 786464 | tf_op jit(solution)/shard_map/ppermute | solution.py:37
  221.8 1.6 add_convert_fusion
  223.4 0.9 slice_bitcast_fusion
  (63 shorter events, 0.1 us)
Async XLA Ops:
  0.6 4.8 %copy-start.15 = (s32[4]{0:T(128)S(1)}, s32[4]{0:T(128)}, u32[]{:S(2)}) copy-start(s32[4]{0:T(128)} %counts_ref.17) | copy-start | bytes 52
  0.6 4.8 %copy-start.14 = (s32[4,16]{1,0:T(4,128)S(1)}, s32[4,16]{1,0:T(4,128)}, u32[]{:S(2)}) copy-start(s32[4,16]{1,0:T(4,128)} %lists_ref.17) | copy-start | bytes 772
  0.7 4.8 %copy-start.9 = (bf16[192,1024]{1,0:T(8,128)(2,1)S(1)}, bf16[192,1024]{1,0:T(8,128)(2,1)}, u32[]{:S(2)}) copy-start(bf16[192,1024]{1,0:T(8,128)(2,1)} %q_ref.17) | copy-start | bytes 1179652
  1.9 21.2 %collective-permute-start = (bf16[2,192,1024]{2,1,0:T(8,128)(2,1)S(1)}, bf16[2,192,1024]{2,1,0:T(8,128)(2,1)S(1)}, u32[]{:S(2)}, u32[]{:S(2)}) collective-permute-start(bf16[2,192,1024]{2,1,0:T(8,128)(2,1)S(1)} %pad_maximum_fusion.refs_0_), channel_id=1, source_target_pairs={{0,8},{4,12},{8,16},{12,20},{16,24},{20,28},{1,9},{5,13},{9,17},{1... | collective-permute-start | bytes 2359304 | tf_op jit(solution)/shard_map/ppermute | solution.py:37
  5.5 33.2 %copy-start.4 = (s32[2]{0:T(128)}, s32[2]{0:T(128)S(1)}, u32[]{:S(2)}) copy-start(s32[2]{0:T(128)S(1)} %pad_add_fusion.place_ref) | copy-start | bytes 28
  23.1 35.0 %copy-start.1 = (bf16[192,768]{1,0:T(8,128)(2,1)S(1)}, bf16[192,768]{1,0:T(8,128)(2,1)}, u32[]{:S(2)}) copy-start(bf16[192,768]{1,0:T(8,128)(2,1)} %w0) | copy-start | bytes 884740
  23.1 31.8 %collective-permute-start.1 = (bf16[2,192,1024]{2,1,0:T(8,128)(2,1)S(1)}, bf16[2,192,1024]{2,1,0:T(8,128)(2,1)}, u32[]{:S(2)}, u32[]{:S(2)}) collective-permute-start(bf16[2,192,1024]{2,1,0:T(8,128)(2,1)S(1)} %collective-permute-done.refs_0_), channel_id=1, source_target_pairs={{0,8},{4,12},{8,16},{12,20},{16,24},{20,28},{1,9},{5,13},{9,17},{1... | collective-permute-start | bytes 2359304 | tf_op jit(solution)/shard_map/ppermute | solution.py:37
  26.7 31.4 %collective-permute-start.5 = (bf16[2,192,1024]{2,1,0:T(8,128)(2,1)S(1)}, bf16[2,192,1024]{2,1,0:T(8,128)(2,1)}, u32[]{:S(2)}, u32[]{:S(2)}) collective-permute-start(bf16[2,192,1024]{2,1,0:T(8,128)(2,1)S(1)} %pad_maximum_fusion.refs_0_), channel_id=1, source_target_pairs={{0,4},{8,12},{16,20},{24,28},{1,5},{9,13},{17,21},{25,29},{2,6},{1... | collective-permute-start | bytes 2359304 | tf_op jit(solution)/shard_map/ppermute | solution.py:45
  31.0 27.1 %collective-permute-start.4 = (bf16[2,192,1024]{2,1,0:T(8,128)(2,1)S(1)}, bf16[2,192,1024]{2,1,0:T(8,128)(2,1)}, u32[]{:S(2)}, u32[]{:S(2)}) collective-permute-start(bf16[2,192,1024]{2,1,0:T(8,128)(2,1)S(1)} %collective-permute-done.refs_0_), channel_id=1, source_target_pairs={{4,0},{12,8},{20,16},{28,24},{5,1},{13,9},{21,17},{29,25},{6,2},{1... | collective-permute-start | bytes 2359304 | tf_op jit(solution)/shard_map/ppermute | solution.py:49
  32.3 45.3 %collective-permute-start.3 = (bf16[2,192,1024]{2,1,0:T(8,128)(2,1)S(1)}, bf16[2,192,1024]{2,1,0:T(8,128)(2,1)}, u32[]{:S(2)}, u32[]{:S(2)}) collective-permute-start(bf16[2,192,1024]{2,1,0:T(8,128)(2,1)S(1)} %collective-permute-done.refs_0_), channel_id=1, source_target_pairs={{0,4},{8,12},{16,20},{24,28},{1,5},{9,13},{17,21},{25,29},{2,6},{1... | collective-permute-start | bytes 2359304 | tf_op jit(solution)/shard_map/ppermute | solution.py:45
  54.0 0.9 copy-start.18
  54.9 25.4 %collective-permute-start.2 = (bf16[2,192,1024]{2,1,0:T(8,128)(2,1)}, bf16[2,192,1024]{2,1,0:T(8,128)(2,1)}, u32[]{:S(2)}, u32[]{:S(2)}) collective-permute-start(bf16[2,192,1024]{2,1,0:T(8,128)(2,1)} %collective-permute-done.1.refs_0_.refs_2_), channel_id=1, source_target_pairs={{4,0},{12,8},{20,16},{28,24},{5,1},{13,9},{21,17},{29,25},{6,2},{1... | collective-permute-start | bytes 2359304 | tf_op jit(solution)/shard_map/ppermute | solution.py:49
  58.1 26.0 %collective-permute-start.12 = (f32[48,256]{1,0:T(8,128)}, f32[48,256]{1,0:T(8,128)S(1)}, u32[]{:S(2)}, u32[]{:S(2)}) collective-permute-start(f32[48,256]{1,0:T(8,128)} %shard_map.152), channel_id=1, source_target_pairs={{0,28},{4,24},{8,20},{12,16},{16,12},{20,8},{24,4},{28,0},{1,29},{... | collective-permute-start | bytes 147464 | tf_op jit(solution)/shard_map/ppermute | solution.py:54
  58.1 26.7 %collective-permute-start.11 = (bf16[192,768]{1,0:T(8,128)(2,1)S(1)}, bf16[192,768]{1,0:T(8,128)(2,1)S(1)}, u32[]{:S(2)}, u32[]{:S(2)}) collective-permute-start(bf16[192,768]{1,0:T(8,128)(2,1)S(1)} %copy-done.1), channel_id=1, source_target_pairs={{0,3},{1,2},{2,1},{3,0},{4,7},{5,6},{6,5},{7,4},{8,11},{9,10},{10,... | collective-permute-start | bytes 884744 | tf_op jit(solution)/shard_map/ppermute | solution.py:58
  58.2 26.7 %collective-permute-start.10 = (bf16[192,768]{1,0:T(8,128)(2,1)S(1)}, bf16[192,768]{1,0:T(8,128)(2,1)S(1)}, u32[]{:S(2)}, u32[]{:S(2)}) collective-permute-start(bf16[192,768]{1,0:T(8,128)(2,1)S(1)} %copy-done.1), channel_id=1, source_target_pairs={{0,2},{1,3},{2,0},{3,1},{4,6},{5,7},{6,4},{7,5},{8,10},{9,11},{10,... | collective-permute-start | bytes 884744 | tf_op jit(solution)/shard_map/ppermute | solution.py:58
  59.7 0.6 copy-start.5
  60.3 1.1 copy-start.19
  77.6 7.2 %collective-permute-start.9 = (bf16[192,768]{1,0:T(8,128)(2,1)S(1)}, bf16[192,768]{1,0:T(8,128)(2,1)S(1)}, u32[]{:S(2)}, u32[]{:S(2)}) collective-permute-start(bf16[192,768]{1,0:T(8,128)(2,1)S(1)} %copy-done.1), channel_id=1, source_target_pairs={{0,1},{1,0},{2,3},{3,2},{4,5},{5,4},{6,7},{7,6},{8,9},{9,8},{10,11... | collective-permute-start | bytes 884744 | tf_op jit(solution)/shard_map/ppermute | solution.py:58
  80.3 4.5 %copy-start.28 = (f32[768]{0:T(1024)S(1)}, f32[768]{0:T(1024)}, u32[]{:S(2)}) copy-start(f32[768]{0:T(1024)} %param.19) | copy-start | bytes 9220
  80.3 9.8 %copy-start = (bf16[1024,768]{1,0:T(8,128)(2,1)S(1)}, bf16[1024,768]{1,0:T(8,128)(2,1)}, u32[]{:S(2)}) copy-start(bf16[1024,768]{1,0:T(8,128)(2,1)} %stream_ref.1) | copy-start | bytes 4718596
  80.3 9.8 %copy-start.2 = (f32[1024,48]{0,1:T(8,128)S(1)}, f32[1024,48]{0,1:T(8,128)}, u32[]{:S(2)}) copy-start(f32[1024,48]{0,1:T(8,128)} %param.21) | copy-start | bytes 589828
  80.3 9.8 %copy-start.3 = (bf16[96,768]{1,0:T(8,128)(2,1)S(1)}, bf16[96,768]{1,0:T(8,128)(2,1)}, u32[]{:S(2)}) copy-start(bf16[96,768]{1,0:T(8,128)(2,1)} %head_ref.1) | copy-start | bytes 442372
  80.4 9.8 %copy-start.6 = (s32[2]{0:T(128)S(1)}, s32[2]{0:T(128)}, u32[]{:S(2)}) copy-start(s32[2]{0:T(128)} %copy-done.4) | copy-start | bytes 28
  82.9 4.8 %collective-permute-start.8 = (bf16[192,256]{1,0:T(8,128)(2,1)S(1)}, bf16[192,256]{1,0:T(8,128)(2,1)S(1)}, u32[]{:S(2)}, u32[]{:S(2)}) collective-permute-start(bf16[192,256]{1,0:T(8,128)(2,1)S(1)} %get-tuple-element.98), channel_id=1, source_target_pairs={{0,3},{1,2},{2,1},{3,0},{4,7},{5,6},{6,5},{7,4},{8,11},{9,10},{10,... | collective-permute-start | bytes 294920 | tf_op jit(solution)/shard_map/ppermute | solution.py:58
  84.0 6.1 %collective-permute-start.7 = (bf16[192,256]{1,0:T(8,128)(2,1)S(1)}, bf16[192,256]{1,0:T(8,128)(2,1)S(1)}, u32[]{:S(2)}, u32[]{:S(2)}) collective-permute-start(bf16[192,256]{1,0:T(8,128)(2,1)S(1)} %get-tuple-element.99), channel_id=1, source_target_pairs={{0,2},{1,3},{2,0},{3,1},{4,6},{5,7},{6,4},{7,5},{8,10},{9,11},{10,... | collective-permute-start | bytes 294920 | tf_op jit(solution)/shard_map/ppermute | solution.py:58
  84.8 5.3 %collective-permute-start.6 = (bf16[192,256]{1,0:T(8,128)(2,1)S(1)}, bf16[192,256]{1,0:T(8,128)(2,1)S(1)}, u32[]{:S(2)}, u32[]{:S(2)}) collective-permute-start(bf16[192,256]{1,0:T(8,128)(2,1)S(1)} %get-tuple-element.100), channel_id=1, source_target_pairs={{0,1},{1,0},{2,3},{3,2},{4,5},{5,4},{6,7},{7,6},{8,9},{9,8},{10,11... | collective-permute-start | bytes 294920 | tf_op jit(solution)/shard_map/ppermute | solution.py:58
  92.6 6.9 %collective-permute-start.13 = (bf16[192,256]{1,0:T(8,128)(2,1)S(1)}, bf16[192,256]{1,0:T(8,128)(2,1)S(1)}, u32[]{:S(2)}, u32[]{:S(2)}) collective-permute-start(bf16[192,256]{1,0:T(8,128)(2,1)S(1)} %get-tuple-element.68), channel_id=1, source_target_pairs={{0,1},{1,0},{2,3},{3,2},{4,5},{5,4},{6,7},{7,6},{8,9},{9,8},{10,11... | collective-permute-start | bytes 294920 | tf_op jit(solution)/shard_map/ppermute | solution.py:58
  92.7 6.9 %collective-permute-start.14 = (bf16[192,256]{1,0:T(8,128)(2,1)S(1)}, bf16[192,256]{1,0:T(8,128)(2,1)S(1)}, u32[]{:S(2)}, u32[]{:S(2)}) collective-permute-start(bf16[192,256]{1,0:T(8,128)(2,1)S(1)} %get-tuple-element.69), channel_id=1, source_target_pairs={{0,2},{1,3},{2,0},{3,1},{4,6},{5,7},{6,4},{7,5},{8,10},{9,11},{10,... | collective-permute-start | bytes 294920 | tf_op jit(solution)/shard_map/ppermute | solution.py:58
  94.3 5.3 %collective-permute-start.15 = (bf16[192,256]{1,0:T(8,128)(2,1)S(1)}, bf16[192,256]{1,0:T(8,128)(2,1)S(1)}, u32[]{:S(2)}, u32[]{:S(2)}) collective-permute-start(bf16[192,256]{1,0:T(8,128)(2,1)S(1)} %get-tuple-element.70), channel_id=1, source_target_pairs={{0,3},{1,2},{2,1},{3,0},{4,7},{5,6},{6,5},{7,4},{8,11},{9,10},{10,... | collective-permute-start | bytes 294920 | tf_op jit(solution)/shard_map/ppermute | solution.py:58
  94.6 5.0 %collective-permute-start.16 = (f32[48,256]{1,0:T(8,128)S(1)}, f32[48,256]{1,0:T(8,128)S(1)}, u32[]{:S(2)}, u32[]{:S(2)}) collective-permute-start(f32[48,256]{1,0:T(8,128)S(1)} %get-tuple-element.71), channel_id=1, source_target_pairs={{0,28},{4,24},{8,20},{12,16},{16,12},{20,8},{24,4},{28,0},{1,29},{... | collective-permute-start | bytes 147464 | tf_op jit(solution)/shard_map/ppermute | solution.py:54
  99.6 0.6 copy-start.27
  99.6 5.2 %copy-start.10 = (bf16[192,256]{1,0:T(8,128)(2,1)}, bf16[192,256]{1,0:T(8,128)(2,1)S(1)}, u32[]{:S(2)}) copy-start(bf16[192,256]{1,0:T(8,128)(2,1)S(1)} %collective-permute-done.15.g3) | copy-start | bytes 294916
  100.2 42.5 %copy-start.7 = (s32[2]{0:T(128)S(1)}, s32[2]{0:T(128)}, u32[]{:S(2)}) copy-start(s32[2]{0:T(128)} %copy-done.4) | copy-start | bytes 28
  104.8 0.9 copy-start.16
  105.7 58.5 %collective-permute-start.17 = (bf16[2,192,1024]{2,1,0:T(8,128)(2,1)}, bf16[2,192,1024]{2,1,0:T(8,128)(2,1)}, u32[]{:S(2)}, u32[]{:S(2)}) collective-permute-start(bf16[2,192,1024]{2,1,0:T(8,128)(2,1)} %get-tuple-element.81), channel_id=1, source_target_pairs={{0,4},{4,0},{8,12},{12,8},{16,20},{20,16},{24,28},{28,24},{1,5},{5... | collective-permute-start | bytes 2359304 | tf_op jit(solution)/shard_map/ppermute | solution.py:41
  140.8 23.5 %collective-permute-start.20 = (f32[48,256]{1,0:T(8,128)}, f32[48,256]{1,0:T(8,128)S(1)}, u32[]{:S(2)}, u32[]{:S(2)}) collective-permute-start(f32[48,256]{1,0:T(8,128)} %shard_map.155.p0), channel_id=1, source_target_pairs={{0,3},{1,2},{2,1},{3,0},{4,7},{5,6},{6,5},{7,4},{8,11},{9,10},{10,... | collective-permute-start | bytes 147464 | tf_op jit(solution)/shard_map/ppermute | solution.py:58
  141.3 23.0 %collective-permute-start.19 = (f32[48,256]{1,0:T(8,128)}, f32[48,256]{1,0:T(8,128)S(1)}, u32[]{:S(2)}, u32[]{:S(2)}) collective-permute-start(f32[48,256]{1,0:T(8,128)} %shard_map.155.p0), channel_id=1, source_target_pairs={{0,2},{1,3},{2,0},{3,1},{4,6},{5,7},{6,4},{7,5},{8,10},{9,11},{10,... | collective-permute-start | bytes 147464 | tf_op jit(solution)/shard_map/ppermute | solution.py:58
  142.3 22.0 %collective-permute-start.18 = (f32[48,256]{1,0:T(8,128)}, f32[48,256]{1,0:T(8,128)S(1)}, u32[]{:S(2)}, u32[]{:S(2)}) collective-permute-start(f32[48,256]{1,0:T(8,128)} %shard_map.155.p0), channel_id=1, source_target_pairs={{0,1},{1,0},{2,3},{3,2},{4,5},{5,4},{6,7},{7,6},{8,9},{9,8},{10,11... | collective-permute-start | bytes 147464 | tf_op jit(solution)/shard_map/ppermute | solution.py:58
  142.6 0.9 copy-start.11
  143.5 1.1 copy-start.17
  164.1 2.8 %copy-start.12 = (bf16[192,256]{1,0:T(8,128)(2,1)S(1)}, bf16[192,256]{1,0:T(8,128)(2,1)}, u32[]{:S(2)}) copy-start(bf16[192,256]{1,0:T(8,128)(2,1)} %copy-done.10) | copy-start | bytes 294916
  164.1 21.2 %collective-permute-start.21 = (bf16[2,192,1024]{2,1,0:T(8,128)(2,1)S(1)}, bf16[2,192,1024]{2,1,0:T(8,128)(2,1)S(1)}, u32[]{:S(2)}, u32[]{:S(2)}) collective-permute-start(bf16[2,192,1024]{2,1,0:T(8,128)(2,1)S(1)} %get-tuple-element.90), channel_id=1, source_target_pairs={{0,4},{4,0},{8,12},{12,8},{16,20},{20,16},{24,28},{28,24},{1,5},{5... | collective-permute-start | bytes 2359304 | tf_op jit(solution)/shard_map/ppermute | solution.py:41
  164.3 21.0 %copy-start.24 = (f32[48,256]{1,0:T(8,128)}, f32[48,256]{1,0:T(8,128)S(1)}, u32[]{:S(2)}) copy-start(f32[48,256]{1,0:T(8,128)S(1)} %collective-permute-done.20.p3) | copy-start | bytes 147460
  164.3 0.6 copy-start.25
  164.3 0.6 copy-start.26
  165.0 21.5 %collective-permute-start.22 = (bf16[2,192,1024]{2,1,0:T(8,128)(2,1)S(1)}, bf16[2,192,1024]{2,1,0:T(8,128)(2,1)S(1)}, u32[]{:S(2)}, u32[]{:S(2)}) collective-permute-start(bf16[2,192,1024]{2,1,0:T(8,128)(2,1)S(1)} %select_add_fusion), channel_id=1, source_target_pairs={{8,0},{12,4},{16,8},{20,12},{24,16},{28,20},{9,1},{13,5},{17,9},{2... | collective-permute-start | bytes 2359304 | tf_op jit(solution)/shard_map/ppermute | solution.py:37
  185.3 3.5 %copy-start.20 = (f32[192,1024]{1,0:T(8,128)}, f32[192,1024]{1,0:T(8,128)S(1)}, u32[]{:S(2)}) copy-start(f32[192,1024]{1,0:T(8,128)S(1)} %get-tuple-element.92.refs_1_) | copy-start | bytes 2359300
  185.3 3.5 %copy-start.22 = (bf16[2,192,1024]{2,1,0:T(8,128)(2,1)}, bf16[2,192,1024]{2,1,0:T(8,128)(2,1)S(1)}, u32[]{:S(2)}) copy-start(bf16[2,192,1024]{2,1,0:T(8,128)(2,1)S(1)} %collective-permute-done.21) | copy-start | bytes 2359300
  186.5 6.1 %copy-start.8 = (s32[2]{0:T(128)S(1)}, s32[2]{0:T(128)}, u32[]{:S(2)}) copy-start(s32[2]{0:T(128)} %copy-done.4) | copy-start | bytes 28
  186.5 6.1 %copy-start.13 = (bf16[192,256]{1,0:T(8,128)(2,1)S(1)}, bf16[192,256]{1,0:T(8,128)(2,1)}, u32[]{:S(2)}) copy-start(bf16[192,256]{1,0:T(8,128)(2,1)} %copy-done.10) | copy-start | bytes 294916
  188.7 33.1 %collective-permute-start.23 = (bf16[2,192,1024]{2,1,0:T(8,128)(2,1)}, bf16[2,192,1024]{2,1,0:T(8,128)(2,1)}, u32[]{:S(2)}, u32[]{:S(2)}) collective-permute-start(bf16[2,192,1024]{2,1,0:T(8,128)(2,1)} %add_add_fusion), channel_id=1, source_target_pairs={{8,0},{12,4},{16,8},{20,12},{24,16},{28,20},{9,1},{13,5},{17,9},{2... | collective-permute-start | bytes 2359304 | tf_op jit(solution)/shard_map/ppermute | solution.py:37
  192.5 1.1 copy-start.21
  193.7 28.2 %copy-start.23 = (bf16[2,192,1024]{2,1,0:T(8,128)(2,1)S(1)}, bf16[2,192,1024]{2,1,0:T(8,128)(2,1)}, u32[]{:S(2)}) copy-start(bf16[2,192,1024]{2,1,0:T(8,128)(2,1)} %copy-done.22) | copy-start | bytes 2359300
where the time goes:
time: 225 us; the launch traced here: 224 us
  Pallas kernels  109 us (48%)
  starting transfers between devices  65.6 us (29%)
  waiting for transfers between devices  34.4 us (15%)
  local copies, waits for them, and re-layouts  8.99 us (4%)
  other arithmetic  5.24 us (2%)
    pallas_call x4, Pallas kernels, backward(): pl.pallas_call(functools.partial(backward_kernel, regions, diagonal, last...  54.9 us
    pallas_call x5, Pallas kernels, forward(): pl.pallas_call(functools.partial(forward_kernel, regions, not state, clos...  46.5 us
    ppermute x2, starting transfers between devices, mate(): lax.ppermute(array, 'row', [(i, i ^ 1) for i in range(lax.axis_size('row'...  33.5 us
    ppermute x4, waiting for transfers between devices, hop(): return lax.ppermute(array, 'row', pairs)  24.1 us
    ppermute x4, starting transfers between devices, hop(): return lax.ppermute(array, 'row', pairs)  11.2 us
    ppermute x2, starting transfers between devices, upward(): lax.ppermute(array, 'row', [(i, i + 1) for i in range(0, lax.axis_size('r...  10.7 us
    unnamed x58, local copies, waits for them, and re-layouts  7.99 us
    ppermute x12, starting transfers between devices, across(): lax.ppermute(array, 'col', [(i, i ^ bits) for i in range(lax.axis_size('c...  7.69 us
  transfers between devices with their start and end apart: 24, of which 6 were waited for; matrix products, arithmetic and copies ran while one was open for 0% of the time, Pallas kernels for 45%

commit v1 on v0

--- a/solution.py
+++ b/solution.py
@@ -109,26 +109,30 @@
     )(place, *pieces)
 
 
-def live_slots(lists_ref, counts_ref, place_ref, regions, blocks, first, items_ref):
+def live_items(lists_ref, counts_ref, place_ref, regions, blocks, first, items_ref, together):
     row = place_ref[0]
     odd = lax.rem(row, 2)
+    slots = len(regions) * blocks
     wanted = [jnp.where(odd == 1, region[1], region[0]) for region in regions]
     found = []
+    total = 0
     for b in range(blocks):
 
         def look(j, count, b=b):
             block = lists_ref[b, j]
             distance = row - lax.div(block, blocks)
-            slot, hit = 0, 0
+            slot, hit = b * slots, 0
             for r, want in enumerate(wanted):
                 here = (distance == want).astype(jnp.int32)
                 slot = slot + here * r * blocks
                 hit = hit + here
-            items_ref[b * LIST + count] = slot + lax.rem(block, blocks)
+            items_ref[count] = slot + lax.rem(block, blocks)
             return count + hit
 
-        found.append(lax.fori_loop(first, counts_ref[b], look, 0))
-    return found
+        start = total if together else b * LIST
+        total = lax.fori_loop(first, counts_ref[b], look, start)
+        found.append(total - start)
+    return total if together else found
 
 
 def staged(place_ref, regions, refs, copy):
@@ -162,16 +166,18 @@
 def forward_kernel(regions, opening, closing, lists_ref, counts_ref, place_ref, q_ref, *refs):
     heads = q_ref.shape[0] // HEAD_DIM
     blocks = q_ref.shape[1] // BLOCK
+    slots = len(regions) * blocks
     refs = list(refs)
     slabs = [refs.pop(0) for _ in range(region_inputs(regions))]
     if not opening:
         acc_in, stat_in = refs.pop(0), refs.pop(0)
     if closing:
         att_ref, lse_ref = refs.pop(0), refs.pop(0)
-        key_rows, value_cols, items, acc_ref = refs
     else:
-        acc_ref, stat_ref = refs.pop(0), refs.pop(0)
-        key_rows, value_cols, items = refs
+        acc_out, stat_out = refs.pop(0), refs.pop(0)
+    key_rows, value_cols, scaled, items, found_ref, acc_ref, stat_ref = refs
+    if not closing:
+        acc_ref, stat_ref = acc_out, stat_out
 
     def copy(r, ref):
         for b in range(blocks):
@@ -181,68 +187,93 @@
                 key_rows[slot, h] = ref[0, head_rows(h), cols].T
 
     staged(place_ref, regions, slabs, copy)
-    found = live_slots(
-        lists_ref, counts_ref, place_ref, regions, blocks, 1 if opening else 0, items)
-    acc_ref[...] = jnp.zeros_like(acc_ref) if opening else acc_in[...]
-    keep = causal()
-
-    for b in range(blocks):
-        cols = slice(b * BLOCK, (b + 1) * BLOCK)
-        queries = [q_ref[head_rows(h), cols] * BF16(SCALE) for h in range(heads)]
-
-        def entry(slot, state, masked, cols=cols, queries=queries):
-            out = []
+    for b, found in enumerate(live_items(
+            lists_ref, counts_ref, place_ref, regions, blocks, int(opening), items, False)):
+        found_ref[b] = found
+        scaled[b] = q_ref[:, b * BLOCK:(b + 1) * BLOCK] * BF16(SCALE)
+    if not opening:
+        acc_ref[...] = acc_in[...]
+        stat_ref[...] = stat_in[...]
+
+    def entries(b, chosen, masked=False):
+        scores = [[dot(key_rows[slot, h], scaled[b, head_rows(h)]) for slot in chosen]
+                  for h in range(heads)]
+        for h in range(heads):
+            rows = head_rows(h)
+            tiles = scores[h]
+            if masked:
+                keep = causal()
+                tiles = [jnp.where(keep, tile, NEG) for tile in tiles]
+            peak = tiles[0]
+            for tile in tiles[1:]:
+                peak = jnp.maximum(peak, tile)
+            peak = jnp.max(peak, axis=0, keepdims=True)
+            if masked:
+                newest, total, acc = peak, 0.0, 0.0
+            else:
+                newest = jnp.maximum(stat_ref[b, 2 * h], peak)
+                fade = jnp.exp(stat_ref[b, 2 * h] - newest)
+                total = stat_ref[b, 2 * h + 1] * fade
+                acc = acc_ref[b, rows] * fade
+            for slot, tile in zip(chosen, tiles):
+                weights = jnp.exp(tile - newest)
+                total = total + jnp.sum(weights, axis=0, keepdims=True)
+                acc = acc + dot(value_cols[slot, rows], weights.astype(BF16))
+            acc_ref[b, rows] = acc
+            stat_ref[b, 2 * h] = newest
+            stat_ref[b, 2 * h + 1] = total
+
+    def one_block(b, carry):
+        found = found_ref[b]
+        if opening:
+            entries(b, [b], True)
+
+        def slot_at(i):
+            return items[b * LIST + i] - b * slots
+
+        @pl.loop(0, lax.div(found, 2))
+        def _(i):
+            entries(b, [slot_at(2 * i), slot_at(2 * i + 1)])
+
+        @pl.when(lax.rem(found, 2) == 1)
+        def _():
+            entries(b, [slot_at(found - 1)])
+
+        return carry
+
+    lax.fori_loop(0, blocks, one_block, 0)
+    if closing:
+        for b in range(blocks):
+            cols = slice(b * BLOCK, (b + 1) * BLOCK)
             for h in range(heads):
-                rows = head_rows(h)
-                top, total = state[2 * h], state[2 * h + 1]
-                scores = dot(key_rows[slot, h], queries[h])
-                if masked:
-                    scores = jnp.where(keep, scores, NEG)
-                newest = jnp.maximum(top, jnp.max(scores, axis=0, keepdims=True))
-                weights = jnp.exp(scores - newest)
-                fade = jnp.exp(top - newest)
-                total = total * fade + jnp.sum(weights, axis=0, keepdims=True)
-                acc_ref[rows, cols] = acc_ref[rows, cols] * fade + dot(
-                    value_cols[slot, rows], weights.astype(BF16))
-                out += [newest, total]
-            return tuple(out)
-
-        if opening:
-            state = (jnp.full((1, BLOCK), NEG, F32), jnp.zeros((1, BLOCK), F32)) * heads
-            state = entry(b, state, True)
-        else:
-            state = tuple(stat_in[i, :, cols] for i in range(2 * heads))
-        state = lax.fori_loop(
-            0, found[b], lambda i, s: entry(items[b * LIST + i], s, False), state)
-        for h in range(heads):
-            if closing:
-                att_ref[head_rows(h), cols] = (
-                    acc_ref[head_rows(h), cols] / state[2 * h + 1]).astype(BF16)
-                lse_ref[h, :, cols] = state[2 * h] + jnp.log(state[2 * h + 1])
-            else:
-                stat_ref[2 * h, :, cols] = state[2 * h]
-                stat_ref[2 * h + 1, :, cols] = state[2 * h + 1]
-
-
-def forward(tables, queries, regions, slabs, state=None, closing=False, pairs=1):
+                top, total = stat_ref[b, 2 * h], stat_ref[b, 2 * h + 1]
+                att_ref[head_rows(h), cols] = (acc_ref[b, head_rows(h)] / total).astype(BF16)
+                lse_ref[b, h] = top + jnp.log(total)
+
+
+def forward(tables, queries, regions, slabs, state=None, closing=False, pairs=16):
     width, tokens = queries.shape
-    heads = width // HEAD_DIM
-    slots = len(regions) * (tokens // BLOCK)
-    running = (jax.ShapeDtypeStruct((width, tokens), F32),
-               jax.ShapeDtypeStruct((2 * heads, 1, tokens), F32))
+    heads, blocks = width // HEAD_DIM, tokens // BLOCK
+    slots = len(regions) * blocks
+    acc, stat = (blocks, width, BLOCK), (blocks, 2 * heads, 1, BLOCK)
     result = (jax.ShapeDtypeStruct((width, tokens), BF16),
-              jax.ShapeDtypeStruct((heads, 1, tokens), F32))
+              jax.ShapeDtypeStruct((blocks, heads, 1, BLOCK), F32))
     state = () if state is None else state
     return pl.pallas_call(
         functools.partial(forward_kernel, regions, not state, closing),
-        out_shape=result if closing else running,
+        out_shape=result if closing else tuple(
+            jax.ShapeDtypeStruct(shape, F32) for shape in (acc, stat)),
         in_specs=smem(3) + vmem(1 + len(slabs) + len(state)),
         out_specs=tuple(vmem(2)),
         scratch_shapes=[
             pltpu.VMEM((slots, heads, BLOCK, HEAD_DIM), BF16),
             pltpu.VMEM((slots, width, BLOCK), BF16),
-            pltpu.SMEM((tokens // BLOCK * LIST,), jnp.int32),
-        ] + [pltpu.VMEM((width, tokens), F32)] * closing,
+            pltpu.VMEM((blocks, width, BLOCK), BF16),
+            pltpu.SMEM((blocks * LIST,), jnp.int32),
+            pltpu.SMEM((blocks,), jnp.int32),
+            pltpu.VMEM(acc if closing else (8, BLOCK), F32),
+            pltpu.VMEM(stat if closing else (8, BLOCK), F32),
+        ],
         compiler_params=pltpu.CompilerParams(vmem_limit_bytes=48 << 20),
         cost_estimate=pl.CostEstimate(
             flops=pairs * 10 ** 9, bytes_accessed=6 << 20, transcendentals=pairs * 10 ** 5),
@@ -295,12 +326,14 @@
                     lse_ref, g0, g1, g2, g3, *refs):
     heads = q_ref.shape[0] // HEAD_DIM
     blocks = q_ref.shape[1] // BLOCK
+    slots = len(regions) * blocks
     refs = list(refs)
     slabs = [refs.pop(0) for _ in range(region_inputs(regions))]
-    dq_in = None if len(refs) < 10 + len(regions) else refs.pop(0)
+    dq_in = None if len(refs) < 12 + len(regions) else refs.pop(0)
     dq_ref = refs.pop(0)
     outs = [refs.pop(0) for _ in regions]
-    key_rows, value_rows, key_cols, grad_cols, grad_keys, grad_values, items, acc_ref = refs
+    (key_rows, value_rows, key_cols, grad_cols, scaled, sums, grad_keys, grad_values, items,
+     acc_ref) = refs
     me = place_ref[1]
     for k, ref in enumerate((g0, g1, g2, g3)):
         grad_cols[jnp.bitwise_xor(me, k)] = ref[...]
@@ -316,44 +349,54 @@
     staged(place_ref, regions, slabs, copy)
     grad_keys[...] = jnp.zeros_like(grad_keys)
     grad_values[...] = jnp.zeros_like(grad_values)
-    found = live_slots(
-        lists_ref, counts_ref, place_ref, regions, blocks, 1 if diagonal else 0, items)
-    acc_ref[...] = jnp.zeros_like(acc_ref) if dq_in is None else dq_in[...]
-    keep = causal()
-
+    found = live_items(
+        lists_ref, counts_ref, place_ref, regions, blocks, int(diagonal), items, True)
     for b in range(blocks):
         cols = slice(b * BLOCK, (b + 1) * BLOCK)
-        queries, grads, sums, tops = [], [], [], []
+        scaled[b] = q_ref[:, cols] * BF16(SCALE)
         for h in range(heads):
             rows = head_rows(h)
-            queries.append(q_ref[rows, cols] * BF16(SCALE))
-            grads.append(grad_cols[b, rows])
-            sums.append(jnp.sum(grads[h].astype(F32) * att_ref[rows, cols].astype(F32),
-                                axis=0, keepdims=True))
-            tops.append(lse_ref[h, :, cols])
-
-        def entry(slot, masked, cols=cols, queries=queries, grads=grads, sums=sums, tops=tops):
-            for h in range(heads):
-                rows = head_rows(h)
-                scores = dot(key_rows[slot, h], queries[h])
-                if masked:
-                    scores = jnp.where(keep, scores, NEG)
-                probs = jnp.exp(scores - tops[h])
-                grad_scores = (
-                    probs * (dot(value_rows[slot, h], grads[h]) - sums[h])).astype(BF16)
-                acc_ref[rows, cols] += dot(key_cols[slot, rows], grad_scores)
-                grad_keys[slot, rows] += dot(queries[h], grad_scores, 1, 1)
-                grad_values[slot, rows] += dot(grads[h], probs.astype(BF16), 1, 1)
-
-        if diagonal:
-            entry(b, True)
-
-        @pl.loop(0, found[b])
-        def _(i, b=b, entry=entry):
-            entry(items[b * LIST + i], False)
+            sums[b, h] = jnp.sum(
+                grad_cols[b, rows].astype(F32) * att_ref[rows, cols].astype(F32),
+                axis=0, keepdims=True)
+    acc_ref[...] = jnp.zeros_like(acc_ref) if dq_in is None else dq_in[...]
+
+    def entries(chosen, masked=False):
+        tiles = [(b, slot, h, head_rows(h)) for b, slot in chosen for h in range(heads)]
+        scores = [dot(key_rows[slot, h], scaled[b, rows]) for b, slot, h, rows in tiles]
+        if masked:
+            keep = causal()
+            scores = [jnp.where(keep, tile, NEG) for tile in scores]
+        grads = [dot(value_rows[slot, h], grad_cols[b, rows]) for b, slot, h, rows in tiles]
+        probs = [jnp.exp(tile - lse_ref[b, h]) for tile, (b, _, h, _) in zip(scores, tiles)]
+        grads = [(p * (g - sums[b, h])).astype(BF16)
+                 for p, g, (b, _, h, _) in zip(probs, grads, tiles)]
+        probs = [p.astype(BF16) for p in probs]
+        for p, g, (b, slot, h, rows) in zip(probs, grads, tiles):
+            acc_ref[b, rows] += dot(key_cols[slot, rows], g)
+            grad_keys[slot, rows] += dot(scaled[b, rows], g, 1, 1)
+            grad_values[slot, rows] += dot(grad_cols[b, rows], p, 1, 1)
+
+    def item_at(i):
+        return lax.div(items[i], slots), lax.rem(items[i], slots)
+
+    if diagonal:
+
+        @pl.loop(0, blocks // 2)
+        def _(i):
+            entries([(2 * i, 2 * i), (2 * i + 1, 2 * i + 1)], True)
+
+    @pl.loop(0, lax.div(found, 2))
+    def _(i):
+        entries([item_at(2 * i), item_at(2 * i + 1)])
+
+    @pl.when(lax.rem(found, 2) == 1)
+    def _():
+        entries([item_at(found - 1)])
 
     if last:
-        dq_ref[...] = (acc_ref[...] * SCALE).astype(BF16)
+        for b in range(blocks):
+            dq_ref[:, b * BLOCK:(b + 1) * BLOCK] = (acc_ref[b] * SCALE).astype(BF16)
     else:
         dq_ref[...] = acc_ref[...]
     for r, ref in enumerate(outs):
@@ -371,7 +414,8 @@
     given = () if dq is None else (dq,)
     return pl.pallas_call(
         functools.partial(backward_kernel, regions, diagonal, last),
-        out_shape=(jax.ShapeDtypeStruct((width, tokens), BF16 if last else F32),)
+        out_shape=(jax.ShapeDtypeStruct((width, tokens), BF16) if last else
+                   jax.ShapeDtypeStruct((blocks, width, BLOCK), F32),)
         + (jax.ShapeDtypeStruct((2, width, tokens), F32 if diagonal else BF16),) * len(regions),
         in_specs=smem(3) + vmem(7 + len(slabs) + len(given)),
         out_specs=tuple(vmem(1 + len(regions))),
@@ -380,10 +424,12 @@
             pltpu.VMEM((slots, heads, BLOCK, HEAD_DIM), BF16),
             pltpu.VMEM((slots, width, BLOCK), BF16),
             pltpu.VMEM((blocks, width, BLOCK), BF16),
+            pltpu.VMEM((blocks, width, BLOCK), BF16),
+            pltpu.VMEM((blocks, heads, 1, BLOCK), F32),
             pltpu.VMEM((slots, width, BLOCK), F32),
             pltpu.VMEM((slots, width, BLOCK), F32),
             pltpu.SMEM((blocks * LIST,), jnp.int32),
-            pltpu.VMEM((width, tokens), F32),
+            pltpu.VMEM((blocks, width, BLOCK), F32),
         ],
         compiler_params=pltpu.CompilerParams(vmem_limit_bytes=48 << 20),
         cost_estimate=pl.CostEstimate(

time: 225 us -> 177 us (0.79); the launches traced: 224 us -> 173 us
  Pallas kernels: 109 us -> 29.8 us
  waiting for transfers between devices: 34.4 us -> 81.4 us
  starting transfers between devices: 65.6 us -> 46.9 us
    pallas_call x4, Pallas kernels: 54.9 us -> 12.6 us  [backward(): pl.pallas_call(functools.partial(backward_kernel, regions, diagonal, last...]
    pallas_call x5, Pallas kernels: 46.5 us -> 9.64 us  [forward(): pl.pallas_call(functools.partial(forward_kernel, regions, not state, clos...]
    ppermute x2, starting transfers between devices: 33.5 us -> 2.1 us  [mate(): lax.ppermute(array, 'row', [(i, i ^ 1) for i in range(lax.axis_size('row'...]
    ppermute x4, waiting for transfers between devices: 24.1 us -> 45.2 us  [hop(): return lax.ppermute(array, 'row', pairs)]
    ppermute x2, waiting for transfers between devices: 0.01 us -> 17 us  [mate(): lax.ppermute(array, 'row', [(i, i ^ 1) for i in range(lax.axis_size('row'...]
    ppermute x4, starting transfers between devices: 11.2 us -> 18.3 us  [hop(): return lax.ppermute(array, 'row', pairs)]
    ppermute x2, waiting for transfers between devices: 0.01 us -> 6.41 us  [downward(): lax.ppermute(array, 'row', [(i + 1, i) for i in range(0, lax.axis_size('r...]
    ppermute x2, starting transfers between devices: 0.01 us -> 6.09 us  [mirror(): return lax.ppermute(array, 'row', [(i, size - 1 - i) for i in range(size)])]
  transfers between devices with their start and end apart: 24 -> 24, of which waited for: 6 -> 12; matrix products, arithmetic and copies ran while one was open for 0% -> 0% of each run, Pallas kernels for 45% -> 13%
where the time goes in v1:
time: 177 us; the launch traced here: 173 us
  waiting for transfers between devices  81.4 us (46%)
  starting transfers between devices  46.9 us (26%)
  Pallas kernels  29.8 us (17%)
  local copies, waits for them, and re-layouts  8.98 us (5%)
  other arithmetic  5.23 us (3%)
    ppermute x4, waiting for transfers between devices, hop(): return lax.ppermute(array, 'row', pairs)  45.2 us
    ppermute x4, starting transfers between devices, hop(): return lax.ppermute(array, 'row', pairs)  18.3 us
    ppermute x2, waiting for transfers between devices, mate(): lax.ppermute(array, 'row', [(i, i ^ 1) for i in range(lax.axis_size('row'...  17 us
    pallas_call x4, Pallas kernels, backward(): pl.pallas_call(functools.partial(backward_kernel, regions, diagonal, last...  12.6 us
    ppermute x2, starting transfers between devices, upward(): lax.ppermute(array, 'row', [(i, i + 1) for i in range(0, lax.axis_size('r...  10.7 us
    pallas_call x5, Pallas kernels, forward(): pl.pallas_call(functools.partial(forward_kernel, regions, not state, clos...  9.64 us
    unnamed x58, local copies, waits for them, and re-layouts  7.98 us
    ppermute x12, starting transfers between devices, across(): lax.ppermute(array, 'col', [(i, i ^ bits) for i in range(lax.axis_size('c...  7.21 us
  transfers between devices with their start and end apart: 24, of which 12 were waited for; matrix products, arithmetic and copies ran while one was open for 0% of the time, Pallas kernels for 13%

profile of v1, /device:TPU:8, one launch (start us, length us, event | category | flops | bytes accessed | tf_op | source)
XLA Modules:
  0.0 173.4 jit_solution(4800079172612695771)
XLA Ops:
  0.7 1.2 pad_maximum_fusion.refs_0_
  1.9 3.5 %collective-permute-start = (bf16[2,192,1024]{2,1,0:T(8,128)(2,1)S(1)}, bf16[2,192,1024]{2,1,0:T(8,128)(2,1)S(1)}, u32[]{:S(2)}, u32[]{:S(2)}) collective-permute-start(bf16[2,192,1024]{2,1,0:T(8,128)(2,1)S(1)} %pad_maximum_fusion.refs_0_), channel_id=1, source_target_pairs={{0,8},{4,12},{8,16},{12,20},{16,24},{20,28},{1,9},{5,13},{9,17},{1... | collective-permute-start | bytes 2359304 | tf_op jit(solution)/shard_map/ppermute | solution.py:37
  5.4 0.1 pad_add_fusion.place_ref
  5.5 2.8 %shard_map.147 = (f32[4,192,256]{2,1,0:T(8,128)S(1)}, f32[4,6,1,256]{3,2,1,0:T(1,128)S(1)}) custom-call(s32[4,16]{1,0:T(4,128)S(1)} %copy-done.14, s32[4]{0:T(128)S(1)} %copy-done.15, s32[2]{0:T(128)S(1)} %pad_add_fusion.place_ref, bf16[192,1024]{1,0:T(8,128)(2,1)S(1)} %copy-done.9, bf16[2,192,1024]{2,1,0:T(8,128)(2,1)S(1)} %pad_maximum_fusion.refs_0_), custom_call_target="tpu_custom_call" | custom-call | flops 1000000000 | bytes 6291456 | tf_op jit(solution)/shard_map/pallas_call | solution.py:262
  8.3 14.7 %collective-permute-done.refs_0_ = bf16[2,192,1024]{2,1,0:T(8,128)(2,1)S(1)} collective-permute-done((bf16[2,192,1024]{2,1,0:T(8,128)(2,1)S(1)}, bf16[2,192,1024]{2,1,0:T(8,128)(2,1)S(1)}, u32[]{:S(2)}, u32[]{:S(2)}) %collective-permute-start) | collective-permute-done | bytes 786464 | tf_op jit(solution)/shard_map/ppermute | solution.py:37
  23.1 3.6 %collective-permute-start.1 = (bf16[2,192,1024]{2,1,0:T(8,128)(2,1)S(1)}, bf16[2,192,1024]{2,1,0:T(8,128)(2,1)}, u32[]{:S(2)}, u32[]{:S(2)}) collective-permute-start(bf16[2,192,1024]{2,1,0:T(8,128)(2,1)S(1)} %collective-permute-done.refs_0_), channel_id=1, source_target_pairs={{0,8},{4,12},{8,16},{12,20},{16,24},{20,28},{1,9},{5,13},{9,17},{1... | collective-permute-start | bytes 2359304 | tf_op jit(solution)/shard_map/ppermute | solution.py:37
  26.7 4.3 %collective-permute-start.5 = (bf16[2,192,1024]{2,1,0:T(8,128)(2,1)S(1)}, bf16[2,192,1024]{2,1,0:T(8,128)(2,1)}, u32[]{:S(2)}, u32[]{:S(2)}) collective-permute-start(bf16[2,192,1024]{2,1,0:T(8,128)(2,1)S(1)} %pad_maximum_fusion.refs_0_), channel_id=1, source_target_pairs={{0,4},{8,12},{16,20},{24,28},{1,5},{9,13},{17,21},{25,29},{2,6},{1... | collective-permute-start | bytes 2359304 | tf_op jit(solution)/shard_map/ppermute | solution.py:45
  31.0 1.3 collective-permute-start.4
  32.3 6.4 %collective-permute-start.3 = (bf16[2,192,1024]{2,1,0:T(8,128)(2,1)S(1)}, bf16[2,192,1024]{2,1,0:T(8,128)(2,1)}, u32[]{:S(2)}, u32[]{:S(2)}) collective-permute-start(bf16[2,192,1024]{2,1,0:T(8,128)(2,1)S(1)} %collective-permute-done.refs_0_), channel_id=1, source_target_pairs={{0,4},{8,12},{16,20},{24,28},{1,5},{9,13},{17,21},{25,29},{2,6},{1... | collective-permute-start | bytes 2359304 | tf_op jit(solution)/shard_map/ppermute | solution.py:45
  38.7 1.1 shard_map.148
  39.8 0.9 copy-done.18
  40.7 2.9 %collective-permute-done.1.refs_0_.refs_2_ = bf16[2,192,1024]{2,1,0:T(8,128)(2,1)} collective-permute-done((bf16[2,192,1024]{2,1,0:T(8,128)(2,1)S(1)}, bf16[2,192,1024]{2,1,0:T(8,128)(2,1)}, u32[]{:S(2)}, u32[]{:S(2)}) %collective-permute-start.1) | collective-permute-done | bytes 786464 | tf_op jit(solution)/shard_map/ppermute | solution.py:37
  43.6 1.3 collective-permute-start.2
  44.9 1.9 %shard_map.152 = f32[48,256]{1,0:T(8,128)} custom-call(s32[2]{0:T(128)} %copy-done.4, s32[1,1024]{1,0:T(1,128)} %bitcast.17, f32[48,1024]{1,0:T(8,128)} %bitcast.16), custom_call_target="tpu_custom_call" | custom-call | tf_op jit(solution)/shard_map/pallas_call | solution.py:88
  46.8 4.6 %collective-permute-start.12 = (f32[48,256]{1,0:T(8,128)}, f32[48,256]{1,0:T(8,128)S(1)}, u32[]{:S(2)}, u32[]{:S(2)}) collective-permute-start(f32[48,256]{1,0:T(8,128)} %shard_map.152), channel_id=1, source_target_pairs={{0,28},{4,24},{8,20},{12,16},{16,12},{20,8},{24,4},{28,0},{1,29},{... | collective-permute-start | bytes 147464 | tf_op jit(solution)/shard_map/ppermute | solution.py:54
  51.3 3.2 %collective-permute-done.4.refs_0_ = bf16[2,192,1024]{2,1,0:T(8,128)(2,1)} collective-permute-done((bf16[2,192,1024]{2,1,0:T(8,128)(2,1)S(1)}, bf16[2,192,1024]{2,1,0:T(8,128)(2,1)}, u32[]{:S(2)}, u32[]{:S(2)}) %collective-permute-start.4) | collective-permute-done | bytes 786464 | tf_op jit(solution)/shard_map/ppermute | solution.py:49
  54.5 1.5 collective-permute-start.10
  56.0 0.6 copy-done.5
  56.6 1.1 copy-done.19
  57.8 1.9 %shard_map.149 = (f32[4,192,256]{2,1,0:T(8,128)S(1)}, f32[4,6,1,256]{3,2,1,0:T(1,128)S(1)}) custom-call(s32[4,16]{1,0:T(4,128)S(1)} %copy-done.14, s32[4]{0:T(128)S(1)} %copy-done.15, s32[2]{0:T(128)S(1)} %copy-done.5, bf16[192,1024]{1,0:T(8,128)(2,1)S(1)} %copy-done.9, bf16[2,192,1024]{2,1,0:T(8,128)(2,1)} %collective-permute-done.4.refs_0_, ...), custom_call_target="tpu_custom_call" | custom-call | flops 1000000000 | bytes 6291456 | tf_op jit(solution)/shard_map/pallas_call | solution.py:262
  59.7 4.0 %collective-permute-done.3.refs_1_ = bf16[2,192,1024]{2,1,0:T(8,128)(2,1)} collective-permute-done((bf16[2,192,1024]{2,1,0:T(8,128)(2,1)S(1)}, bf16[2,192,1024]{2,1,0:T(8,128)(2,1)}, u32[]{:S(2)}, u32[]{:S(2)}) %collective-permute-start.3) | collective-permute-done | bytes 786464 | tf_op jit(solution)/shard_map/ppermute | solution.py:45
  63.7 1.9 %shard_map.150 = (f32[4,192,256]{2,1,0:T(8,128)S(1)}, f32[4,6,1,256]{3,2,1,0:T(1,128)S(1)}) custom-call(s32[4,16]{1,0:T(4,128)S(1)} %copy-done.14, s32[4]{0:T(128)S(1)} %copy-done.15, s32[2]{0:T(128)S(1)} %copy-done.5, bf16[192,1024]{1,0:T(8,128)(2,1)S(1)} %copy-done.9, bf16[2,192,1024]{2,1,0:T(8,128)(2,1)} %collective-permute-done.1.refs_0_.refs_2_, ...), custom_call_target="tpu_custom_call" | custom-call | flops 1000000000 | bytes 6291456 | tf_op jit(solution)/shard_map/pallas_call | solution.py:262
  65.6 3.2 %collective-permute-done.2.refs_0_ = bf16[2,192,1024]{2,1,0:T(8,128)(2,1)} collective-permute-done((bf16[2,192,1024]{2,1,0:T(8,128)(2,1)}, bf16[2,192,1024]{2,1,0:T(8,128)(2,1)}, u32[]{:S(2)}, u32[]{:S(2)}) %collective-permute-start.2) | collective-permute-done | bytes 786464 | tf_op jit(solution)/shard_map/ppermute | solution.py:49
  68.8 1.9 %shard_map.151 = (bf16[192,1024]{1,0:T(8,128)(2,1)S(1)}, f32[4,3,1,256]{3,2,1,0:T(1,128)S(1)}) custom-call(s32[4,16]{1,0:T(4,128)S(1)} %copy-done.14, s32[4]{0:T(128)S(1)} %copy-done.15, s32[2]{0:T(128)S(1)} %copy-done.5, bf16[192,1024]{1,0:T(8,128)(2,1)S(1)} %copy-done.9, bf16[2,192,1024]{2,1,0:T(8,128)(2,1)} %collective-permute-done.2.refs_0_, ...), custom_call_target="tpu_custom_call" | custom-call | flops 1000000000 | bytes 6291456 | tf_op jit(solution)/shard_map/pallas_call | solution.py:262
  70.7 0.1 constant_dynamic-slice_fusion
  70.7 0.1 collective-permute-start.8
  70.8 1.6 collective-permute-start.7
  72.4 0.3 collective-permute-start.6
  72.7 3.2 %collective-permute-done.8.a3 = bf16[192,256]{1,0:T(8,128)(2,1)S(1)} collective-permute-done((bf16[192,256]{1,0:T(8,128)(2,1)S(1)}, bf16[192,256]{1,0:T(8,128)(2,1)S(1)}, u32[]{:S(2)}, u32[]{:S(2)}) %collective-permute-start.8) | collective-permute-done | bytes 98336 | tf_op jit(solution)/shard_map/ppermute | solution.py:58
  75.9 2.2 %collective-permute-done.7.a2 = bf16[192,256]{1,0:T(8,128)(2,1)S(1)} collective-permute-done((bf16[192,256]{1,0:T(8,128)(2,1)S(1)}, bf16[192,256]{1,0:T(8,128)(2,1)S(1)}, u32[]{:S(2)}, u32[]{:S(2)}) %collective-permute-start.7) | collective-permute-done | bytes 98336 | tf_op jit(solution)/shard_map/ppermute | solution.py:58
  78.0 2.5 %shard_map.153 = (f32[48,256]{1,0:T(8,128)S(1)}, bf16[192,256]{1,0:T(8,128)(2,1)S(1)}, bf16[192,256]{1,0:T(8,128)(2,1)S(1)}, bf16[192,256]{1,0:T(8,128)(2,1)S(1)}, bf16[192,256]{1,0:T(8,128)(2,1)S(1)}) custom-call(s32[2]{0:T(128)S(1)} %copy-done.6, bf16[192,256]{1,0:T(8,128)(2,1)S(1)} %get-tuple-element.101.a0, ...), custom_call_target="tpu_custom_call" | custom-call | tf_op jit(solution)/shard_map/pallas_call | solution.py:313
  80.5 0.1 collective-permute-start.13
  80.6 0.3 collective-permute-start.14
  81.0 1.5 collective-permute-start.15
  82.4 1.5 collective-permute-start.16
  84.0 3.5 %collective-permute-done.16.x_ref = f32[48,256]{1,0:T(8,128)S(1)} collective-permute-done((f32[48,256]{1,0:T(8,128)S(1)}, f32[48,256]{1,0:T(8,128)S(1)}, u32[]{:S(2)}, u32[]{:S(2)}) %collective-permute-start.16) | collective-permute-done | bytes 49184 | tf_op jit(solution)/shard_map/ppermute | solution.py:54
  87.5 0.6 copy-done.27
  88.1 4.3 %shard_map.154 = (f32[4,192,256]{2,1,0:T(8,128)S(1)}, bf16[2,192,1024]{2,1,0:T(8,128)(2,1)}, bf16[2,192,1024]{2,1,0:T(8,128)(2,1)S(1)}) custom-call(s32[4,16]{1,0:T(4,128)S(1)} %copy-done.14, s32[4]{0:T(128)S(1)} %copy-done.15, s32[2]{0:T(128)S(1)} %copy-done.6, bf16[192,1024]{1,0:T(8,128)(2,1)S(1)} %copy-done.9, ...), custom_call_target="tpu_custom_call" | custom-call | flops 1000000000 | bytes 8388608 | tf_op jit(solution)/shard_map/pallas_call | solution.py:415
  92.3 0.9 copy-done.16
  93.2 0.3 collective-permute-start.17
  93.6 1.7 shard_map.155.p0
  95.2 1.1 collective-permute-start.19
  96.4 0.7 collective-permute-start.18
  97.1 0.9 copy-done.11
  98.0 1.1 copy-done.17
  99.1 2.4 %shard_map.156 = (f32[4,192,256]{2,1,0:T(8,128)S(1)}, bf16[2,192,1024]{2,1,0:T(8,128)(2,1)S(1)}) custom-call(s32[4,16]{1,0:T(4,128)S(1)} %copy-done.14, s32[4]{0:T(128)S(1)} %copy-done.15, s32[2]{0:T(128)S(1)} %copy-done.7, bf16[192,1024]{1,0:T(8,128)(2,1)S(1)} %copy-done.9, bf16[192,1024]{1,0:T(8,128)(2,1)S(1)} %get-tuple-element.64.att_ref, ...), custom_call_target="tpu_custom_call" | custom-call | flops 1000000000 | bytes 8388608 | tf_op jit(solution)/shard_map/pallas_call | solution.py:415
  101.5 0.0 copy-start.12
  101.5 1.7 %collective-permute-start.21 = (bf16[2,192,1024]{2,1,0:T(8,128)(2,1)S(1)}, bf16[2,192,1024]{2,1,0:T(8,128)(2,1)S(1)}, u32[]{:S(2)}, u32[]{:S(2)}) collective-permute-start(bf16[2,192,1024]{2,1,0:T(8,128)(2,1)S(1)} %get-tuple-element.90), channel_id=1, source_target_pairs={{0,4},{4,0},{8,12},{12,8},{16,20},{20,16},{24,28},{28,24},{1,5},{5... | collective-permute-start | bytes 2359304 | tf_op jit(solution)/shard_map/ppermute | solution.py:41
  103.3 10.7 %collective-permute-done.17 = bf16[2,192,1024]{2,1,0:T(8,128)(2,1)} collective-permute-done((bf16[2,192,1024]{2,1,0:T(8,128)(2,1)}, bf16[2,192,1024]{2,1,0:T(8,128)(2,1)}, u32[]{:S(2)}, u32[]{:S(2)}) %collective-permute-start.17) | collective-permute-done | bytes 786464 | tf_op jit(solution)/shard_map/ppermute | solution.py:41
  114.0 0.1 select_add_fusion
  114.2 0.6 copy-done.25
  114.8 0.0 copy-done.26
  114.8 6.8 %collective-permute-start.22 = (bf16[2,192,1024]{2,1,0:T(8,128)(2,1)S(1)}, bf16[2,192,1024]{2,1,0:T(8,128)(2,1)S(1)}, u32[]{:S(2)}, u32[]{:S(2)}) collective-permute-start(bf16[2,192,1024]{2,1,0:T(8,128)(2,1)S(1)} %select_add_fusion), channel_id=1, source_target_pairs={{8,0},{12,4},{16,8},{20,12},{24,16},{28,20},{9,1},{13,5},{17,9},{2... | collective-permute-start | bytes 2359304 | tf_op jit(solution)/shard_map/ppermute | solution.py:37
  121.6 1.5 shard_map.158
  123.2 6.3 %collective-permute-done.21 = bf16[2,192,1024]{2,1,0:T(8,128)(2,1)S(1)} collective-permute-done((bf16[2,192,1024]{2,1,0:T(8,128)(2,1)S(1)}, bf16[2,192,1024]{2,1,0:T(8,128)(2,1)S(1)}, u32[]{:S(2)}, u32[]{:S(2)}) %collective-permute-start.21) | collective-permute-done | bytes 786464 | tf_op jit(solution)/shard_map/ppermute | solution.py:41
  129.5 8.9 %collective-permute-done.22 = bf16[2,192,1024]{2,1,0:T(8,128)(2,1)S(1)} collective-permute-done((bf16[2,192,1024]{2,1,0:T(8,128)(2,1)S(1)}, bf16[2,192,1024]{2,1,0:T(8,128)(2,1)S(1)}, u32[]{:S(2)}, u32[]{:S(2)}) %collective-permute-start.22) | collective-permute-done | bytes 786464 | tf_op jit(solution)/shard_map/ppermute | solution.py:37
  138.4 2.3 %add_add_fusion = bf16[2,192,1024]{2,1,0:T(8,128)(2,1)} fusion(bf16[2,192,1024]{2,1,0:T(8,128)(2,1)S(1)} %collective-permute-done.22, bf16[2,192,1024]{2,1,0:T(8,128)(2,1)S(1)} %get-tuple-element.89, bf16[2,192,1024]{2,1,0:T(8,128)(2,1)S(1)} %collective-permute-done.21, bf16[2,192,1024]{2,1,0:T(8,128)(2,1)} %collective-permute-done.17, pred[]{:T(512)S(6)} %eq.5), kind=kLoop, calls=%fused_computation.2 | loop fusion | flops 1179648 | bytes 3932161 | tf_op jit(solution)/shard_map/add | solution.py:497
  140.7 4.4 %collective-permute-start.23 = (bf16[2,192,1024]{2,1,0:T(8,128)(2,1)}, bf16[2,192,1024]{2,1,0:T(8,128)(2,1)}, u32[]{:S(2)}, u32[]{:S(2)}) collective-permute-start(bf16[2,192,1024]{2,1,0:T(8,128)(2,1)} %add_add_fusion), channel_id=1, source_target_pairs={{8,0},{12,4},{16,8},{20,12},{24,16},{28,20},{9,1},{13,5},{17,9},{2... | collective-permute-start | bytes 2359304 | tf_op jit(solution)/shard_map/ppermute | solution.py:37
  145.0 1.6 shard_map.157
  146.6 1.1 copy-done.21
  147.8 4.5 %shard_map.159 = (bf16[192,1024]{1,0:T(8,128)(2,1)}, f32[2,192,1024]{2,1,0:T(8,128)S(1)}) custom-call(s32[4,16]{1,0:T(4,128)S(1)} %copy-done.14, s32[4]{0:T(128)S(1)} %copy-done.15, s32[2]{0:T(128)S(1)} %copy-done.8, bf16[192,1024]{1,0:T(8,128)(2,1)S(1)} %copy-done.9, bf16[192,1024]{1,0:T(8,128)(2,1)S(1)} %get-tuple-element.64.att_ref, ...), custom_call_target="tpu_custom_call" | custom-call | flops 1000000000 | bytes 8388608 | tf_op jit(solution)/shard_map/pallas_call | solution.py:415
  152.2 18.6 %collective-permute-done.23 = bf16[2,192,1024]{2,1,0:T(8,128)(2,1)} collective-permute-done((bf16[2,192,1024]{2,1,0:T(8,128)(2,1)}, bf16[2,192,1024]{2,1,0:T(8,128)(2,1)}, u32[]{:S(2)}, u32[]{:S(2)}) %collective-permute-start.23) | collective-permute-done | bytes 786464 | tf_op jit(solution)/shard_map/ppermute | solution.py:37
  170.9 1.6 add_convert_fusion
  172.4 0.9 slice_bitcast_fusion
  (63 shorter events, 0.1 us)
Async XLA Ops:
  0.6 4.8 %copy-start.15 = (s32[4]{0:T(128)S(1)}, s32[4]{0:T(128)}, u32[]{:S(2)}) copy-start(s32[4]{0:T(128)} %counts_ref.17) | copy-start | bytes 52
  0.6 4.8 %copy-start.14 = (s32[4,16]{1,0:T(4,128)S(1)}, s32[4,16]{1,0:T(4,128)}, u32[]{:S(2)}) copy-start(s32[4,16]{1,0:T(4,128)} %lists_ref.17) | copy-start | bytes 772
  0.7 4.8 %copy-start.9 = (bf16[192,1024]{1,0:T(8,128)(2,1)S(1)}, bf16[192,1024]{1,0:T(8,128)(2,1)}, u32[]{:S(2)}) copy-start(bf16[192,1024]{1,0:T(8,128)(2,1)} %q_ref.17) | copy-start | bytes 1179652
  1.9 21.2 %collective-permute-start = (bf16[2,192,1024]{2,1,0:T(8,128)(2,1)S(1)}, bf16[2,192,1024]{2,1,0:T(8,128)(2,1)S(1)}, u32[]{:S(2)}, u32[]{:S(2)}) collective-permute-start(bf16[2,192,1024]{2,1,0:T(8,128)(2,1)S(1)} %pad_maximum_fusion.refs_0_), channel_id=1, source_target_pairs={{0,8},{4,12},{8,16},{12,20},{16,24},{20,28},{1,9},{5,13},{9,17},{1... | collective-permute-start | bytes 2359304 | tf_op jit(solution)/shard_map/ppermute | solution.py:37
  5.5 33.2 %copy-start.4 = (s32[2]{0:T(128)}, s32[2]{0:T(128)S(1)}, u32[]{:S(2)}) copy-start(s32[2]{0:T(128)S(1)} %pad_add_fusion.place_ref) | copy-start | bytes 28
  23.1 28.2 %copy-start.1 = (bf16[192,768]{1,0:T(8,128)(2,1)S(1)}, bf16[192,768]{1,0:T(8,128)(2,1)}, u32[]{:S(2)}) copy-start(bf16[192,768]{1,0:T(8,128)(2,1)} %w0) | copy-start | bytes 884740
  23.1 20.5 %collective-permute-start.1 = (bf16[2,192,1024]{2,1,0:T(8,128)(2,1)S(1)}, bf16[2,192,1024]{2,1,0:T(8,128)(2,1)}, u32[]{:S(2)}, u32[]{:S(2)}) collective-permute-start(bf16[2,192,1024]{2,1,0:T(8,128)(2,1)S(1)} %collective-permute-done.refs_0_), channel_id=1, source_target_pairs={{0,8},{4,12},{8,16},{12,20},{16,24},{20,28},{1,9},{5,13},{9,17},{1... | collective-permute-start | bytes 2359304 | tf_op jit(solution)/shard_map/ppermute | solution.py:37
  26.7 24.6 %collective-permute-start.5 = (bf16[2,192,1024]{2,1,0:T(8,128)(2,1)S(1)}, bf16[2,192,1024]{2,1,0:T(8,128)(2,1)}, u32[]{:S(2)}, u32[]{:S(2)}) collective-permute-start(bf16[2,192,1024]{2,1,0:T(8,128)(2,1)S(1)} %pad_maximum_fusion.refs_0_), channel_id=1, source_target_pairs={{0,4},{8,12},{16,20},{24,28},{1,5},{9,13},{17,21},{25,29},{2,6},{1... | collective-permute-start | bytes 2359304 | tf_op jit(solution)/shard_map/ppermute | solution.py:45
  31.0 23.5 %collective-permute-start.4 = (bf16[2,192,1024]{2,1,0:T(8,128)(2,1)S(1)}, bf16[2,192,1024]{2,1,0:T(8,128)(2,1)}, u32[]{:S(2)}, u32[]{:S(2)}) collective-permute-start(bf16[2,192,1024]{2,1,0:T(8,128)(2,1)S(1)} %collective-permute-done.refs_0_), channel_id=1, source_target_pairs={{4,0},{12,8},{20,16},{28,24},{5,1},{13,9},{21,17},{29,25},{6,2},{1... | collective-permute-start | bytes 2359304 | tf_op jit(solution)/shard_map/ppermute | solution.py:49
  32.3 31.4 %collective-permute-start.3 = (bf16[2,192,1024]{2,1,0:T(8,128)(2,1)S(1)}, bf16[2,192,1024]{2,1,0:T(8,128)(2,1)}, u32[]{:S(2)}, u32[]{:S(2)}) collective-permute-start(bf16[2,192,1024]{2,1,0:T(8,128)(2,1)S(1)} %collective-permute-done.refs_0_), channel_id=1, source_target_pairs={{0,4},{8,12},{16,20},{24,28},{1,5},{9,13},{17,21},{25,29},{2,6},{1... | collective-permute-start | bytes 2359304 | tf_op jit(solution)/shard_map/ppermute | solution.py:45
  39.8 0.9 copy-start.18
  43.6 25.2 %collective-permute-start.2 = (bf16[2,192,1024]{2,1,0:T(8,128)(2,1)}, bf16[2,192,1024]{2,1,0:T(8,128)(2,1)}, u32[]{:S(2)}, u32[]{:S(2)}) collective-permute-start(bf16[2,192,1024]{2,1,0:T(8,128)(2,1)} %collective-permute-done.1.refs_0_.refs_2_), channel_id=1, source_target_pairs={{4,0},{12,8},{20,16},{28,24},{5,1},{13,9},{21,17},{29,25},{6,2},{1... | collective-permute-start | bytes 2359304 | tf_op jit(solution)/shard_map/ppermute | solution.py:49
  46.8 24.1 %collective-permute-start.12 = (f32[48,256]{1,0:T(8,128)}, f32[48,256]{1,0:T(8,128)S(1)}, u32[]{:S(2)}, u32[]{:S(2)}) collective-permute-start(f32[48,256]{1,0:T(8,128)} %shard_map.152), channel_id=1, source_target_pairs={{0,28},{4,24},{8,20},{12,16},{16,12},{20,8},{24,4},{28,0},{1,29},{... | collective-permute-start | bytes 147464 | tf_op jit(solution)/shard_map/ppermute | solution.py:54
  51.3 21.1 %collective-permute-start.11 = (bf16[192,768]{1,0:T(8,128)(2,1)S(1)}, bf16[192,768]{1,0:T(8,128)(2,1)S(1)}, u32[]{:S(2)}, u32[]{:S(2)}) collective-permute-start(bf16[192,768]{1,0:T(8,128)(2,1)S(1)} %copy-done.1), channel_id=1, source_target_pairs={{0,3},{1,2},{2,1},{3,0},{4,7},{5,6},{6,5},{7,4},{8,11},{9,10},{10,... | collective-permute-start | bytes 884744 | tf_op jit(solution)/shard_map/ppermute | solution.py:58
  54.5 18.1 %collective-permute-start.10 = (bf16[192,768]{1,0:T(8,128)(2,1)S(1)}, bf16[192,768]{1,0:T(8,128)(2,1)S(1)}, u32[]{:S(2)}, u32[]{:S(2)}) collective-permute-start(bf16[192,768]{1,0:T(8,128)(2,1)S(1)} %copy-done.1), channel_id=1, source_target_pairs={{0,2},{1,3},{2,0},{3,1},{4,6},{5,7},{6,4},{7,5},{8,10},{9,11},{10,... | collective-permute-start | bytes 884744 | tf_op jit(solution)/shard_map/ppermute | solution.py:58
  56.0 0.6 copy-start.5
  56.6 1.1 copy-start.19
  63.7 9.0 %collective-permute-start.9 = (bf16[192,768]{1,0:T(8,128)(2,1)S(1)}, bf16[192,768]{1,0:T(8,128)(2,1)S(1)}, u32[]{:S(2)}, u32[]{:S(2)}) collective-permute-start(bf16[192,768]{1,0:T(8,128)(2,1)S(1)} %copy-done.1), channel_id=1, source_target_pairs={{0,1},{1,0},{2,3},{3,2},{4,5},{5,4},{6,7},{7,6},{8,9},{9,8},{10,11... | collective-permute-start | bytes 884744 | tf_op jit(solution)/shard_map/ppermute | solution.py:58
  68.8 3.9 %copy-start.28 = (f32[768]{0:T(1024)S(1)}, f32[768]{0:T(1024)}, u32[]{:S(2)}) copy-start(f32[768]{0:T(1024)} %param.19) | copy-start | bytes 9220
  68.8 9.2 %copy-start = (bf16[1024,768]{1,0:T(8,128)(2,1)S(1)}, bf16[1024,768]{1,0:T(8,128)(2,1)}, u32[]{:S(2)}) copy-start(bf16[1024,768]{1,0:T(8,128)(2,1)} %stream_ref.1) | copy-start | bytes 4718596
  68.8 9.2 %copy-start.2 = (f32[1024,48]{0,1:T(8,128)S(1)}, f32[1024,48]{0,1:T(8,128)}, u32[]{:S(2)}) copy-start(f32[1024,48]{0,1:T(8,128)} %param.21) | copy-start | bytes 589828
  68.8 9.2 %copy-start.3 = (bf16[96,768]{1,0:T(8,128)(2,1)S(1)}, bf16[96,768]{1,0:T(8,128)(2,1)}, u32[]{:S(2)}) copy-start(bf16[96,768]{1,0:T(8,128)(2,1)} %head_ref.1) | copy-start | bytes 442372
  68.8 9.3 %copy-start.6 = (s32[2]{0:T(128)S(1)}, s32[2]{0:T(128)}, u32[]{:S(2)}) copy-start(s32[2]{0:T(128)} %copy-done.4) | copy-start | bytes 28
  70.7 5.1 %collective-permute-start.8 = (bf16[192,256]{1,0:T(8,128)(2,1)S(1)}, bf16[192,256]{1,0:T(8,128)(2,1)S(1)}, u32[]{:S(2)}, u32[]{:S(2)}) collective-permute-start(bf16[192,256]{1,0:T(8,128)(2,1)S(1)} %get-tuple-element.98), channel_id=1, source_target_pairs={{0,3},{1,2},{2,1},{3,0},{4,7},{5,6},{6,5},{7,4},{8,11},{9,10},{10,... | collective-permute-start | bytes 294920 | tf_op jit(solution)/shard_map/ppermute | solution.py:58
  70.8 7.2 %collective-permute-start.7 = (bf16[192,256]{1,0:T(8,128)(2,1)S(1)}, bf16[192,256]{1,0:T(8,128)(2,1)S(1)}, u32[]{:S(2)}, u32[]{:S(2)}) collective-permute-start(bf16[192,256]{1,0:T(8,128)(2,1)S(1)} %get-tuple-element.99), channel_id=1, source_target_pairs={{0,2},{1,3},{2,0},{3,1},{4,6},{5,7},{6,4},{7,5},{8,10},{9,11},{10,... | collective-permute-start | bytes 294920 | tf_op jit(solution)/shard_map/ppermute | solution.py:58
  72.4 5.6 %collective-permute-start.6 = (bf16[192,256]{1,0:T(8,128)(2,1)S(1)}, bf16[192,256]{1,0:T(8,128)(2,1)S(1)}, u32[]{:S(2)}, u32[]{:S(2)}) collective-permute-start(bf16[192,256]{1,0:T(8,128)(2,1)S(1)} %get-tuple-element.100), channel_id=1, source_target_pairs={{0,1},{1,0},{2,3},{3,2},{4,5},{5,4},{6,7},{7,6},{8,9},{9,8},{10,11... | collective-permute-start | bytes 294920 | tf_op jit(solution)/shard_map/ppermute | solution.py:58
  80.5 6.9 %collective-permute-start.13 = (bf16[192,256]{1,0:T(8,128)(2,1)S(1)}, bf16[192,256]{1,0:T(8,128)(2,1)S(1)}, u32[]{:S(2)}, u32[]{:S(2)}) collective-permute-start(bf16[192,256]{1,0:T(8,128)(2,1)S(1)} %get-tuple-element.68), channel_id=1, source_target_pairs={{0,1},{1,0},{2,3},{3,2},{4,5},{5,4},{6,7},{7,6},{8,9},{9,8},{10,11... | collective-permute-start | bytes 294920 | tf_op jit(solution)/shard_map/ppermute | solution.py:58
  80.6 6.8 %collective-permute-start.14 = (bf16[192,256]{1,0:T(8,128)(2,1)S(1)}, bf16[192,256]{1,0:T(8,128)(2,1)S(1)}, u32[]{:S(2)}, u32[]{:S(2)}) collective-permute-start(bf16[192,256]{1,0:T(8,128)(2,1)S(1)} %get-tuple-element.69), channel_id=1, source_target_pairs={{0,2},{1,3},{2,0},{3,1},{4,6},{5,7},{6,4},{7,5},{8,10},{9,11},{10,... | collective-permute-start | bytes 294920 | tf_op jit(solution)/shard_map/ppermute | solution.py:58
  81.0 6.5 %collective-permute-start.15 = (bf16[192,256]{1,0:T(8,128)(2,1)S(1)}, bf16[192,256]{1,0:T(8,128)(2,1)S(1)}, u32[]{:S(2)}, u32[]{:S(2)}) collective-permute-start(bf16[192,256]{1,0:T(8,128)(2,1)S(1)} %get-tuple-element.70), channel_id=1, source_target_pairs={{0,3},{1,2},{2,1},{3,0},{4,7},{5,6},{6,5},{7,4},{8,11},{9,10},{10,... | collective-permute-start | bytes 294920 | tf_op jit(solution)/shard_map/ppermute | solution.py:58
  82.4 5.0 %collective-permute-start.16 = (f32[48,256]{1,0:T(8,128)S(1)}, f32[48,256]{1,0:T(8,128)S(1)}, u32[]{:S(2)}, u32[]{:S(2)}) collective-permute-start(f32[48,256]{1,0:T(8,128)S(1)} %get-tuple-element.71), channel_id=1, source_target_pairs={{0,28},{4,24},{8,20},{12,16},{16,12},{20,8},{24,4},{28,0},{1,29},{... | collective-permute-start | bytes 147464 | tf_op jit(solution)/shard_map/ppermute | solution.py:54
  87.4 0.6 copy-start.27
  87.5 4.9 %copy-start.10 = (bf16[192,256]{1,0:T(8,128)(2,1)}, bf16[192,256]{1,0:T(8,128)(2,1)S(1)}, u32[]{:S(2)}) copy-start(bf16[192,256]{1,0:T(8,128)(2,1)S(1)} %collective-permute-done.15.g3) | copy-start | bytes 294916
  88.1 9.0 %copy-start.7 = (s32[2]{0:T(128)S(1)}, s32[2]{0:T(128)}, u32[]{:S(2)}) copy-start(s32[2]{0:T(128)} %copy-done.4) | copy-start | bytes 28
  92.3 0.9 copy-start.16
  93.2 20.8 %collective-permute-start.17 = (bf16[2,192,1024]{2,1,0:T(8,128)(2,1)}, bf16[2,192,1024]{2,1,0:T(8,128)(2,1)}, u32[]{:S(2)}, u32[]{:S(2)}) collective-permute-start(bf16[2,192,1024]{2,1,0:T(8,128)(2,1)} %get-tuple-element.81), channel_id=1, source_target_pairs={{0,4},{4,0},{8,12},{12,8},{16,20},{20,16},{24,28},{28,24},{1,5},{5... | collective-permute-start | bytes 2359304 | tf_op jit(solution)/shard_map/ppermute | solution.py:41
  95.2 18.9 %collective-permute-start.20 = (f32[48,256]{1,0:T(8,128)}, f32[48,256]{1,0:T(8,128)S(1)}, u32[]{:S(2)}, u32[]{:S(2)}) collective-permute-start(f32[48,256]{1,0:T(8,128)} %shard_map.155.p0), channel_id=1, source_target_pairs={{0,3},{1,2},{2,1},{3,0},{4,7},{5,6},{6,5},{7,4},{8,11},{9,10},{10,... | collective-permute-start | bytes 147464 | tf_op jit(solution)/shard_map/ppermute | solution.py:58
  95.2 18.9 %collective-permute-start.19 = (f32[48,256]{1,0:T(8,128)}, f32[48,256]{1,0:T(8,128)S(1)}, u32[]{:S(2)}, u32[]{:S(2)}) collective-permute-start(f32[48,256]{1,0:T(8,128)} %shard_map.155.p0), channel_id=1, source_target_pairs={{0,2},{1,3},{2,0},{3,1},{4,6},{5,7},{6,4},{7,5},{8,10},{9,11},{10,... | collective-permute-start | bytes 147464 | tf_op jit(solution)/shard_map/ppermute | solution.py:58
  96.4 17.8 %collective-permute-start.18 = (f32[48,256]{1,0:T(8,128)}, f32[48,256]{1,0:T(8,128)S(1)}, u32[]{:S(2)}, u32[]{:S(2)}) collective-permute-start(f32[48,256]{1,0:T(8,128)} %shard_map.155.p0), channel_id=1, source_target_pairs={{0,1},{1,0},{2,3},{3,2},{4,5},{5,4},{6,7},{7,6},{8,9},{9,8},{10,11... | collective-permute-start | bytes 147464 | tf_op jit(solution)/shard_map/ppermute | solution.py:58
  97.1 0.9 copy-start.11
  98.0 1.1 copy-start.17
  101.5 20.1 %copy-start.12 = (bf16[192,256]{1,0:T(8,128)(2,1)S(1)}, bf16[192,256]{1,0:T(8,128)(2,1)}, u32[]{:S(2)}) copy-start(bf16[192,256]{1,0:T(8,128)(2,1)} %copy-done.10) | copy-start | bytes 294916
  101.5 27.9 %collective-permute-start.21 = (bf16[2,192,1024]{2,1,0:T(8,128)(2,1)S(1)}, bf16[2,192,1024]{2,1,0:T(8,128)(2,1)S(1)}, u32[]{:S(2)}, u32[]{:S(2)}) collective-permute-start(bf16[2,192,1024]{2,1,0:T(8,128)(2,1)S(1)} %get-tuple-element.90), channel_id=1, source_target_pairs={{0,4},{4,0},{8,12},{12,8},{16,20},{20,16},{24,28},{28,24},{1,5},{5... | collective-permute-start | bytes 2359304 | tf_op jit(solution)/shard_map/ppermute | solution.py:41
  114.1 9.1 %copy-start.24 = (f32[48,256]{1,0:T(8,128)}, f32[48,256]{1,0:T(8,128)S(1)}, u32[]{:S(2)}) copy-start(f32[48,256]{1,0:T(8,128)S(1)} %collective-permute-done.20.p3) | copy-start | bytes 147460
  114.1 0.6 copy-start.25
  114.1 0.6 copy-start.26
  114.8 23.6 %collective-permute-start.22 = (bf16[2,192,1024]{2,1,0:T(8,128)(2,1)S(1)}, bf16[2,192,1024]{2,1,0:T(8,128)(2,1)S(1)}, u32[]{:S(2)}, u32[]{:S(2)}) collective-permute-start(bf16[2,192,1024]{2,1,0:T(8,128)(2,1)S(1)} %select_add_fusion), channel_id=1, source_target_pairs={{8,0},{12,4},{16,8},{20,12},{24,16},{28,20},{9,1},{13,5},{17,9},{2... | collective-permute-start | bytes 2359304 | tf_op jit(solution)/shard_map/ppermute | solution.py:37
  123.2 17.5 %copy-start.20 = (f32[4,192,256]{2,1,0:T(8,128)}, f32[4,192,256]{2,1,0:T(8,128)S(1)}, u32[]{:S(2)}) copy-start(f32[4,192,256]{2,1,0:T(8,128)S(1)} %get-tuple-element.92.refs_1_) | copy-start | bytes 2359300
  129.5 11.2 %copy-start.22 = (bf16[2,192,1024]{2,1,0:T(8,128)(2,1)}, bf16[2,192,1024]{2,1,0:T(8,128)(2,1)S(1)}, u32[]{:S(2)}) copy-start(bf16[2,192,1024]{2,1,0:T(8,128)(2,1)S(1)} %collective-permute-done.21) | copy-start | bytes 2359300
  138.4 8.3 %copy-start.8 = (s32[2]{0:T(128)S(1)}, s32[2]{0:T(128)}, u32[]{:S(2)}) copy-start(s32[2]{0:T(128)} %copy-done.4) | copy-start | bytes 28
  138.4 8.3 %copy-start.13 = (bf16[192,256]{1,0:T(8,128)(2,1)S(1)}, bf16[192,256]{1,0:T(8,128)(2,1)}, u32[]{:S(2)}) copy-start(bf16[192,256]{1,0:T(8,128)(2,1)} %copy-done.10) | copy-start | bytes 294916
  140.7 30.2 %collective-permute-start.23 = (bf16[2,192,1024]{2,1,0:T(8,128)(2,1)}, bf16[2,192,1024]{2,1,0:T(8,128)(2,1)}, u32[]{:S(2)}, u32[]{:S(2)}) collective-permute-start(bf16[2,192,1024]{2,1,0:T(8,128)(2,1)} %add_add_fusion), channel_id=1, source_target_pairs={{8,0},{12,4},{16,8},{20,12},{24,16},{28,20},{9,1},{13,5},{17,9},{2... | collective-permute-start | bytes 2359304 | tf_op jit(solution)/shard_map/ppermute | solution.py:37
  146.6 1.1 copy-start.21
  147.8 23.1 %copy-start.23 = (bf16[2,192,1024]{2,1,0:T(8,128)(2,1)S(1)}, bf16[2,192,1024]{2,1,0:T(8,128)(2,1)}, u32[]{:S(2)}) copy-start(bf16[2,192,1024]{2,1,0:T(8,128)(2,1)} %copy-done.22) | copy-start | bytes 2359300

commit v2 on v1

--- a/solution.py
+++ b/solution.py
@@ -251,7 +251,7 @@
                 lse_ref[b, h] = top + jnp.log(total)
 
 
-def forward(tables, queries, regions, slabs, state=None, closing=False, pairs=16):
+def forward(tables, queries, regions, slabs, state=None, closing=False, pairs=1):
     width, tokens = queries.shape
     heads, blocks = width // HEAD_DIM, tokens // BLOCK
     slots = len(regions) * blocks
@@ -446,26 +446,27 @@
     place = jnp.stack([row, col]).astype(jnp.int32)
 
     tables = (block_lists, counts, place)
+    tie = lax.optimization_barrier
     own = jnp.stack([key_rows, values])
     slab2 = hop(own, 2)
-    state = forward(tables, queries, [(0, 0, "both")], [own], pairs=1)
-    *state, slab2, out_proj = lax.optimization_barrier([*state, slab2, out_proj])
-    up1 = upward(own)
-    slab4 = hop(slab2, 2)
-    up2 = upward(slab2)
-    down1 = downward(slab2)
-
+    state = forward(tables, queries, [(0, 0, "both")], [own])
+    *state, out_proj, cotangent, own_again = tie([*state, out_proj, cotangent, own])
     order = token_order.reshape(1, tokens)
     grad_latent = mirror(permuted(scatter_kernel, place, order, cotangent.T))
-    weights = [out_proj] + [across(out_proj, k) for k in range(1, cols)]
-
-    state = forward(tables, queries, [(2, 2, "both")], [slab2], tuple(state), pairs=1)
-    *state, slab4 = lax.optimization_barrier([*state, slab4])
+    weights = [across(out_proj, k) for k in range(1, cols)]
+    up1 = upward(own_again)
+    *state, slab2, grad_latent, out_proj, w1, w2, w3 = tie(
+        [*state, slab2, grad_latent, out_proj, *weights])
+    weights = [out_proj, w1, w2, w3]
+    slab4 = hop(slab2, 2)
+    down1 = downward(slab2)
+    up2 = upward(slab2)
+    state = forward(tables, queries, [(2, 2, "both")], [slab2], tuple(state))
+    *state, slab4 = tie([*state, slab4])
     down2 = downward(slab4)
-    state = forward(tables, queries, [(1, 1, "each")], [down1, up1], tuple(state), pairs=1)
-    state = forward(tables, queries, [(4, 4, "both"), (-1, 3, "one")], [slab4, up2], state,
-                    pairs=1)
-    attended, lse = forward(tables, queries, [(3, -1, "one")], [down2], state, True, pairs=1)
+    state = forward(tables, queries, [(1, 1, "each")], [down1, up1], tuple(state))
+    state = forward(tables, queries, [(4, 4, "both"), (-1, 3, "one")], [slab4, up2], state)
+    attended, lse = forward(tables, queries, [(3, -1, "one")], [down2], state, True)
 
     def block_of(array, b):
         return lax.dynamic_slice_in_dim(array, b * BLOCK, BLOCK, 1)
@@ -475,30 +476,29 @@
     latent, *grads = flow(
         place, parts, weights, stream, norm_gain.reshape(1, -1), head_proj, patches.T,
         grad_latent)
-    *grads, mirrored = lax.optimization_barrier(
-        [grads[0]] + [across(grads[k], k) for k in range(1, cols)] + [mirror(latent)])
+    grads = [grads[0]] + [across(grads[k], k) for k in range(1, cols)]
 
     shared = (tables, queries, attended, lse, grads)
-    grad_queries, part3, part4 = backward(
-        *shared, [(3, 3, "each"), (4, 4, "both")], [down2, up2, slab4], pairs=1)
+    grad_queries, part3 = backward(*shared, [(3, 3, "each")], [down2, up2])
     from3 = mate(part3)
-    reordered = permuted(gather_kernel, place, order, mirrored)
-    grad_queries, reordered = lax.optimization_barrier((grad_queries, reordered))
-    pieces = [reordered] + [across(reordered, k) for k in range(1, cols)]
-    grad_queries, part1 = backward(
-        *shared, [(1, 1, "each")], [down1, up1], grad_queries, pairs=1)
+    grad_queries, part4, part1 = backward(
+        *shared, [(4, 4, "both"), (1, 1, "each")], [slab4, down1, up1], grad_queries)
     from1 = mate(part1)
     zero = jnp.zeros_like(part1)
     far = part4 + jnp.where(odd, from3, zero)
-    grad_queries, far, *pieces = lax.optimization_barrier([grad_queries, far] + pieces)
+    grad_queries, far, latent = tie([grad_queries, far, latent])
     far = hop(far, -2)
+    mirrored = mirror(latent)
+    grad_queries, part2 = backward(*shared, [(2, 2, "both")], [slab2], grad_queries)
+    grad_queries, mirrored = tie([grad_queries, mirrored])
+    reordered = permuted(gather_kernel, place, order, mirrored)
+    near = part2 + jnp.where(odd, from1, from3) + far
+    grad_queries, near, reordered = tie([grad_queries, near, reordered])
+    near = hop(near, -2)
+    pieces = [reordered] + [across(reordered, k) for k in range(1, cols)]
+    grad_queries, own_grad = backward(*shared, [(0, 0, "both")], [own], grad_queries, True)
+    own_grad, *pieces = tie([own_grad] + pieces)
     latent_out = assembled(place, pieces, tokens).T
-    grad_queries, part2 = backward(*shared, [(2, 2, "both")], [slab2], grad_queries, pairs=1)
-    near = part2 + jnp.where(odd, from1, from3) + far
-    grad_queries, near = lax.optimization_barrier((grad_queries, near))
-    near = hop(near, -2)
-    grad_queries, own_grad = backward(
-        *shared, [(0, 0, "both")], [own], grad_queries, True, pairs=1)
     own_grad = own_grad + jnp.where(odd, zero, from1).astype(F32) + near.astype(F32)
     own_grad = own_grad.astype(BF16)
     return (latent_out, grad_queries, own_grad[0], own_grad[1])

time: 177 us -> 192 us (1.085)
  the two profiles are of different devices: /device:TPU:8 before, /device:TPU:0 now
where the time goes in v2:
time: 192 us; the launch traced here: 191 us
  starting transfers between devices  65.9 us (34%)
  waiting for transfers between devices  58.4 us (30%)
  Pallas kernels  37.2 us (19%)
  local copies, waits for them, and re-layouts  21.4 us (11%)
  other arithmetic  6.66 us (3%)
    ppermute x2, starting transfers between devices, mirror(): return lax.ppermute(array, 'row', [(i, size - 1 - i) for i in range(size)])  25.3 us
    unnamed x120, local copies, waits for them, and re-layouts  20.4 us
    ppermute x2, waiting for transfers between devices, mirror(): return lax.ppermute(array, 'row', [(i, size - 1 - i) for i in range(size)])  19.6 us
    pallas_call x4, Pallas kernels, backward(): pl.pallas_call(functools.partial(backward_kernel, regions, diagonal, last...  17.5 us
    ppermute x12, waiting for transfers between devices, across(): lax.ppermute(array, 'col', [(i, i ^ bits) for i in range(lax.axis_size('c...  12.9 us
    pallas_call x5, Pallas kernels, forward(): pl.pallas_call(functools.partial(forward_kernel, regions, not state, clos...  12.2 us
    ppermute x2, starting transfers between devices, mate(): lax.ppermute(array, 'row', [(i, i ^ 1) for i in range(lax.axis_size('row'...  11.6 us
    ppermute x2, waiting for transfers between devices, upward(): lax.ppermute(array, 'row', [(i, i + 1) for i in range(0, lax.axis_size('r...  10.9 us
  transfers between devices with their start and end apart: 24, of which 13 were waited for; matrix products, arithmetic and copies ran while one was open for 1% of the time, Pallas kernels for 15%

profile of v2, /device:TPU:0, one launch (start us, length us, event | category | flops | bytes accessed | tf_op | source)
XLA Modules:
  0.0 190.8 jit_solution(8334898950817902354)
XLA Ops:
  0.7 1.2 pad_maximum_fusion.refs_0_
  1.9 5.8 %collective-permute-start = (bf16[2,192,1024]{2,1,0:T(8,128)(2,1)S(1)}, bf16[2,192,1024]{2,1,0:T(8,128)(2,1)}, u32[]{:S(2)}, u32[]{:S(2)}) collective-permute-start(bf16[2,192,1024]{2,1,0:T(8,128)(2,1)S(1)} %pad_maximum_fusion.refs_0_), channel_id=1, source_target_pairs={{0,8},{4,12},{8,16},{12,20},{16,24},{20,28},{1,9},{5,13},{9,17},{1... | collective-permute-start | bytes 2359304 | tf_op jit(solution)/shard_map/ppermute | solution.py:37
  7.8 5.5 %shard_map.147 = (f32[4,192,256]{2,1,0:T(8,128)S(1)}, f32[4,6,1,256]{3,2,1,0:T(1,128)S(1)}) custom-call(s32[4,16]{1,0:T(4,128)S(1)} %copy-done.34, s32[4]{0:T(128)S(1)} %copy-done.38, s32[2]{0:T(128)S(1)} %pad_add_fusion.place_ref, bf16[192,1024]{1,0:T(8,128)(2,1)S(1)} %copy-done.2, bf16[2,192,1024]{2,1,0:T(8,128)(2,1)S(1)} %pad_maximum_fusion.refs_0_), custom_call_target="tpu_custom_call" | custom-call | flops 1000000000 | bytes 6291456 | tf_op jit(solution)/shard_map/pallas_call | solution.py:262
  13.4 0.9 copy-done.48
  15.5 0.9 collective-permute-start.3
  16.7 1.8 shard_map.148
  18.6 2.0 %collective-permute-start.1 = (f32[48,256]{1,0:T(8,128)}, f32[48,256]{1,0:T(8,128)S(1)}, u32[]{:S(2)}, u32[]{:S(2)}) collective-permute-start(f32[48,256]{1,0:T(8,128)} %shard_map.148), channel_id=1, source_target_pairs={{0,28},{4,24},{8,20},{12,16},{16,12},{20,8},{24,4},{28,0},{1,29},{... | collective-permute-start | bytes 147464 | tf_op jit(solution)/shard_map/ppermute | solution.py:54
  20.6 5.0 %collective-permute-done.1.grad_ref = f32[48,256]{1,0:T(8,128)S(1)} collective-permute-done((f32[48,256]{1,0:T(8,128)}, f32[48,256]{1,0:T(8,128)S(1)}, u32[]{:S(2)}, u32[]{:S(2)}) %collective-permute-start.1) | collective-permute-done | bytes 49184 | tf_op jit(solution)/shard_map/ppermute | solution.py:54
  26.2 0.7 copy-done.8
  26.9 3.6 %collective-permute-done.3.w2 = bf16[192,768]{1,0:T(8,128)(2,1)S(1)} collective-permute-done((bf16[192,768]{1,0:T(8,128)(2,1)S(1)}, bf16[192,768]{1,0:T(8,128)(2,1)S(1)}, u32[]{:S(2)}, u32[]{:S(2)}) %collective-permute-start.3) | collective-permute-done | bytes 294944 | tf_op jit(solution)/shard_map/ppermute | solution.py:58
  30.5 0.7 copy-done.10
  31.2 0.7 copy-done.12
  31.9 1.4 collective-permute-start.5
  33.4 3.5 %collective-permute-start.9 = (bf16[2,192,1024]{2,1,0:T(8,128)(2,1)S(1)}, bf16[2,192,1024]{2,1,0:T(8,128)(2,1)S(1)}, u32[]{:S(2)}, u32[]{:S(2)}) collective-permute-start(bf16[2,192,1024]{2,1,0:T(8,128)(2,1)S(1)} %pad_maximum_fusion.refs_0_), channel_id=1, source_target_pairs={{0,4},{8,12},{16,20},{24,28},{1,5},{9,13},{17,21},{25,29},{2,6},{1... | collective-permute-start | bytes 2359304 | tf_op jit(solution)/shard_map/ppermute | solution.py:45
  36.9 1.3 collective-permute-start.8
  38.2 5.5 %collective-permute-start.7 = (bf16[2,192,1024]{2,1,0:T(8,128)(2,1)}, bf16[2,192,1024]{2,1,0:T(8,128)(2,1)}, u32[]{:S(2)}, u32[]{:S(2)}) collective-permute-start(bf16[2,192,1024]{2,1,0:T(8,128)(2,1)} %collective-permute-done.refs_0_), channel_id=1, source_target_pairs={{0,4},{8,12},{16,20},{24,28},{1,5},{9,13},{17,21},{25,29},{2,6},{1... | collective-permute-start | bytes 2359304 | tf_op jit(solution)/shard_map/ppermute | solution.py:45
  44.4 1.1 copy-done.49
  45.5 0.7 copy-done.53
  46.2 1.7 shard_map.149
  48.0 0.9 copy-done.44
  49.5 1.4 collective-permute-done.5.refs_0_
  50.9 1.3 collective-permute-start.6
  52.2 2.6 %collective-permute-done.9.refs_1_.refs_2_ = bf16[2,192,1024]{2,1,0:T(8,128)(2,1)S(1)} collective-permute-done((bf16[2,192,1024]{2,1,0:T(8,128)(2,1)S(1)}, bf16[2,192,1024]{2,1,0:T(8,128)(2,1)S(1)}, u32[]{:S(2)}, u32[]{:S(2)}) %collective-permute-start.9) | collective-permute-done | bytes 786464 | tf_op jit(solution)/shard_map/ppermute | solution.py:45
  54.8 4.7 %collective-permute-done.8.refs_0_.refs_1_ = bf16[2,192,1024]{2,1,0:T(8,128)(2,1)S(1)} collective-permute-done((bf16[2,192,1024]{2,1,0:T(8,128)(2,1)}, bf16[2,192,1024]{2,1,0:T(8,128)(2,1)S(1)}, u32[]{:S(2)}, u32[]{:S(2)}) %collective-permute-start.8) | collective-permute-done | bytes 786464 | tf_op jit(solution)/shard_map/ppermute | solution.py:49
  59.5 1.1 copy-done.45
  60.6 0.7 copy-done.51
  61.4 1.2 shard_map.150
  62.5 8.3 %collective-permute-done.7.refs_1_ = bf16[2,192,1024]{2,1,0:T(8,128)(2,1)} collective-permute-done((bf16[2,192,1024]{2,1,0:T(8,128)(2,1)}, bf16[2,192,1024]{2,1,0:T(8,128)(2,1)}, u32[]{:S(2)}, u32[]{:S(2)}) %collective-permute-start.7) | collective-permute-done | bytes 786464 | tf_op jit(solution)/shard_map/ppermute | solution.py:45
  70.8 1.8 shard_map.151
  72.7 2.5 %collective-permute-done.6.refs_0_ = bf16[2,192,1024]{2,1,0:T(8,128)(2,1)} collective-permute-done((bf16[2,192,1024]{2,1,0:T(8,128)(2,1)S(1)}, bf16[2,192,1024]{2,1,0:T(8,128)(2,1)}, u32[]{:S(2)}, u32[]{:S(2)}) %collective-permute-start.6) | collective-permute-done | bytes 786464 | tf_op jit(solution)/shard_map/ppermute | solution.py:49
  75.3 2.0 %shard_map.152 = (bf16[192,1024]{1,0:T(8,128)(2,1)S(1)}, f32[4,3,1,256]{3,2,1,0:T(1,128)S(1)}) custom-call(s32[4,16]{1,0:T(4,128)S(1)} %copy-done.35, s32[4]{0:T(128)S(1)} %copy-done.39, s32[2]{0:T(128)S(1)} %copy-done.32, bf16[192,1024]{1,0:T(8,128)(2,1)S(1)} %copy-done.3, bf16[2,192,1024]{2,1,0:T(8,128)(2,1)} %collective-permute-done.6.refs_0_, ...), custom_call_target="tpu_custom_call" | custom-call | flops 1000000000 | bytes 6291456 | tf_op jit(solution)/shard_map/pallas_call | solution.py:262
  77.5 1.1 collective-permute-start.11
  78.5 0.8 collective-permute-start.10
  79.3 3.1 %collective-permute-done.12.a3 = bf16[192,256]{1,0:T(8,128)(2,1)S(1)} collective-permute-done((bf16[192,256]{1,0:T(8,128)(2,1)S(1)}, bf16[192,256]{1,0:T(8,128)(2,1)S(1)}, u32[]{:S(2)}, u32[]{:S(2)}) %collective-permute-start.12) | collective-permute-done | bytes 98336 | tf_op jit(solution)/shard_map/ppermute | solution.py:58
  82.5 1.3 collective-permute-done.11.a2
  83.9 2.4 %shard_map.153 = (f32[48,256]{1,0:T(8,128)S(1)}, bf16[192,256]{1,0:T(8,128)(2,1)S(1)}, bf16[192,256]{1,0:T(8,128)(2,1)S(1)}, bf16[192,256]{1,0:T(8,128)(2,1)S(1)}, bf16[192,256]{1,0:T(8,128)(2,1)S(1)}) custom-call(s32[2]{0:T(128)S(1)} %copy-done.32, bf16[192,256]{1,0:T(8,128)(2,1)S(1)} %get-tuple-element.115.a0, ...), custom_call_target="tpu_custom_call" | custom-call | tf_op jit(solution)/shard_map/pallas_call | solution.py:313
  87.2 1.1 collective-permute-start.14
  88.8 4.0 %collective-permute-done.14.g2 = bf16[192,256]{1,0:T(8,128)(2,1)S(1)} collective-permute-done((bf16[192,256]{1,0:T(8,128)(2,1)S(1)}, bf16[192,256]{1,0:T(8,128)(2,1)S(1)}, u32[]{:S(2)}, u32[]{:S(2)}) %collective-permute-start.14) | collective-permute-done | bytes 98336 | tf_op jit(solution)/shard_map/ppermute | solution.py:58
  92.8 0.9 collective-permute-done.15.g3
  93.6 3.5 %shard_map.154 = (f32[4,192,256]{2,1,0:T(8,128)S(1)}, bf16[2,192,1024]{2,1,0:T(8,128)(2,1)}) custom-call(s32[4,16]{1,0:T(4,128)S(1)} %copy-done.35, s32[4]{0:T(128)S(1)} %copy-done.39, s32[2]{0:T(128)S(1)} %copy-done.32, bf16[192,1024]{1,0:T(8,128)(2,1)S(1)} %copy-done.3, bf16[192,1024]{1,0:T(8,128)(2,1)S(1)} %get-tuple-element.76.att_ref, ...), custom_call_target="tpu_custom_call" | custom-call | flops 1000000000 | bytes 8388608 | tf_op jit(solution)/shard_map/pallas_call | solution.py:415
  97.2 0.9 copy-done.1
  98.6 1.0 copy-done.4
  99.6 0.9 copy-done.17
  100.5 0.9 copy-done.20
  101.4 0.9 copy-done.23
  102.3 0.9 copy-done.26
  103.2 0.7 copy-done.36
  104.5 3.7 %shard_map.155 = (f32[4,192,256]{2,1,0:T(8,128)S(1)}, bf16[2,192,1024]{2,1,0:T(8,128)(2,1)S(1)}, bf16[2,192,1024]{2,1,0:T(8,128)(2,1)}) custom-call(s32[4,16]{1,0:T(4,128)S(1)} %copy-done.36, s32[4]{0:T(128)S(1)} %copy-done.40, s32[2]{0:T(128)S(1)} %copy-done.32, bf16[192,1024]{1,0:T(8,128)(2,1)S(1)} %copy-done.4, ...), custom_call_target="tpu_custom_call" | custom-call | flops 1000000000 | bytes 8388608 | tf_op jit(solution)/shard_map/pallas_call | solution.py:415
  108.2 11.1 %collective-permute-start.18 = (bf16[2,192,1024]{2,1,0:T(8,128)(2,1)}, bf16[2,192,1024]{2,1,0:T(8,128)(2,1)}, u32[]{:S(2)}, u32[]{:S(2)}) collective-permute-start(bf16[2,192,1024]{2,1,0:T(8,128)(2,1)} %get-tuple-element.97), channel_id=1, source_target_pairs={{0,4},{4,0},{8,12},{12,8},{16,20},{20,16},{24,28},{28,24},{1,5},{5... | collective-permute-start | bytes 2359304 | tf_op jit(solution)/shard_map/ppermute | solution.py:41
  119.3 1.0 select_add_fusion
  120.3 1.3 collective-permute-start.19
  121.6 23.3 %collective-permute-start.17 = (f32[48,256]{1,0:T(8,128)S(1)}, f32[48,256]{1,0:T(8,128)S(1)}, u32[]{:S(2)}, u32[]{:S(2)}) collective-permute-start(f32[48,256]{1,0:T(8,128)S(1)} %copy-done.43), channel_id=1, source_target_pairs={{0,28},{4,24},{8,20},{12,16},{16,12},{20,8},{24,4},{28,0},{1,29},{... | collective-permute-start | bytes 147464 | tf_op jit(solution)/shard_map/ppermute | solution.py:54
  144.9 2.2 %shard_map.156 = (f32[4,192,256]{2,1,0:T(8,128)S(1)}, bf16[2,192,1024]{2,1,0:T(8,128)(2,1)S(1)}) custom-call(s32[4,16]{1,0:T(4,128)S(1)} %copy-done.36, s32[4]{0:T(128)S(1)} %copy-done.40, s32[2]{0:T(128)S(1)} %copy-done.32, bf16[192,1024]{1,0:T(8,128)(2,1)S(1)} %copy-done.4, bf16[192,1024]{1,0:T(8,128)(2,1)S(1)} %get-tuple-element.76.att_ref, ...), custom_call_target="tpu_custom_call" | custom-call | flops 1000000000 | bytes 8388608 | tf_op jit(solution)/shard_map/pallas_call | solution.py:415
  147.1 0.9 copy-done.46
  148.0 14.6 %collective-permute-done.17.x_ref = f32[48,256]{1,0:T(8,128)S(1)} collective-permute-done((f32[48,256]{1,0:T(8,128)S(1)}, f32[48,256]{1,0:T(8,128)S(1)}, u32[]{:S(2)}, u32[]{:S(2)}) %collective-permute-start.17) | collective-permute-done | bytes 49184 | tf_op jit(solution)/shard_map/ppermute | solution.py:54
  163.3 1.7 shard_map.157.p0
  165.0 2.6 %add_add_fusion = bf16[2,192,1024]{2,1,0:T(8,128)(2,1)} fusion(bf16[2,192,1024]{2,1,0:T(8,128)(2,1)} %collective-permute-done.19, bf16[2,192,1024]{2,1,0:T(8,128)(2,1)S(1)} %get-tuple-element.96, bf16[2,192,1024]{2,1,0:T(8,128)(2,1)} %collective-permute-done.18, bf16[2,192,1024]{2,1,0:T(8,128)(2,1)} %collective-permute-done.16, pred[]{:T(512)S(6)} %eq.5), kind=kLoop, calls=%fused_computation.2 | loop fusion | flops 1179648 | bytes 3932161 | tf_op jit(solution)/shard_map/add | solution.py:495
  167.6 1.3 collective-permute-start.23
  169.5 1.3 collective-permute-start.20
  170.8 8.1 %shard_map.158 = (bf16[192,1024]{1,0:T(8,128)(2,1)}, f32[2,192,1024]{2,1,0:T(8,128)S(1)}) custom-call(s32[4,16]{1,0:T(4,128)S(1)} %copy-done.37, s32[4]{0:T(128)S(1)} %copy-done.41, s32[2]{0:T(128)S(1)} %copy-done.33, bf16[192,1024]{1,0:T(8,128)(2,1)S(1)} %copy-done.5, bf16[192,1024]{1,0:T(8,128)(2,1)S(1)} %get-tuple-element.76.att_ref, ...), custom_call_target="tpu_custom_call" | custom-call | flops 1000000000 | bytes 8388608 | tf_op jit(solution)/shard_map/pallas_call | solution.py:415
  180.2 1.6 shard_map.159
  181.8 6.3 %collective-permute-done.23 = bf16[2,192,1024]{2,1,0:T(8,128)(2,1)} collective-permute-done((bf16[2,192,1024]{2,1,0:T(8,128)(2,1)}, bf16[2,192,1024]{2,1,0:T(8,128)(2,1)}, u32[]{:S(2)}, u32[]{:S(2)}) %collective-permute-start.23) | collective-permute-done | bytes 786464 | tf_op jit(solution)/shard_map/ppermute | solution.py:37
  188.1 1.8 add_convert_fusion
  189.8 0.9 slice_bitcast_fusion
  (125 shorter events, 9.0 us)
Async XLA Ops:
  0.6 7.2 %copy-start.38 = (s32[4]{0:T(128)S(1)}, s32[4]{0:T(128)}, u32[]{:S(2)}) copy-start(s32[4]{0:T(128)} %counts_ref.17) | copy-start | bytes 52
  0.6 7.2 %copy-start.34 = (s32[4,16]{1,0:T(4,128)S(1)}, s32[4,16]{1,0:T(4,128)}, u32[]{:S(2)}) copy-start(s32[4,16]{1,0:T(4,128)} %lists_ref.17) | copy-start | bytes 772
  0.7 7.2 %copy-start.2 = (bf16[192,1024]{1,0:T(8,128)(2,1)S(1)}, bf16[192,1024]{1,0:T(8,128)(2,1)}, u32[]{:S(2)}) copy-start(bf16[192,1024]{1,0:T(8,128)(2,1)} %q_ref.17) | copy-start | bytes 1179652
  1.9 30.0 %collective-permute-start = (bf16[2,192,1024]{2,1,0:T(8,128)(2,1)S(1)}, bf16[2,192,1024]{2,1,0:T(8,128)(2,1)}, u32[]{:S(2)}, u32[]{:S(2)}) collective-permute-start(bf16[2,192,1024]{2,1,0:T(8,128)(2,1)S(1)} %pad_maximum_fusion.refs_0_), channel_id=1, source_target_pairs={{0,8},{4,12},{8,16},{12,20},{16,24},{20,28},{1,9},{5,13},{9,17},{1... | collective-permute-start | bytes 2359304 | tf_op jit(solution)/shard_map/ppermute | solution.py:37
  7.8 5.6 %copy-start.30 = (s32[2]{0:T(128)}, s32[2]{0:T(128)S(1)}, u32[]{:S(2)}) copy-start(s32[2]{0:T(128)S(1)} %pad_add_fusion.place_ref) | copy-start | bytes 28
  7.8 7.1 %copy-start.6 = (bf16[192,768]{1,0:T(8,128)(2,1)S(1)}, bf16[192,768]{1,0:T(8,128)(2,1)}, u32[]{:S(2)}) copy-start(bf16[192,768]{1,0:T(8,128)(2,1)} %w0) | copy-start | bytes 884740
  14.9 11.3 %collective-permute-start.4 = (bf16[192,768]{1,0:T(8,128)(2,1)S(1)}, bf16[192,768]{1,0:T(8,128)(2,1)S(1)}, u32[]{:S(2)}, u32[]{:S(2)}) collective-permute-start(bf16[192,768]{1,0:T(8,128)(2,1)S(1)} %copy-done.6), channel_id=1, source_target_pairs={{0,3},{1,2},{2,1},{3,0},{4,7},{5,6},{6,5},{7,4},{8,11},{9,10},{10,... | collective-permute-start | bytes 884744 | tf_op jit(solution)/shard_map/ppermute | solution.py:58
  15.5 15.0 %collective-permute-start.3 = (bf16[192,768]{1,0:T(8,128)(2,1)S(1)}, bf16[192,768]{1,0:T(8,128)(2,1)S(1)}, u32[]{:S(2)}, u32[]{:S(2)}) collective-permute-start(bf16[192,768]{1,0:T(8,128)(2,1)S(1)} %copy-done.6), channel_id=1, source_target_pairs={{0,2},{1,3},{2,0},{3,1},{4,6},{5,7},{6,4},{7,5},{8,10},{9,11},{10,... | collective-permute-start | bytes 884744 | tf_op jit(solution)/shard_map/ppermute | solution.py:58
  16.4 14.8 %collective-permute-start.2 = (bf16[192,768]{1,0:T(8,128)(2,1)S(1)}, bf16[192,768]{1,0:T(8,128)(2,1)S(1)}, u32[]{:S(2)}, u32[]{:S(2)}) collective-permute-start(bf16[192,768]{1,0:T(8,128)(2,1)S(1)} %copy-done.6), channel_id=1, source_target_pairs={{0,1},{1,0},{2,3},{3,2},{4,5},{5,4},{6,7},{7,6},{8,9},{9,8},{10,11... | collective-permute-start | bytes 884744 | tf_op jit(solution)/shard_map/ppermute | solution.py:58
  16.7 42.7 %copy-start.32 = (s32[2]{0:T(128)S(1)}, s32[2]{0:T(128)}, u32[]{:S(2)}) copy-start(s32[2]{0:T(128)} %copy-done.30) | copy-start | bytes 28
  18.6 7.0 %collective-permute-start.1 = (f32[48,256]{1,0:T(8,128)}, f32[48,256]{1,0:T(8,128)S(1)}, u32[]{:S(2)}, u32[]{:S(2)}) collective-permute-start(f32[48,256]{1,0:T(8,128)} %shard_map.148), channel_id=1, source_target_pairs={{0,28},{4,24},{8,20},{12,16},{16,12},{20,8},{24,4},{28,0},{1,29},{... | collective-permute-start | bytes 147464 | tf_op jit(solution)/shard_map/ppermute | solution.py:54
  31.9 18.9 %collective-permute-start.5 = (bf16[2,192,1024]{2,1,0:T(8,128)(2,1)}, bf16[2,192,1024]{2,1,0:T(8,128)(2,1)S(1)}, u32[]{:S(2)}, u32[]{:S(2)}) collective-permute-start(bf16[2,192,1024]{2,1,0:T(8,128)(2,1)} %collective-permute-done.refs_0_), channel_id=1, source_target_pairs={{0,8},{4,12},{8,16},{12,20},{16,24},{20,28},{1,9},{5,13},{9,17},{1... | collective-permute-start | bytes 2359304 | tf_op jit(solution)/shard_map/ppermute | solution.py:37
  33.4 21.4 %collective-permute-start.9 = (bf16[2,192,1024]{2,1,0:T(8,128)(2,1)S(1)}, bf16[2,192,1024]{2,1,0:T(8,128)(2,1)S(1)}, u32[]{:S(2)}, u32[]{:S(2)}) collective-permute-start(bf16[2,192,1024]{2,1,0:T(8,128)(2,1)S(1)} %pad_maximum_fusion.refs_0_), channel_id=1, source_target_pairs={{0,4},{8,12},{16,20},{24,28},{1,5},{9,13},{17,21},{25,29},{2,6},{1... | collective-permute-start | bytes 2359304 | tf_op jit(solution)/shard_map/ppermute | solution.py:45
  36.9 22.5 %collective-permute-start.8 = (bf16[2,192,1024]{2,1,0:T(8,128)(2,1)}, bf16[2,192,1024]{2,1,0:T(8,128)(2,1)S(1)}, u32[]{:S(2)}, u32[]{:S(2)}) collective-permute-start(bf16[2,192,1024]{2,1,0:T(8,128)(2,1)} %collective-permute-done.refs_0_), channel_id=1, source_target_pairs={{4,0},{12,8},{20,16},{28,24},{5,1},{13,9},{21,17},{29,25},{6,2},{1... | collective-permute-start | bytes 2359304 | tf_op jit(solution)/shard_map/ppermute | solution.py:49
  38.2 32.6 %collective-permute-start.7 = (bf16[2,192,1024]{2,1,0:T(8,128)(2,1)}, bf16[2,192,1024]{2,1,0:T(8,128)(2,1)}, u32[]{:S(2)}, u32[]{:S(2)}) collective-permute-start(bf16[2,192,1024]{2,1,0:T(8,128)(2,1)} %collective-permute-done.refs_0_), channel_id=1, source_target_pairs={{0,4},{8,12},{16,20},{24,28},{1,5},{9,13},{17,21},{25,29},{2,6},{1... | collective-permute-start | bytes 2359304 | tf_op jit(solution)/shard_map/ppermute | solution.py:45
  44.4 1.1 copy-start.49
  50.9 24.3 %collective-permute-start.6 = (bf16[2,192,1024]{2,1,0:T(8,128)(2,1)S(1)}, bf16[2,192,1024]{2,1,0:T(8,128)(2,1)}, u32[]{:S(2)}, u32[]{:S(2)}) collective-permute-start(bf16[2,192,1024]{2,1,0:T(8,128)(2,1)S(1)} %collective-permute-done.5.refs_0_), channel_id=1, source_target_pairs={{4,0},{12,8},{20,16},{28,24},{5,1},{13,9},{21,17},{29,25},{6,2},{1... | collective-permute-start | bytes 2359304 | tf_op jit(solution)/shard_map/ppermute | solution.py:49
  59.5 1.1 copy-start.45
  70.8 4.4 %copy-start.3 = (bf16[192,1024]{1,0:T(8,128)(2,1)S(1)}, bf16[192,1024]{1,0:T(8,128)(2,1)}, u32[]{:S(2)}) copy-start(bf16[192,1024]{1,0:T(8,128)(2,1)} %q_ref.17) | copy-start | bytes 1179652
  70.8 4.4 %copy-start.35 = (s32[4,16]{1,0:T(4,128)S(1)}, s32[4,16]{1,0:T(4,128)}, u32[]{:S(2)}) copy-start(s32[4,16]{1,0:T(4,128)} %lists_ref.17) | copy-start | bytes 772
  70.8 4.4 %copy-start.39 = (s32[4]{0:T(128)S(1)}, s32[4]{0:T(128)}, u32[]{:S(2)}) copy-start(s32[4]{0:T(128)} %counts_ref.17) | copy-start | bytes 52
  75.2 4.1 %copy-start.59 = (f32[768]{0:T(1024)S(1)}, f32[768]{0:T(1024)}, u32[]{:S(2)}) copy-start(f32[768]{0:T(1024)} %param.19) | copy-start | bytes 9220
  75.2 8.6 %copy-start = (bf16[1024,768]{1,0:T(8,128)(2,1)S(1)}, bf16[1024,768]{1,0:T(8,128)(2,1)}, u32[]{:S(2)}) copy-start(bf16[1024,768]{1,0:T(8,128)(2,1)} %stream_ref.1) | copy-start | bytes 4718596
  75.2 8.6 %copy-start.7 = (bf16[192,768]{1,0:T(8,128)(2,1)S(1)}, bf16[192,768]{1,0:T(8,128)(2,1)}, u32[]{:S(2)}) copy-start(bf16[192,768]{1,0:T(8,128)(2,1)} %w0) | copy-start | bytes 884740
  75.3 8.6 %copy-start.9 = (bf16[192,768]{1,0:T(8,128)(2,1)S(1)}, bf16[192,768]{1,0:T(8,128)(2,1)}, u32[]{:S(2)}) copy-start(bf16[192,768]{1,0:T(8,128)(2,1)} %copy-done.8) | copy-start | bytes 884740
  75.3 8.6 %copy-start.11 = (bf16[192,768]{1,0:T(8,128)(2,1)S(1)}, bf16[192,768]{1,0:T(8,128)(2,1)}, u32[]{:S(2)}) copy-start(bf16[192,768]{1,0:T(8,128)(2,1)} %copy-done.10) | copy-start | bytes 884740
  75.3 8.6 %copy-start.13 = (bf16[192,768]{1,0:T(8,128)(2,1)S(1)}, bf16[192,768]{1,0:T(8,128)(2,1)}, u32[]{:S(2)}) copy-start(bf16[192,768]{1,0:T(8,128)(2,1)} %copy-done.12) | copy-start | bytes 884740
  75.3 8.6 %copy-start.14 = (f32[1024,48]{0,1:T(8,128)S(1)}, f32[1024,48]{0,1:T(8,128)}, u32[]{:S(2)}) copy-start(f32[1024,48]{0,1:T(8,128)} %param.21) | copy-start | bytes 589828
  75.3 8.6 %copy-start.15 = (bf16[96,768]{1,0:T(8,128)(2,1)S(1)}, bf16[96,768]{1,0:T(8,128)(2,1)}, u32[]{:S(2)}) copy-start(bf16[96,768]{1,0:T(8,128)(2,1)} %head_ref.1) | copy-start | bytes 442372
  75.3 8.5 %copy-start.29 = (f32[48,256]{1,0:T(8,128)S(1)}, f32[48,256]{1,0:T(8,128)}, u32[]{:S(2)}) copy-start(f32[48,256]{1,0:T(8,128)} %copy-done.28) | copy-start | bytes 147460
  77.4 5.1 %collective-permute-start.12 = (bf16[192,256]{1,0:T(8,128)(2,1)S(1)}, bf16[192,256]{1,0:T(8,128)(2,1)S(1)}, u32[]{:S(2)}, u32[]{:S(2)}) collective-permute-start(bf16[192,256]{1,0:T(8,128)(2,1)S(1)} %get-tuple-element.112), channel_id=1, source_target_pairs={{0,3},{1,2},{2,1},{3,0},{4,7},{5,6},{6,5},{7,4},{8,11},{9,10},{10,... | collective-permute-start | bytes 294920 | tf_op jit(solution)/shard_map/ppermute | solution.py:58
  77.5 6.3 %collective-permute-start.11 = (bf16[192,256]{1,0:T(8,128)(2,1)S(1)}, bf16[192,256]{1,0:T(8,128)(2,1)S(1)}, u32[]{:S(2)}, u32[]{:S(2)}) collective-permute-start(bf16[192,256]{1,0:T(8,128)(2,1)S(1)} %get-tuple-element.113), channel_id=1, source_target_pairs={{0,2},{1,3},{2,0},{3,1},{4,6},{5,7},{6,4},{7,5},{8,10},{9,11},{10,... | collective-permute-start | bytes 294920 | tf_op jit(solution)/shard_map/ppermute | solution.py:58
  78.5 5.3 %collective-permute-start.10 = (bf16[192,256]{1,0:T(8,128)(2,1)S(1)}, bf16[192,256]{1,0:T(8,128)(2,1)S(1)}, u32[]{:S(2)}, u32[]{:S(2)}) collective-permute-start(bf16[192,256]{1,0:T(8,128)(2,1)S(1)} %get-tuple-element.114), channel_id=1, source_target_pairs={{0,1},{1,0},{2,3},{3,2},{4,5},{5,4},{6,7},{7,6},{8,9},{9,8},{10,11... | collective-permute-start | bytes 294920 | tf_op jit(solution)/shard_map/ppermute | solution.py:58
  86.9 10.2 %copy-start.16 = (bf16[192,256]{1,0:T(8,128)(2,1)}, bf16[192,256]{1,0:T(8,128)(2,1)S(1)}, u32[]{:S(2)}) copy-start(bf16[192,256]{1,0:T(8,128)(2,1)S(1)} %get-tuple-element.83.g0) | copy-start | bytes 294916
  86.9 1.9 collective-permute-start.13
  87.2 5.6 %collective-permute-start.14 = (bf16[192,256]{1,0:T(8,128)(2,1)S(1)}, bf16[192,256]{1,0:T(8,128)(2,1)S(1)}, u32[]{:S(2)}, u32[]{:S(2)}) collective-permute-start(bf16[192,256]{1,0:T(8,128)(2,1)S(1)} %get-tuple-element.85), channel_id=1, source_target_pairs={{0,2},{1,3},{2,0},{3,1},{4,6},{5,7},{6,4},{7,5},{8,10},{9,11},{10,... | collective-permute-start | bytes 294920 | tf_op jit(solution)/shard_map/ppermute | solution.py:58
  88.2 5.4 %collective-permute-start.15 = (bf16[192,256]{1,0:T(8,128)(2,1)S(1)}, bf16[192,256]{1,0:T(8,128)(2,1)S(1)}, u32[]{:S(2)}, u32[]{:S(2)}) collective-permute-start(bf16[192,256]{1,0:T(8,128)(2,1)S(1)} %get-tuple-element.86), channel_id=1, source_target_pairs={{0,3},{1,2},{2,1},{3,0},{4,7},{5,6},{6,5},{7,4},{8,11},{9,10},{10,... | collective-permute-start | bytes 294920 | tf_op jit(solution)/shard_map/ppermute | solution.py:58
  88.8 8.3 %copy-start.19 = (bf16[192,256]{1,0:T(8,128)(2,1)}, bf16[192,256]{1,0:T(8,128)(2,1)S(1)}, u32[]{:S(2)}) copy-start(bf16[192,256]{1,0:T(8,128)(2,1)S(1)} %collective-permute-done.13.g1) | copy-start | bytes 294916
  92.8 4.4 %copy-start.22 = (bf16[192,256]{1,0:T(8,128)(2,1)}, bf16[192,256]{1,0:T(8,128)(2,1)S(1)}, u32[]{:S(2)}) copy-start(bf16[192,256]{1,0:T(8,128)(2,1)S(1)} %collective-permute-done.14.g2) | copy-start | bytes 294916
  93.6 3.5 %copy-start.25 = (bf16[192,256]{1,0:T(8,128)(2,1)}, bf16[192,256]{1,0:T(8,128)(2,1)S(1)}, u32[]{:S(2)}) copy-start(bf16[192,256]{1,0:T(8,128)(2,1)S(1)} %collective-permute-done.15.g3) | copy-start | bytes 294916
  97.2 0.9 copy-start.1
  98.1 21.3 %collective-permute-start.16 = (bf16[2,192,1024]{2,1,0:T(8,128)(2,1)}, bf16[2,192,1024]{2,1,0:T(8,128)(2,1)}, u32[]{:S(2)}, u32[]{:S(2)}) collective-permute-start(bf16[2,192,1024]{2,1,0:T(8,128)(2,1)} %get-tuple-element.90), channel_id=1, source_target_pairs={{0,4},{4,0},{8,12},{12,8},{16,20},{20,16},{24,28},{28,24},{1,5},{5... | collective-permute-start | bytes 2359304 | tf_op jit(solution)/shard_map/ppermute | solution.py:41
  98.6 1.0 copy-start.4
  99.6 0.9 copy-start.17
  100.5 0.9 copy-start.20
  108.2 13.4 %copy-start.43 = (f32[48,256]{1,0:T(8,128)S(1)}, f32[48,256]{1,0:T(8,128)}, u32[]{:S(2)}) copy-start(f32[48,256]{1,0:T(8,128)} %copy-done.42) | copy-start | bytes 147460
  108.2 36.7 %copy-start.18 = (bf16[192,256]{1,0:T(8,128)(2,1)S(1)}, bf16[192,256]{1,0:T(8,128)(2,1)}, u32[]{:S(2)}) copy-start(bf16[192,256]{1,0:T(8,128)(2,1)} %copy-done.16) | copy-start | bytes 294916
  108.2 36.7 %copy-start.21 = (bf16[192,256]{1,0:T(8,128)(2,1)S(1)}, bf16[192,256]{1,0:T(8,128)(2,1)}, u32[]{:S(2)}) copy-start(bf16[192,256]{1,0:T(8,128)(2,1)} %copy-done.19) | copy-start | bytes 294916
  108.2 36.7 %copy-start.24 = (bf16[192,256]{1,0:T(8,128)(2,1)S(1)}, bf16[192,256]{1,0:T(8,128)(2,1)}, u32[]{:S(2)}) copy-start(bf16[192,256]{1,0:T(8,128)(2,1)} %copy-done.22) | copy-start | bytes 294916
  108.2 36.7 %copy-start.27 = (bf16[192,256]{1,0:T(8,128)(2,1)S(1)}, bf16[192,256]{1,0:T(8,128)(2,1)}, u32[]{:S(2)}) copy-start(bf16[192,256]{1,0:T(8,128)(2,1)} %copy-done.25) | copy-start | bytes 294916
  108.2 56.7 %collective-permute-start.18 = (bf16[2,192,1024]{2,1,0:T(8,128)(2,1)}, bf16[2,192,1024]{2,1,0:T(8,128)(2,1)}, u32[]{:S(2)}, u32[]{:S(2)}) collective-permute-start(bf16[2,192,1024]{2,1,0:T(8,128)(2,1)} %get-tuple-element.97), channel_id=1, source_target_pairs={{0,4},{4,0},{8,12},{12,8},{16,20},{20,16},{24,28},{28,24},{1,5},{5... | collective-permute-start | bytes 2359304 | tf_op jit(solution)/shard_map/ppermute | solution.py:41
  120.3 44.6 %collective-permute-start.19 = (bf16[2,192,1024]{2,1,0:T(8,128)(2,1)}, bf16[2,192,1024]{2,1,0:T(8,128)(2,1)}, u32[]{:S(2)}, u32[]{:S(2)}) collective-permute-start(bf16[2,192,1024]{2,1,0:T(8,128)(2,1)} %select_add_fusion), channel_id=1, source_target_pairs={{8,0},{12,4},{16,8},{20,12},{24,16},{28,20},{9,1},{13,5},{17,9},{2... | collective-permute-start | bytes 2359304 | tf_op jit(solution)/shard_map/ppermute | solution.py:37
  121.6 41.1 %collective-permute-start.17 = (f32[48,256]{1,0:T(8,128)S(1)}, f32[48,256]{1,0:T(8,128)S(1)}, u32[]{:S(2)}, u32[]{:S(2)}) collective-permute-start(f32[48,256]{1,0:T(8,128)S(1)} %copy-done.43), channel_id=1, source_target_pairs={{0,28},{4,24},{8,20},{12,16},{16,12},{20,8},{24,4},{28,0},{1,29},{... | collective-permute-start | bytes 147464 | tf_op jit(solution)/shard_map/ppermute | solution.py:54
  147.1 0.9 copy-start.46
  164.9 3.9 %copy-start.54 = (f32[48,256]{1,0:T(8,128)S(1)}, f32[48,256]{1,0:T(8,128)}, u32[]{:S(2)}) copy-start(f32[48,256]{1,0:T(8,128)} %shard_map.157.p0) | copy-start | bytes 147460
  164.9 5.9 %copy-start.5 = (bf16[192,1024]{1,0:T(8,128)(2,1)S(1)}, bf16[192,1024]{1,0:T(8,128)(2,1)}, u32[]{:S(2)}) copy-start(bf16[192,1024]{1,0:T(8,128)(2,1)} %q_ref.17) | copy-start | bytes 1179652
  164.9 5.9 %copy-start.33 = (s32[2]{0:T(128)S(1)}, s32[2]{0:T(128)}, u32[]{:S(2)}) copy-start(s32[2]{0:T(128)} %copy-done.30) | copy-start | bytes 28
  165.0 5.9 %copy-start.37 = (s32[4,16]{1,0:T(4,128)S(1)}, s32[4,16]{1,0:T(4,128)}, u32[]{:S(2)}) copy-start(s32[4,16]{1,0:T(4,128)} %lists_ref.17) | copy-start | bytes 772
  165.0 5.9 %copy-start.41 = (s32[4]{0:T(128)S(1)}, s32[4]{0:T(128)}, u32[]{:S(2)}) copy-start(s32[4]{0:T(128)} %counts_ref.17) | copy-start | bytes 52
  165.0 5.8 %copy-start.47 = (f32[4,192,256]{2,1,0:T(8,128)S(1)}, f32[4,192,256]{2,1,0:T(8,128)}, u32[]{:S(2)}) copy-start(f32[4,192,256]{2,1,0:T(8,128)} %copy-done.46) | copy-start | bytes 2359300
  167.6 20.5 %collective-permute-start.23 = (bf16[2,192,1024]{2,1,0:T(8,128)(2,1)}, bf16[2,192,1024]{2,1,0:T(8,128)(2,1)}, u32[]{:S(2)}, u32[]{:S(2)}) collective-permute-start(bf16[2,192,1024]{2,1,0:T(8,128)(2,1)} %add_add_fusion), channel_id=1, source_target_pairs={{8,0},{12,4},{16,8},{20,12},{24,16},{28,20},{9,1},{13,5},{17,9},{2... | collective-permute-start | bytes 2359304 | tf_op jit(solution)/shard_map/ppermute | solution.py:37
  168.9 10.0 %collective-permute-start.22 = (f32[48,256]{1,0:T(8,128)S(1)}, f32[48,256]{1,0:T(8,128)S(1)}, u32[]{:S(2)}, u32[]{:S(2)}) collective-permute-start(f32[48,256]{1,0:T(8,128)S(1)} %copy-done.54), channel_id=1, source_target_pairs={{0,3},{1,2},{2,1},{3,0},{4,7},{5,6},{6,5},{7,4},{8,11},{9,10},{10,... | collective-permute-start | bytes 147464 | tf_op jit(solution)/shard_map/ppermute | solution.py:58
  169.0 10.0 %collective-permute-start.21 = (f32[48,256]{1,0:T(8,128)S(1)}, f32[48,256]{1,0:T(8,128)S(1)}, u32[]{:S(2)}, u32[]{:S(2)}) collective-permute-start(f32[48,256]{1,0:T(8,128)S(1)} %copy-done.54), channel_id=1, source_target_pairs={{0,2},{1,3},{2,0},{3,1},{4,6},{5,7},{6,4},{7,5},{8,10},{9,11},{10,... | collective-permute-start | bytes 147464 | tf_op jit(solution)/shard_map/ppermute | solution.py:58
  169.5 9.4 %collective-permute-start.20 = (f32[48,256]{1,0:T(8,128)S(1)}, f32[48,256]{1,0:T(8,128)S(1)}, u32[]{:S(2)}, u32[]{:S(2)}) collective-permute-start(f32[48,256]{1,0:T(8,128)S(1)} %copy-done.54), channel_id=1, source_target_pairs={{0,1},{1,0},{2,3},{3,2},{4,5},{5,4},{6,7},{7,6},{8,9},{9,8},{10,11... | collective-permute-start | bytes 147464 | tf_op jit(solution)/shard_map/ppermute | solution.py:58
  (20 other events, 14.0 us)

commit v3 on v2

--- a/solution.py
+++ b/solution.py
@@ -25,6 +25,10 @@
 
 def vmem(count):
     return [pl.BlockSpec(memory_space=pltpu.VMEM)] * count
+
+
+def anywhere(count):
+    return [pl.BlockSpec(memory_space=pl.ANY)] * count
 
 
 def smem(count):
@@ -135,18 +139,23 @@
     return total if together else found
 
 
-def staged(place_ref, regions, refs, copy):
+def staged(place_ref, regions, refs, raw, sems, act):
     odd = lax.rem(place_ref[0], 2)
     at = 0
     for r, region in enumerate(regions):
         if region[2] == "both":
-            copy(r, refs[at])
+            act(r, pltpu.make_async_copy(refs[at], raw.at[r], sems.at[r]))
             at += 1
             continue
         for parity in (0, 1):
             if region[parity] >= 0:
-                pl.when(odd == parity)(lambda r=r, ref=refs[at]: copy(r, ref))
+                copy = pltpu.make_async_copy(refs[at], raw.at[r], sems.at[r])
+                pl.when(odd == parity)(lambda r=r, copy=copy: act(r, copy))
                 at += 1
+
+
+def begin(r, copy):
+    copy.start()
 
 
 def region_inputs(regions):
@@ -175,25 +184,33 @@
         att_ref, lse_ref = refs.pop(0), refs.pop(0)
     else:
         acc_out, stat_out = refs.pop(0), refs.pop(0)
-    key_rows, value_cols, scaled, items, found_ref, acc_ref, stat_ref = refs
+    (key_rows, value_cols, scaled, items, found_ref, acc_ref, stat_ref, raw, q_vmem, sems,
+     q_sem) = refs
     if not closing:
         acc_ref, stat_ref = acc_out, stat_out
 
-    def copy(r, ref):
-        for b in range(blocks):
-            slot, cols = r * blocks + b, slice(b * BLOCK, (b + 1) * BLOCK)
-            value_cols[slot] = ref[1, :, cols]
-            for h in range(heads):
-                key_rows[slot, h] = ref[0, head_rows(h), cols].T
-
-    staged(place_ref, regions, slabs, copy)
+    q_copy = pltpu.make_async_copy(q_ref, q_vmem, q_sem)
+    q_copy.start()
+    staged(place_ref, regions, slabs, raw, sems, begin)
     for b, found in enumerate(live_items(
             lists_ref, counts_ref, place_ref, regions, blocks, int(opening), items, False)):
         found_ref[b] = found
-        scaled[b] = q_ref[:, b * BLOCK:(b + 1) * BLOCK] * BF16(SCALE)
     if not opening:
         acc_ref[...] = acc_in[...]
         stat_ref[...] = stat_in[...]
+    q_copy.wait()
+    for b in range(blocks):
+        scaled[b] = q_vmem[:, b * BLOCK:(b + 1) * BLOCK] * BF16(SCALE)
+
+    def spread(r, copy):
+        copy.wait()
+        for b in range(blocks):
+            slot, cols = r * blocks + b, slice(b * BLOCK, (b + 1) * BLOCK)
+            value_cols[slot] = raw[r, 1, :, cols]
+            for h in range(heads):
+                key_rows[slot, h] = raw[r, 0, head_rows(h), cols].T
+
+    staged(place_ref, regions, slabs, raw, sems, spread)
 
     def entries(b, chosen, masked=False):
         scores = [[dot(key_rows[slot, h], scaled[b, head_rows(h)]) for slot in chosen]
@@ -263,7 +280,7 @@
         functools.partial(forward_kernel, regions, not state, closing),
         out_shape=result if closing else tuple(
             jax.ShapeDtypeStruct(shape, F32) for shape in (acc, stat)),
-        in_specs=smem(3) + vmem(1 + len(slabs) + len(state)),
+        in_specs=smem(3) + anywhere(1 + len(slabs)) + vmem(len(state)),
         out_specs=tuple(vmem(2)),
         scratch_shapes=[
             pltpu.VMEM((slots, heads, BLOCK, HEAD_DIM), BF16),
@@ -273,6 +290,10 @@
             pltpu.SMEM((blocks,), jnp.int32),
             pltpu.VMEM(acc if closing else (8, BLOCK), F32),
             pltpu.VMEM(stat if closing else (8, BLOCK), F32),
+            pltpu.VMEM((len(regions), 2, width, tokens), BF16),
+            pltpu.VMEM((width, tokens), BF16),
+            pltpu.SemaphoreType.DMA((len(regions),)),
+            pltpu.SemaphoreType.DMA,
         ],
         compiler_params=pltpu.CompilerParams(vmem_limit_bytes=48 << 20),
         cost_estimate=pl.CostEstimate(
@@ -329,37 +350,45 @@
     slots = len(regions) * blocks
     refs = list(refs)
     slabs = [refs.pop(0) for _ in range(region_inputs(regions))]
-    dq_in = None if len(refs) < 12 + len(regions) else refs.pop(0)
+    dq_in = None if len(refs) < 17 + len(regions) else refs.pop(0)
     dq_ref = refs.pop(0)
     outs = [refs.pop(0) for _ in regions]
     (key_rows, value_rows, key_cols, grad_cols, scaled, sums, grad_keys, grad_values, items,
-     acc_ref) = refs
+     acc_ref, raw, q_vmem, att_vmem, sems, more_sems) = refs
+    q_copy = pltpu.make_async_copy(q_ref, q_vmem, more_sems.at[0])
+    att_copy = pltpu.make_async_copy(att_ref, att_vmem, more_sems.at[1])
+    q_copy.start()
+    att_copy.start()
+    staged(place_ref, regions, slabs, raw, sems, begin)
     me = place_ref[1]
     for k, ref in enumerate((g0, g1, g2, g3)):
         grad_cols[jnp.bitwise_xor(me, k)] = ref[...]
-
-    def copy(r, ref):
-        for b in range(blocks):
-            slot, cols = r * blocks + b, slice(b * BLOCK, (b + 1) * BLOCK)
-            key_cols[slot] = ref[0, :, cols]
-            for h in range(heads):
-                key_rows[slot, h] = ref[0, head_rows(h), cols].T
-                value_rows[slot, h] = ref[1, head_rows(h), cols].T
-
-    staged(place_ref, regions, slabs, copy)
     grad_keys[...] = jnp.zeros_like(grad_keys)
     grad_values[...] = jnp.zeros_like(grad_values)
     found = live_items(
         lists_ref, counts_ref, place_ref, regions, blocks, int(diagonal), items, True)
+    acc_ref[...] = jnp.zeros_like(acc_ref) if dq_in is None else dq_in[...]
+    q_copy.wait()
+    att_copy.wait()
     for b in range(blocks):
         cols = slice(b * BLOCK, (b + 1) * BLOCK)
-        scaled[b] = q_ref[:, cols] * BF16(SCALE)
+        scaled[b] = q_vmem[:, cols] * BF16(SCALE)
         for h in range(heads):
             rows = head_rows(h)
             sums[b, h] = jnp.sum(
-                grad_cols[b, rows].astype(F32) * att_ref[rows, cols].astype(F32),
+                grad_cols[b, rows].astype(F32) * att_vmem[rows, cols].astype(F32),
                 axis=0, keepdims=True)
-    acc_ref[...] = jnp.zeros_like(acc_ref) if dq_in is None else dq_in[...]
+
+    def spread(r, copy):
+        copy.wait()
+        for b in range(blocks):
+            slot, cols = r * blocks + b, slice(b * BLOCK, (b + 1) * BLOCK)
+            key_cols[slot] = raw[r, 0, :, cols]
+            for h in range(heads):
+                key_rows[slot, h] = raw[r, 0, head_rows(h), cols].T
+                value_rows[slot, h] = raw[r, 1, head_rows(h), cols].T
+
+    staged(place_ref, regions, slabs, raw, sems, spread)
 
     def entries(chosen, masked=False):
         tiles = [(b, slot, h, head_rows(h)) for b, slot in chosen for h in range(heads)]
@@ -417,7 +446,7 @@
         out_shape=(jax.ShapeDtypeStruct((width, tokens), BF16) if last else
                    jax.ShapeDtypeStruct((blocks, width, BLOCK), F32),)
         + (jax.ShapeDtypeStruct((2, width, tokens), F32 if diagonal else BF16),) * len(regions),
-        in_specs=smem(3) + vmem(7 + len(slabs) + len(given)),
+        in_specs=smem(3) + anywhere(2) + vmem(5) + anywhere(len(slabs)) + vmem(len(given)),
         out_specs=tuple(vmem(1 + len(regions))),
         scratch_shapes=[
             pltpu.VMEM((slots, heads, BLOCK, HEAD_DIM), BF16),
@@ -430,6 +459,11 @@
             pltpu.VMEM((slots, width, BLOCK), F32),
             pltpu.SMEM((blocks * LIST,), jnp.int32),
             pltpu.VMEM((blocks, width, BLOCK), F32),
+            pltpu.VMEM((len(regions), 2, width, tokens), BF16),
+            pltpu.VMEM((width, tokens), BF16),
+            pltpu.VMEM((width, tokens), BF16),
+            pltpu.SemaphoreType.DMA((len(regions),)),
+            pltpu.SemaphoreType.DMA((2,)),
         ],
         compiler_params=pltpu.CompilerParams(vmem_limit_bytes=48 << 20),
         cost_estimate=pl.CostEstimate(
@@ -450,23 +484,25 @@
     own = jnp.stack([key_rows, values])
     slab2 = hop(own, 2)
     state = forward(tables, queries, [(0, 0, "both")], [own])
-    *state, out_proj, cotangent, own_again = tie([*state, out_proj, cotangent, own])
+    *state, out_proj, own_again = tie([*state, out_proj, own])
     order = token_order.reshape(1, tokens)
-    grad_latent = mirror(permuted(scatter_kernel, place, order, cotangent.T))
+    landed = permuted(scatter_kernel, place, order, cotangent.T)
     weights = [across(out_proj, k) for k in range(1, cols)]
     up1 = upward(own_again)
-    *state, slab2, grad_latent, out_proj, w1, w2, w3 = tie(
-        [*state, slab2, grad_latent, out_proj, *weights])
+    *state, slab2, landed, out_proj, w1, w2, w3 = tie(
+        [*state, slab2, landed, out_proj, *weights])
     weights = [out_proj, w1, w2, w3]
     slab4 = hop(slab2, 2)
     down1 = downward(slab2)
     up2 = upward(slab2)
     state = forward(tables, queries, [(2, 2, "both")], [slab2], tuple(state))
-    *state, slab4 = tie([*state, slab4])
+    *state, slab4, landed = tie([*state, slab4, landed])
     down2 = downward(slab4)
+    grad_latent = mirror(landed)
     state = forward(tables, queries, [(1, 1, "each")], [down1, up1], tuple(state))
     state = forward(tables, queries, [(4, 4, "both"), (-1, 3, "one")], [slab4, up2], state)
-    attended, lse = forward(tables, queries, [(3, -1, "one")], [down2], state, True)
+    *state, grad_latent = tie([*state, grad_latent])
+    attended, lse = forward(tables, queries, [(3, -1, "one")], [down2], tuple(state), True)
 
     def block_of(array, b):
         return lax.dynamic_slice_in_dim(array, b * BLOCK, BLOCK, 1)
@@ -481,21 +517,21 @@
     shared = (tables, queries, attended, lse, grads)
     grad_queries, part3 = backward(*shared, [(3, 3, "each")], [down2, up2])
     from3 = mate(part3)
+    part3, latent = tie([part3, latent])
+    mirrored = mirror(latent)
     grad_queries, part4, part1 = backward(
         *shared, [(4, 4, "both"), (1, 1, "each")], [slab4, down1, up1], grad_queries)
     from1 = mate(part1)
     zero = jnp.zeros_like(part1)
     far = part4 + jnp.where(odd, from3, zero)
-    grad_queries, far, latent = tie([grad_queries, far, latent])
+    grad_queries, far, mirrored = tie([grad_queries, far, mirrored])
     far = hop(far, -2)
-    mirrored = mirror(latent)
+    reordered = permuted(gather_kernel, place, order, mirrored)
+    pieces = [reordered] + [across(reordered, k) for k in range(1, cols)]
     grad_queries, part2 = backward(*shared, [(2, 2, "both")], [slab2], grad_queries)
-    grad_queries, mirrored = tie([grad_queries, mirrored])
-    reordered = permuted(gather_kernel, place, order, mirrored)
     near = part2 + jnp.where(odd, from1, from3) + far
-    grad_queries, near, reordered = tie([grad_queries, near, reordered])
+    grad_queries, near, *pieces = tie([grad_queries, near] + pieces)
     near = hop(near, -2)
-    pieces = [reordered] + [across(reordered, k) for k in range(1, cols)]
     grad_queries, own_grad = backward(*shared, [(0, 0, "both")], [own], grad_queries, True)
     own_grad, *pieces = tie([own_grad] + pieces)
     latent_out = assembled(place, pieces, tokens).T

time: 192 us -> 185 us (0.964)
  the two profiles are of different devices: /device:TPU:0 before, /device:TPU:8 now
where the time goes in v3:
time: 185 us; the launch traced here: 181 us
  starting transfers between devices  59.1 us (32%)
  waiting for transfers between devices  52.4 us (28%)
  Pallas kernels  43 us (23%)
  local copies, waits for them, and re-layouts  19.2 us (10%)
  other arithmetic  6.47 us (3%)
    ppermute x4, waiting for transfers between devices, hop(): return lax.ppermute(array, 'row', pairs)  21.7 us
    pallas_call x4, Pallas kernels, backward(): pl.pallas_call(functools.partial(backward_kernel, regions, diagonal, last...  20.7 us
    ppermute x12, waiting for transfers between devices, across(): lax.ppermute(array, 'col', [(i, i ^ bits) for i in range(lax.axis_size('c...  20.5 us
    ppermute x4, starting transfers between devices, hop(): return lax.ppermute(array, 'row', pairs)  18.8 us
    unnamed x116, local copies, waits for them, and re-layouts  18.2 us
    ppermute x2, starting transfers between devices, mirror(): return lax.ppermute(array, 'row', [(i, size - 1 - i) for i in range(size)])  16.9 us
    pallas_call x5, Pallas kernels, forward(): pl.pallas_call(functools.partial(forward_kernel, regions, not state, clos...  14.7 us
    ppermute x2, starting transfers between devices, upward(): lax.ppermute(array, 'row', [(i, i + 1) for i in range(0, lax.axis_size('r...  9.45 us
  transfers between devices with their start and end apart: 24, of which 11 were waited for; matrix products, arithmetic and copies ran while one was open for 2% of the time, Pallas kernels for 19%

profile of v3, /device:TPU:8, one launch (start us, length us, event | category | flops | bytes accessed | tf_op | source)
XLA Modules:
  0.0 181.4 jit_solution(1593904667802396992)
XLA Ops:
  0.7 1.2 pad_maximum_fusion.refs_0_
  1.9 3.5 %collective-permute-start = (bf16[2,192,1024]{2,1,0:T(8,128)(2,1)S(1)}, bf16[2,192,1024]{2,1,0:T(8,128)(2,1)}, u32[]{:S(2)}, u32[]{:S(2)}) collective-permute-start(bf16[2,192,1024]{2,1,0:T(8,128)(2,1)S(1)} %pad_maximum_fusion.refs_0_), channel_id=1, source_target_pairs={{0,8},{4,12},{8,16},{12,20},{16,24},{20,28},{1,9},{5,13},{9,17},{1... | collective-permute-start | bytes 2359304 | tf_op jit(solution)/shard_map/ppermute | solution.py:41
  5.5 3.2 %shard_map.147 = (f32[4,192,256]{2,1,0:T(8,128)S(1)}, f32[4,6,1,256]{3,2,1,0:T(1,128)S(1)}) custom-call(s32[4,16]{1,0:T(4,128)S(1)} %copy-done.32, s32[4]{0:T(128)S(1)} %copy-done.37, s32[2]{0:T(128)S(1)} %pad_add_fusion.place_ref, bf16[192,1024]{1,0:T(8,128)(2,1)S(1)} %copy-done.2, bf16[2,192,1024]{2,1,0:T(8,128)(2,1)S(1)} %pad_maximum_fusion.refs_0_), custom_call_target="tpu_custom_call" | custom-call | flops 1000000000 | bytes 6291456 | tf_op jit(solution)/shard_map/pallas_call | solution.py:279
  8.8 0.9 copy-done.47
  10.9 0.9 collective-permute-start.2
  12.1 1.8 %shard_map.148 = f32[48,256]{1,0:T(8,128)} custom-call(s32[2]{0:T(128)} %copy-done.28, s32[1,1024]{1,0:T(1,128)} %bitcast.17, f32[48,1024]{1,0:T(8,128)} %bitcast.16), custom_call_target="tpu_custom_call" | custom-call | tf_op jit(solution)/shard_map/pallas_call | solution.py:92
  13.9 5.6 %collective-permute-done.3.w3 = bf16[192,768]{1,0:T(8,128)(2,1)S(1)} collective-permute-done((bf16[192,768]{1,0:T(8,128)(2,1)S(1)}, bf16[192,768]{1,0:T(8,128)(2,1)S(1)}, u32[]{:S(2)}, u32[]{:S(2)}) %collective-permute-start.3) | collective-permute-done | bytes 294944 | tf_op jit(solution)/shard_map/ppermute | solution.py:62
  19.5 0.7 copy-done.8
  20.2 5.6 %collective-permute-done.2.w2 = bf16[192,768]{1,0:T(8,128)(2,1)S(1)} collective-permute-done((bf16[192,768]{1,0:T(8,128)(2,1)S(1)}, bf16[192,768]{1,0:T(8,128)(2,1)S(1)}, u32[]{:S(2)}, u32[]{:S(2)}) %collective-permute-start.2) | collective-permute-done | bytes 294944 | tf_op jit(solution)/shard_map/ppermute | solution.py:62
  25.9 0.7 copy-done.10
  26.6 0.7 copy-done.12
  27.3 5.7 %collective-permute-start.4 = (bf16[2,192,1024]{2,1,0:T(8,128)(2,1)}, bf16[2,192,1024]{2,1,0:T(8,128)(2,1)S(1)}, u32[]{:S(2)}, u32[]{:S(2)}) collective-permute-start(bf16[2,192,1024]{2,1,0:T(8,128)(2,1)} %collective-permute-done.refs_0_), channel_id=1, source_target_pairs={{0,8},{4,12},{8,16},{12,20},{16,24},{20,28},{1,9},{5,13},{9,17},{1... | collective-permute-start | bytes 2359304 | tf_op jit(solution)/shard_map/ppermute | solution.py:41
  33.0 4.0 %collective-permute-start.8 = (bf16[2,192,1024]{2,1,0:T(8,128)(2,1)S(1)}, bf16[2,192,1024]{2,1,0:T(8,128)(2,1)S(1)}, u32[]{:S(2)}, u32[]{:S(2)}) collective-permute-start(bf16[2,192,1024]{2,1,0:T(8,128)(2,1)S(1)} %pad_maximum_fusion.refs_0_), channel_id=1, source_target_pairs={{0,4},{8,12},{16,20},{24,28},{1,5},{9,13},{17,21},{25,29},{2,6},{1... | collective-permute-start | bytes 2359304 | tf_op jit(solution)/shard_map/ppermute | solution.py:49
  37.0 1.3 collective-permute-start.7
  38.3 5.5 %collective-permute-start.6 = (bf16[2,192,1024]{2,1,0:T(8,128)(2,1)}, bf16[2,192,1024]{2,1,0:T(8,128)(2,1)}, u32[]{:S(2)}, u32[]{:S(2)}) collective-permute-start(bf16[2,192,1024]{2,1,0:T(8,128)(2,1)} %collective-permute-done.refs_0_), channel_id=1, source_target_pairs={{0,4},{8,12},{16,20},{24,28},{1,5},{9,13},{17,21},{25,29},{2,6},{1... | collective-permute-start | bytes 2359304 | tf_op jit(solution)/shard_map/ppermute | solution.py:49
  43.8 0.7 copy-done.29
  44.5 1.1 copy-done.48
  45.6 0.7 copy-done.52
  46.3 3.8 %shard_map.149 = (f32[4,192,256]{2,1,0:T(8,128)S(1)}, f32[4,6,1,256]{3,2,1,0:T(1,128)S(1)}) custom-call(s32[4,16]{1,0:T(4,128)S(1)} %copy-done.32, s32[4]{0:T(128)S(1)} %copy-done.37, s32[2]{0:T(128)S(1)} %copy-done.29, bf16[192,1024]{1,0:T(8,128)(2,1)S(1)} %copy-done.2, bf16[2,192,1024]{2,1,0:T(8,128)(2,1)} %collective-permute-done.refs_0_, ...), custom_call_target="tpu_custom_call" | custom-call | flops 1000000000 | bytes 6291456 | tf_op jit(solution)/shard_map/pallas_call | solution.py:279
  50.2 0.9 copy-done.45
  51.6 1.3 collective-permute-start.5
  52.9 6.7 %collective-permute-start.9 = (f32[48,256]{1,0:T(8,128)}, f32[48,256]{1,0:T(8,128)S(1)}, u32[]{:S(2)}, u32[]{:S(2)}) collective-permute-start(f32[48,256]{1,0:T(8,128)} %shard_map.148), channel_id=1, source_target_pairs={{0,28},{4,24},{8,20},{12,16},{16,12},{20,8},{24,4},{28,0},{1,29},{... | collective-permute-start | bytes 147464 | tf_op jit(solution)/shard_map/ppermute | solution.py:58
  59.7 1.1 copy-done.46
  60.8 0.7 copy-done.50
  61.6 3.8 %shard_map.150 = (f32[4,192,256]{2,1,0:T(8,128)S(1)}, f32[4,6,1,256]{3,2,1,0:T(1,128)S(1)}) custom-call(s32[4,16]{1,0:T(4,128)S(1)} %copy-done.32, s32[4]{0:T(128)S(1)} %copy-done.37, s32[2]{0:T(128)S(1)} %copy-done.30, bf16[192,1024]{1,0:T(8,128)(2,1)S(1)} %copy-done.2, bf16[2,192,1024]{2,1,0:T(8,128)(2,1)S(1)} %collective-permute-done.7.refs_0_.refs_1_, ...), custom_call_target="tpu_custom_call" | custom-call | flops 1000000000 | bytes 6291456 | tf_op jit(solution)/shard_map/pallas_call | solution.py:279
  65.4 6.3 %collective-permute-done.6.refs_1_ = bf16[2,192,1024]{2,1,0:T(8,128)(2,1)} collective-permute-done((bf16[2,192,1024]{2,1,0:T(8,128)(2,1)}, bf16[2,192,1024]{2,1,0:T(8,128)(2,1)}, u32[]{:S(2)}, u32[]{:S(2)}) %collective-permute-start.6) | collective-permute-done | bytes 786464 | tf_op jit(solution)/shard_map/ppermute | solution.py:49
  71.7 1.5 shard_map.151
  73.3 2.7 %collective-permute-done.5.refs_0_ = bf16[2,192,1024]{2,1,0:T(8,128)(2,1)} collective-permute-done((bf16[2,192,1024]{2,1,0:T(8,128)(2,1)S(1)}, bf16[2,192,1024]{2,1,0:T(8,128)(2,1)}, u32[]{:S(2)}, u32[]{:S(2)}) %collective-permute-start.5) | collective-permute-done | bytes 786464 | tf_op jit(solution)/shard_map/ppermute | solution.py:53
  76.1 2.4 %shard_map.152 = (bf16[192,1024]{1,0:T(8,128)(2,1)S(1)}, f32[4,3,1,256]{3,2,1,0:T(1,128)S(1)}) custom-call(s32[4,16]{1,0:T(4,128)S(1)} %copy-done.33, s32[4]{0:T(128)S(1)} %copy-done.38, s32[2]{0:T(128)S(1)} %copy-done.30, bf16[192,1024]{1,0:T(8,128)(2,1)S(1)} %copy-done.3, bf16[2,192,1024]{2,1,0:T(8,128)(2,1)} %collective-permute-done.5.refs_0_, ...), custom_call_target="tpu_custom_call" | custom-call | flops 1000000000 | bytes 6291456 | tf_op jit(solution)/shard_map/pallas_call | solution.py:279
  78.6 1.1 collective-permute-start.11
  79.7 0.8 collective-permute-start.10
  80.5 3.1 %collective-permute-done.12.a3 = bf16[192,256]{1,0:T(8,128)(2,1)S(1)} collective-permute-done((bf16[192,256]{1,0:T(8,128)(2,1)S(1)}, bf16[192,256]{1,0:T(8,128)(2,1)S(1)}, u32[]{:S(2)}, u32[]{:S(2)}) %collective-permute-start.12) | collective-permute-done | bytes 98336 | tf_op jit(solution)/shard_map/ppermute | solution.py:62
  83.6 1.4 collective-permute-done.11.a2
  85.0 2.5 %shard_map.153 = (f32[48,256]{1,0:T(8,128)S(1)}, bf16[192,256]{1,0:T(8,128)(2,1)S(1)}, bf16[192,256]{1,0:T(8,128)(2,1)S(1)}, bf16[192,256]{1,0:T(8,128)(2,1)S(1)}, bf16[192,256]{1,0:T(8,128)(2,1)S(1)}) custom-call(s32[2]{0:T(128)S(1)} %copy-done.30, bf16[192,256]{1,0:T(8,128)(2,1)S(1)} %get-tuple-element.125.a0, ...), custom_call_target="tpu_custom_call" | custom-call | tf_op jit(solution)/shard_map/pallas_call | solution.py:334
  87.8 1.0 collective-permute-start.14
  89.4 4.0 %collective-permute-done.14.g2 = bf16[192,256]{1,0:T(8,128)(2,1)S(1)} collective-permute-done((bf16[192,256]{1,0:T(8,128)(2,1)S(1)}, bf16[192,256]{1,0:T(8,128)(2,1)S(1)}, u32[]{:S(2)}, u32[]{:S(2)}) %collective-permute-start.14) | collective-permute-done | bytes 98336 | tf_op jit(solution)/shard_map/ppermute | solution.py:62
  93.4 0.9 collective-permute-done.15.g3
  94.3 3.8 %shard_map.154 = (f32[4,192,256]{2,1,0:T(8,128)S(1)}, bf16[2,192,1024]{2,1,0:T(8,128)(2,1)}) custom-call(s32[4,16]{1,0:T(4,128)S(1)} %copy-done.33, s32[4]{0:T(128)S(1)} %copy-done.38, s32[2]{0:T(128)S(1)} %copy-done.30, bf16[192,1024]{1,0:T(8,128)(2,1)S(1)} %copy-done.3, bf16[192,1024]{1,0:T(8,128)(2,1)S(1)} %get-tuple-element.84.att_ref, ...), custom_call_target="tpu_custom_call" | custom-call | flops 1000000000 | bytes 8388608 | tf_op jit(solution)/shard_map/pallas_call | solution.py:444
  98.1 0.9 copy-done.1
  99.0 3.6 %collective-permute-start.16 = (bf16[2,192,1024]{2,1,0:T(8,128)(2,1)}, bf16[2,192,1024]{2,1,0:T(8,128)(2,1)}, u32[]{:S(2)}, u32[]{:S(2)}) collective-permute-start(bf16[2,192,1024]{2,1,0:T(8,128)(2,1)} %get-tuple-element.98), channel_id=1, source_target_pairs={{0,4},{4,0},{8,12},{12,8},{16,20},{20,16},{24,28},{28,24},{1,5},{5... | collective-permute-start | bytes 2359304 | tf_op jit(solution)/shard_map/ppermute | solution.py:45
  102.5 10.1 %collective-permute-start.17 = (f32[48,256]{1,0:T(8,128)}, f32[48,256]{1,0:T(8,128)S(1)}, u32[]{:S(2)}, u32[]{:S(2)}) collective-permute-start(f32[48,256]{1,0:T(8,128)} %copy-done.44), channel_id=1, source_target_pairs={{0,28},{4,24},{8,20},{12,16},{16,12},{20,8},{24,4},{28,0},{1,29},{... | collective-permute-start | bytes 147464 | tf_op jit(solution)/shard_map/ppermute | solution.py:58
  112.7 1.0 copy-done.4
  113.7 0.9 copy-done.17
  114.6 0.9 copy-done.20
  115.5 0.9 copy-done.23
  116.3 0.9 copy-done.26
  117.2 0.7 copy-done.34
  118.6 7.3 %shard_map.155 = (f32[4,192,256]{2,1,0:T(8,128)S(1)}, bf16[2,192,1024]{2,1,0:T(8,128)(2,1)S(1)}, bf16[2,192,1024]{2,1,0:T(8,128)(2,1)}) custom-call(s32[4,16]{1,0:T(4,128)S(1)} %copy-done.34, s32[4]{0:T(128)S(1)} %copy-done.39, s32[2]{0:T(128)S(1)} %copy-done.30, bf16[192,1024]{1,0:T(8,128)(2,1)S(1)} %copy-done.4, ...), custom_call_target="tpu_custom_call" | custom-call | flops 1000000000 | bytes 8388608 | tf_op jit(solution)/shard_map/pallas_call | solution.py:444
  126.2 1.0 select_add_fusion
  127.8 7.7 %collective-permute-start.19 = (bf16[2,192,1024]{2,1,0:T(8,128)(2,1)}, bf16[2,192,1024]{2,1,0:T(8,128)(2,1)}, u32[]{:S(2)}, u32[]{:S(2)}) collective-permute-start(bf16[2,192,1024]{2,1,0:T(8,128)(2,1)} %select_add_fusion), channel_id=1, source_target_pairs={{8,0},{12,4},{16,8},{20,12},{24,16},{28,20},{9,1},{13,5},{17,9},{2... | collective-permute-start | bytes 2359304 | tf_op jit(solution)/shard_map/ppermute | solution.py:41
  135.5 1.7 shard_map.157.p0
  137.1 0.8 collective-permute-start.21
  137.9 1.1 collective-permute-start.20
  139.1 1.1 copy-done.43
  140.2 4.6 %shard_map.156 = (f32[4,192,256]{2,1,0:T(8,128)S(1)}, bf16[2,192,1024]{2,1,0:T(8,128)(2,1)S(1)}) custom-call(s32[4,16]{1,0:T(4,128)S(1)} %copy-done.35, s32[4]{0:T(128)S(1)} %copy-done.40, s32[2]{0:T(128)S(1)} %copy-done.31, bf16[192,1024]{1,0:T(8,128)(2,1)S(1)} %copy-done.5, bf16[192,1024]{1,0:T(8,128)(2,1)S(1)} %get-tuple-element.84.att_ref, ...), custom_call_target="tpu_custom_call" | custom-call | flops 1000000000 | bytes 8388608 | tf_op jit(solution)/shard_map/pallas_call | solution.py:444
  144.8 1.0 collective-permute-done.18
  145.9 9.1 %collective-permute-done.19 = bf16[2,192,1024]{2,1,0:T(8,128)(2,1)} collective-permute-done((bf16[2,192,1024]{2,1,0:T(8,128)(2,1)}, bf16[2,192,1024]{2,1,0:T(8,128)(2,1)}, u32[]{:S(2)}, u32[]{:S(2)}) %collective-permute-start.19) | collective-permute-done | bytes 786464 | tf_op jit(solution)/shard_map/ppermute | solution.py:41
  154.9 2.4 %add_add_fusion = bf16[2,192,1024]{2,1,0:T(8,128)(2,1)} fusion(bf16[2,192,1024]{2,1,0:T(8,128)(2,1)} %collective-permute-done.19, bf16[2,192,1024]{2,1,0:T(8,128)(2,1)S(1)} %get-tuple-element.103, bf16[2,192,1024]{2,1,0:T(8,128)(2,1)} %collective-permute-done.18, bf16[2,192,1024]{2,1,0:T(8,128)(2,1)} %collective-permute-done.16, pred[]{:T(512)S(6)} %eq.5), kind=kLoop, calls=%fused_computation.2 | loop fusion | flops 1179648 | bytes 3932161 | tf_op jit(solution)/shard_map/add | solution.py:532
  157.4 1.9 %collective-permute-start.23 = (bf16[2,192,1024]{2,1,0:T(8,128)(2,1)}, bf16[2,192,1024]{2,1,0:T(8,128)(2,1)}, u32[]{:S(2)}, u32[]{:S(2)}) collective-permute-start(bf16[2,192,1024]{2,1,0:T(8,128)(2,1)} %add_add_fusion), channel_id=1, source_target_pairs={{8,0},{12,4},{16,8},{20,12},{24,16},{28,20},{9,1},{13,5},{17,9},{2... | collective-permute-start | bytes 2359304 | tf_op jit(solution)/shard_map/ppermute | solution.py:41
  159.4 5.0 %shard_map.158 = (bf16[192,1024]{1,0:T(8,128)(2,1)}, f32[2,192,1024]{2,1,0:T(8,128)S(1)}) custom-call(s32[4,16]{1,0:T(4,128)S(1)} %copy-done.36, s32[4]{0:T(128)S(1)} %copy-done.41, s32[2]{0:T(128)S(1)} %copy-done.31, bf16[192,1024]{1,0:T(8,128)(2,1)S(1)} %copy-done.5, bf16[192,1024]{1,0:T(8,128)(2,1)S(1)} %get-tuple-element.84.att_ref, ...), custom_call_target="tpu_custom_call" | custom-call | flops 1000000000 | bytes 8388608 | tf_op jit(solution)/shard_map/pallas_call | solution.py:444
  164.4 1.6 shard_map.159
  166.0 12.7 %collective-permute-done.23 = bf16[2,192,1024]{2,1,0:T(8,128)(2,1)} collective-permute-done((bf16[2,192,1024]{2,1,0:T(8,128)(2,1)}, bf16[2,192,1024]{2,1,0:T(8,128)(2,1)}, u32[]{:S(2)}, u32[]{:S(2)}) %collective-permute-start.23) | collective-permute-done | bytes 786464 | tf_op jit(solution)/shard_map/ppermute | solution.py:41
  178.7 1.7 add_convert_fusion
  180.4 0.9 slice_bitcast_fusion
  (121 shorter events, 5.0 us)
Async XLA Ops:
  0.6 4.9 %copy-start.37 = (s32[4]{0:T(128)S(1)}, s32[4]{0:T(128)}, u32[]{:S(2)}) copy-start(s32[4]{0:T(128)} %counts_ref.17) | copy-start | bytes 52
  0.6 4.8 %copy-start.32 = (s32[4,16]{1,0:T(4,128)S(1)}, s32[4,16]{1,0:T(4,128)}, u32[]{:S(2)}) copy-start(s32[4,16]{1,0:T(4,128)} %lists_ref.17) | copy-start | bytes 772
  0.7 4.8 %copy-start.2 = (bf16[192,1024]{1,0:T(8,128)(2,1)S(1)}, bf16[192,1024]{1,0:T(8,128)(2,1)}, u32[]{:S(2)}) copy-start(bf16[192,1024]{1,0:T(8,128)(2,1)} %q_ref.17) | copy-start | bytes 1179652
  1.9 25.4 %collective-permute-start = (bf16[2,192,1024]{2,1,0:T(8,128)(2,1)S(1)}, bf16[2,192,1024]{2,1,0:T(8,128)(2,1)}, u32[]{:S(2)}, u32[]{:S(2)}) collective-permute-start(bf16[2,192,1024]{2,1,0:T(8,128)(2,1)S(1)} %pad_maximum_fusion.refs_0_), channel_id=1, source_target_pairs={{0,8},{4,12},{8,16},{12,20},{16,24},{20,28},{1,9},{5,13},{9,17},{1... | collective-permute-start | bytes 2359304 | tf_op jit(solution)/shard_map/ppermute | solution.py:41
  5.5 3.2 %copy-start.28 = (s32[2]{0:T(128)}, s32[2]{0:T(128)S(1)}, u32[]{:S(2)}) copy-start(s32[2]{0:T(128)S(1)} %pad_add_fusion.place_ref) | copy-start | bytes 28
  5.5 4.7 %copy-start.6 = (bf16[192,768]{1,0:T(8,128)(2,1)S(1)}, bf16[192,768]{1,0:T(8,128)(2,1)}, u32[]{:S(2)}) copy-start(bf16[192,768]{1,0:T(8,128)(2,1)} %w0) | copy-start | bytes 884740
  10.2 9.3 %collective-permute-start.3 = (bf16[192,768]{1,0:T(8,128)(2,1)S(1)}, bf16[192,768]{1,0:T(8,128)(2,1)S(1)}, u32[]{:S(2)}, u32[]{:S(2)}) collective-permute-start(bf16[192,768]{1,0:T(8,128)(2,1)S(1)} %copy-done.6), channel_id=1, source_target_pairs={{0,3},{1,2},{2,1},{3,0},{4,7},{5,6},{6,5},{7,4},{8,11},{9,10},{10,... | collective-permute-start | bytes 884744 | tf_op jit(solution)/shard_map/ppermute | solution.py:62
  10.9 15.0 %collective-permute-start.2 = (bf16[192,768]{1,0:T(8,128)(2,1)S(1)}, bf16[192,768]{1,0:T(8,128)(2,1)S(1)}, u32[]{:S(2)}, u32[]{:S(2)}) collective-permute-start(bf16[192,768]{1,0:T(8,128)(2,1)S(1)} %copy-done.6), channel_id=1, source_target_pairs={{0,2},{1,3},{2,0},{3,1},{4,6},{5,7},{6,4},{7,5},{8,10},{9,11},{10,... | collective-permute-start | bytes 884744 | tf_op jit(solution)/shard_map/ppermute | solution.py:62
  11.8 14.8 %collective-permute-start.1 = (bf16[192,768]{1,0:T(8,128)(2,1)S(1)}, bf16[192,768]{1,0:T(8,128)(2,1)S(1)}, u32[]{:S(2)}, u32[]{:S(2)}) collective-permute-start(bf16[192,768]{1,0:T(8,128)(2,1)S(1)} %copy-done.6), channel_id=1, source_target_pairs={{0,1},{1,0},{2,3},{3,2},{4,5},{5,4},{6,7},{7,6},{8,9},{9,8},{10,11... | collective-permute-start | bytes 884744 | tf_op jit(solution)/shard_map/ppermute | solution.py:62
  12.1 47.6 %copy-start.30 = (s32[2]{0:T(128)S(1)}, s32[2]{0:T(128)}, u32[]{:S(2)}) copy-start(s32[2]{0:T(128)} %copy-done.28) | copy-start | bytes 28
  27.3 24.3 %collective-permute-start.4 = (bf16[2,192,1024]{2,1,0:T(8,128)(2,1)}, bf16[2,192,1024]{2,1,0:T(8,128)(2,1)S(1)}, u32[]{:S(2)}, u32[]{:S(2)}) collective-permute-start(bf16[2,192,1024]{2,1,0:T(8,128)(2,1)} %collective-permute-done.refs_0_), channel_id=1, source_target_pairs={{0,8},{4,12},{8,16},{12,20},{16,24},{20,28},{1,9},{5,13},{9,17},{1... | collective-permute-start | bytes 2359304 | tf_op jit(solution)/shard_map/ppermute | solution.py:41
  33.0 26.6 %collective-permute-start.8 = (bf16[2,192,1024]{2,1,0:T(8,128)(2,1)S(1)}, bf16[2,192,1024]{2,1,0:T(8,128)(2,1)S(1)}, u32[]{:S(2)}, u32[]{:S(2)}) collective-permute-start(bf16[2,192,1024]{2,1,0:T(8,128)(2,1)S(1)} %pad_maximum_fusion.refs_0_), channel_id=1, source_target_pairs={{0,4},{8,12},{16,20},{24,28},{1,5},{9,13},{17,21},{25,29},{2,6},{1... | collective-permute-start | bytes 2359304 | tf_op jit(solution)/shard_map/ppermute | solution.py:49
  37.0 22.7 %collective-permute-start.7 = (bf16[2,192,1024]{2,1,0:T(8,128)(2,1)}, bf16[2,192,1024]{2,1,0:T(8,128)(2,1)S(1)}, u32[]{:S(2)}, u32[]{:S(2)}) collective-permute-start(bf16[2,192,1024]{2,1,0:T(8,128)(2,1)} %collective-permute-done.refs_0_), channel_id=1, source_target_pairs={{4,0},{12,8},{20,16},{28,24},{5,1},{13,9},{21,17},{29,25},{6,2},{1... | collective-permute-start | bytes 2359304 | tf_op jit(solution)/shard_map/ppermute | solution.py:53
  38.3 33.4 %collective-permute-start.6 = (bf16[2,192,1024]{2,1,0:T(8,128)(2,1)}, bf16[2,192,1024]{2,1,0:T(8,128)(2,1)}, u32[]{:S(2)}, u32[]{:S(2)}) collective-permute-start(bf16[2,192,1024]{2,1,0:T(8,128)(2,1)} %collective-permute-done.refs_0_), channel_id=1, source_target_pairs={{0,4},{8,12},{16,20},{24,28},{1,5},{9,13},{17,21},{25,29},{2,6},{1... | collective-permute-start | bytes 2359304 | tf_op jit(solution)/shard_map/ppermute | solution.py:49
  44.5 1.1 copy-start.48
  51.6 24.4 %collective-permute-start.5 = (bf16[2,192,1024]{2,1,0:T(8,128)(2,1)S(1)}, bf16[2,192,1024]{2,1,0:T(8,128)(2,1)}, u32[]{:S(2)}, u32[]{:S(2)}) collective-permute-start(bf16[2,192,1024]{2,1,0:T(8,128)(2,1)S(1)} %collective-permute-done.4.refs_0_), channel_id=1, source_target_pairs={{4,0},{12,8},{20,16},{28,24},{5,1},{13,9},{21,17},{29,25},{6,2},{1... | collective-permute-start | bytes 2359304 | tf_op jit(solution)/shard_map/ppermute | solution.py:53
  52.9 20.3 %collective-permute-start.9 = (f32[48,256]{1,0:T(8,128)}, f32[48,256]{1,0:T(8,128)S(1)}, u32[]{:S(2)}, u32[]{:S(2)}) collective-permute-start(f32[48,256]{1,0:T(8,128)} %shard_map.148), channel_id=1, source_target_pairs={{0,28},{4,24},{8,20},{12,16},{16,12},{20,8},{24,4},{28,0},{1,29},{... | collective-permute-start | bytes 147464 | tf_op jit(solution)/shard_map/ppermute | solution.py:58
  59.7 1.1 copy-start.46
  71.7 4.4 %copy-start.3 = (bf16[192,1024]{1,0:T(8,128)(2,1)S(1)}, bf16[192,1024]{1,0:T(8,128)(2,1)}, u32[]{:S(2)}) copy-start(bf16[192,1024]{1,0:T(8,128)(2,1)} %q_ref.17) | copy-start | bytes 1179652
  71.7 4.4 %copy-start.33 = (s32[4,16]{1,0:T(4,128)S(1)}, s32[4,16]{1,0:T(4,128)}, u32[]{:S(2)}) copy-start(s32[4,16]{1,0:T(4,128)} %lists_ref.17) | copy-start | bytes 772
  71.7 4.4 %copy-start.38 = (s32[4]{0:T(128)S(1)}, s32[4]{0:T(128)}, u32[]{:S(2)}) copy-start(s32[4]{0:T(128)} %counts_ref.17) | copy-start | bytes 52
  73.2 7.2 %copy-start.57 = (f32[768]{0:T(1024)S(1)}, f32[768]{0:T(1024)}, u32[]{:S(2)}) copy-start(f32[768]{0:T(1024)} %param.19) | copy-start | bytes 9220
  73.2 11.7 %copy-start = (bf16[1024,768]{1,0:T(8,128)(2,1)S(1)}, bf16[1024,768]{1,0:T(8,128)(2,1)}, u32[]{:S(2)}) copy-start(bf16[1024,768]{1,0:T(8,128)(2,1)} %stream_ref.1) | copy-start | bytes 4718596
  73.3 11.7 %copy-start.7 = (bf16[192,768]{1,0:T(8,128)(2,1)S(1)}, bf16[192,768]{1,0:T(8,128)(2,1)}, u32[]{:S(2)}) copy-start(bf16[192,768]{1,0:T(8,128)(2,1)} %w0) | copy-start | bytes 884740
  73.3 11.7 %copy-start.9 = (bf16[192,768]{1,0:T(8,128)(2,1)S(1)}, bf16[192,768]{1,0:T(8,128)(2,1)}, u32[]{:S(2)}) copy-start(bf16[192,768]{1,0:T(8,128)(2,1)} %copy-done.8) | copy-start | bytes 884740
  73.3 11.7 %copy-start.11 = (bf16[192,768]{1,0:T(8,128)(2,1)S(1)}, bf16[192,768]{1,0:T(8,128)(2,1)}, u32[]{:S(2)}) copy-start(bf16[192,768]{1,0:T(8,128)(2,1)} %copy-done.10) | copy-start | bytes 884740
  73.3 11.7 %copy-start.13 = (bf16[192,768]{1,0:T(8,128)(2,1)S(1)}, bf16[192,768]{1,0:T(8,128)(2,1)}, u32[]{:S(2)}) copy-start(bf16[192,768]{1,0:T(8,128)(2,1)} %copy-done.12) | copy-start | bytes 884740
  73.3 11.7 %copy-start.14 = (f32[1024,48]{0,1:T(8,128)S(1)}, f32[1024,48]{0,1:T(8,128)}, u32[]{:S(2)}) copy-start(f32[1024,48]{0,1:T(8,128)} %param.21) | copy-start | bytes 589828
  73.3 11.7 %copy-start.15 = (bf16[96,768]{1,0:T(8,128)(2,1)S(1)}, bf16[96,768]{1,0:T(8,128)(2,1)}, u32[]{:S(2)}) copy-start(bf16[96,768]{1,0:T(8,128)(2,1)} %head_ref.1) | copy-start | bytes 442372
  78.5 5.1 %collective-permute-start.12 = (bf16[192,256]{1,0:T(8,128)(2,1)S(1)}, bf16[192,256]{1,0:T(8,128)(2,1)S(1)}, u32[]{:S(2)}, u32[]{:S(2)}) collective-permute-start(bf16[192,256]{1,0:T(8,128)(2,1)S(1)} %get-tuple-element.122), channel_id=1, source_target_pairs={{0,3},{1,2},{2,1},{3,0},{4,7},{5,6},{6,5},{7,4},{8,11},{9,10},{10,... | collective-permute-start | bytes 294920 | tf_op jit(solution)/shard_map/ppermute | solution.py:62
  78.6 6.4 %collective-permute-start.11 = (bf16[192,256]{1,0:T(8,128)(2,1)S(1)}, bf16[192,256]{1,0:T(8,128)(2,1)S(1)}, u32[]{:S(2)}, u32[]{:S(2)}) collective-permute-start(bf16[192,256]{1,0:T(8,128)(2,1)S(1)} %get-tuple-element.123), channel_id=1, source_target_pairs={{0,2},{1,3},{2,0},{3,1},{4,6},{5,7},{6,4},{7,5},{8,10},{9,11},{10,... | collective-permute-start | bytes 294920 | tf_op jit(solution)/shard_map/ppermute | solution.py:62
  79.7 5.3 %collective-permute-start.10 = (bf16[192,256]{1,0:T(8,128)(2,1)S(1)}, bf16[192,256]{1,0:T(8,128)(2,1)S(1)}, u32[]{:S(2)}, u32[]{:S(2)}) collective-permute-start(bf16[192,256]{1,0:T(8,128)(2,1)S(1)} %get-tuple-element.124), channel_id=1, source_target_pairs={{0,1},{1,0},{2,3},{3,2},{4,5},{5,4},{6,7},{7,6},{8,9},{9,8},{10,11... | collective-permute-start | bytes 294920 | tf_op jit(solution)/shard_map/ppermute | solution.py:62
  87.5 6.8 %copy-start.44 = (f32[48,256]{1,0:T(8,128)}, f32[48,256]{1,0:T(8,128)S(1)}, u32[]{:S(2)}) copy-start(f32[48,256]{1,0:T(8,128)S(1)} %get-tuple-element.100) | copy-start | bytes 147460
  87.5 10.5 %copy-start.16 = (bf16[192,256]{1,0:T(8,128)(2,1)}, bf16[192,256]{1,0:T(8,128)(2,1)S(1)}, u32[]{:S(2)}) copy-start(bf16[192,256]{1,0:T(8,128)(2,1)S(1)} %get-tuple-element.91.g0) | copy-start | bytes 294916
  87.5 1.9 %collective-permute-start.13 = (bf16[192,256]{1,0:T(8,128)(2,1)S(1)}, bf16[192,256]{1,0:T(8,128)(2,1)S(1)}, u32[]{:S(2)}, u32[]{:S(2)}) collective-permute-start(bf16[192,256]{1,0:T(8,128)(2,1)S(1)} %get-tuple-element.92), channel_id=1, source_target_pairs={{0,1},{1,0},{2,3},{3,2},{4,5},{5,4},{6,7},{7,6},{8,9},{9,8},{10,11... | collective-permute-start | bytes 294920 | tf_op jit(solution)/shard_map/ppermute | solution.py:62
  87.8 5.6 %collective-permute-start.14 = (bf16[192,256]{1,0:T(8,128)(2,1)S(1)}, bf16[192,256]{1,0:T(8,128)(2,1)S(1)}, u32[]{:S(2)}, u32[]{:S(2)}) collective-permute-start(bf16[192,256]{1,0:T(8,128)(2,1)S(1)} %get-tuple-element.93), channel_id=1, source_target_pairs={{0,2},{1,3},{2,0},{3,1},{4,6},{5,7},{6,4},{7,5},{8,10},{9,11},{10,... | collective-permute-start | bytes 294920 | tf_op jit(solution)/shard_map/ppermute | solution.py:62
  88.8 5.5 %collective-permute-start.15 = (bf16[192,256]{1,0:T(8,128)(2,1)S(1)}, bf16[192,256]{1,0:T(8,128)(2,1)S(1)}, u32[]{:S(2)}, u32[]{:S(2)}) collective-permute-start(bf16[192,256]{1,0:T(8,128)(2,1)S(1)} %get-tuple-element.94), channel_id=1, source_target_pairs={{0,3},{1,2},{2,1},{3,0},{4,7},{5,6},{6,5},{7,4},{8,11},{9,10},{10,... | collective-permute-start | bytes 294920 | tf_op jit(solution)/shard_map/ppermute | solution.py:62
  89.4 8.6 %copy-start.19 = (bf16[192,256]{1,0:T(8,128)(2,1)}, bf16[192,256]{1,0:T(8,128)(2,1)S(1)}, u32[]{:S(2)}) copy-start(bf16[192,256]{1,0:T(8,128)(2,1)S(1)} %collective-permute-done.13.g1) | copy-start | bytes 294916
  93.4 4.7 %copy-start.22 = (bf16[192,256]{1,0:T(8,128)(2,1)}, bf16[192,256]{1,0:T(8,128)(2,1)S(1)}, u32[]{:S(2)}) copy-start(bf16[192,256]{1,0:T(8,128)(2,1)S(1)} %collective-permute-done.14.g2) | copy-start | bytes 294916
  94.3 3.8 %copy-start.25 = (bf16[192,256]{1,0:T(8,128)(2,1)}, bf16[192,256]{1,0:T(8,128)(2,1)S(1)}, u32[]{:S(2)}) copy-start(bf16[192,256]{1,0:T(8,128)(2,1)S(1)} %collective-permute-done.15.g3) | copy-start | bytes 294916
  99.0 27.2 %collective-permute-start.16 = (bf16[2,192,1024]{2,1,0:T(8,128)(2,1)}, bf16[2,192,1024]{2,1,0:T(8,128)(2,1)}, u32[]{:S(2)}, u32[]{:S(2)}) collective-permute-start(bf16[2,192,1024]{2,1,0:T(8,128)(2,1)} %get-tuple-element.98), channel_id=1, source_target_pairs={{0,4},{4,0},{8,12},{12,8},{16,20},{20,16},{24,28},{28,24},{1,5},{5... | collective-permute-start | bytes 2359304 | tf_op jit(solution)/shard_map/ppermute | solution.py:45
  102.5 24.6 %collective-permute-start.17 = (f32[48,256]{1,0:T(8,128)}, f32[48,256]{1,0:T(8,128)S(1)}, u32[]{:S(2)}, u32[]{:S(2)}) collective-permute-start(f32[48,256]{1,0:T(8,128)} %copy-done.44), channel_id=1, source_target_pairs={{0,28},{4,24},{8,20},{12,16},{16,12},{20,8},{24,4},{28,0},{1,29},{... | collective-permute-start | bytes 147464 | tf_op jit(solution)/shard_map/ppermute | solution.py:58
  112.7 1.0 copy-start.4
  125.9 1.3 copy-start.42
  125.9 13.1 %copy-start.5 = (bf16[192,1024]{1,0:T(8,128)(2,1)S(1)}, bf16[192,1024]{1,0:T(8,128)(2,1)}, u32[]{:S(2)}) copy-start(bf16[192,1024]{1,0:T(8,128)(2,1)} %q_ref.17) | copy-start | bytes 1179652
  125.9 13.1 %copy-start.18 = (bf16[192,256]{1,0:T(8,128)(2,1)S(1)}, bf16[192,256]{1,0:T(8,128)(2,1)}, u32[]{:S(2)}) copy-start(bf16[192,256]{1,0:T(8,128)(2,1)} %copy-done.16) | copy-start | bytes 294916
  125.9 13.1 %copy-start.21 = (bf16[192,256]{1,0:T(8,128)(2,1)S(1)}, bf16[192,256]{1,0:T(8,128)(2,1)}, u32[]{:S(2)}) copy-start(bf16[192,256]{1,0:T(8,128)(2,1)} %copy-done.19) | copy-start | bytes 294916
  125.9 13.1 %copy-start.24 = (bf16[192,256]{1,0:T(8,128)(2,1)S(1)}, bf16[192,256]{1,0:T(8,128)(2,1)}, u32[]{:S(2)}) copy-start(bf16[192,256]{1,0:T(8,128)(2,1)} %copy-done.22) | copy-start | bytes 294916
  125.9 13.1 %copy-start.27 = (bf16[192,256]{1,0:T(8,128)(2,1)S(1)}, bf16[192,256]{1,0:T(8,128)(2,1)}, u32[]{:S(2)}) copy-start(bf16[192,256]{1,0:T(8,128)(2,1)} %copy-done.25) | copy-start | bytes 294916
  125.9 13.1 %copy-start.31 = (s32[2]{0:T(128)S(1)}, s32[2]{0:T(128)}, u32[]{:S(2)}) copy-start(s32[2]{0:T(128)} %copy-done.28) | copy-start | bytes 28
  125.9 13.1 %copy-start.35 = (s32[4,16]{1,0:T(4,128)S(1)}, s32[4,16]{1,0:T(4,128)}, u32[]{:S(2)}) copy-start(s32[4,16]{1,0:T(4,128)} %lists_ref.17) | copy-start | bytes 772
  126.0 13.1 %copy-start.40 = (s32[4]{0:T(128)S(1)}, s32[4]{0:T(128)}, u32[]{:S(2)}) copy-start(s32[4]{0:T(128)} %counts_ref.17) | copy-start | bytes 52
  126.0 19.9 %collective-permute-start.18 = (bf16[2,192,1024]{2,1,0:T(8,128)(2,1)}, bf16[2,192,1024]{2,1,0:T(8,128)(2,1)}, u32[]{:S(2)}, u32[]{:S(2)}) collective-permute-start(bf16[2,192,1024]{2,1,0:T(8,128)(2,1)} %get-tuple-element.104), channel_id=1, source_target_pairs={{0,4},{4,0},{8,12},{12,8},{16,20},{20,16},{24,28},{28,24},{1,5},{5... | collective-permute-start | bytes 2359304 | tf_op jit(solution)/shard_map/ppermute | solution.py:45
  127.8 27.2 %collective-permute-start.19 = (bf16[2,192,1024]{2,1,0:T(8,128)(2,1)}, bf16[2,192,1024]{2,1,0:T(8,128)(2,1)}, u32[]{:S(2)}, u32[]{:S(2)}) collective-permute-start(bf16[2,192,1024]{2,1,0:T(8,128)(2,1)} %select_add_fusion), channel_id=1, source_target_pairs={{8,0},{12,4},{16,8},{20,12},{24,16},{28,20},{9,1},{13,5},{17,9},{2... | collective-permute-start | bytes 2359304 | tf_op jit(solution)/shard_map/ppermute | solution.py:41
  137.1 20.2 %collective-permute-start.22 = (f32[48,256]{1,0:T(8,128)}, f32[48,256]{1,0:T(8,128)S(1)}, u32[]{:S(2)}, u32[]{:S(2)}) collective-permute-start(f32[48,256]{1,0:T(8,128)} %shard_map.157.p0), channel_id=1, source_target_pairs={{0,3},{1,2},{2,1},{3,0},{4,7},{5,6},{6,5},{7,4},{8,11},{9,10},{10,... | collective-permute-start | bytes 147464 | tf_op jit(solution)/shard_map/ppermute | solution.py:62
  137.1 20.2 %collective-permute-start.21 = (f32[48,256]{1,0:T(8,128)}, f32[48,256]{1,0:T(8,128)S(1)}, u32[]{:S(2)}, u32[]{:S(2)}) collective-permute-start(f32[48,256]{1,0:T(8,128)} %shard_map.157.p0), channel_id=1, source_target_pairs={{0,2},{1,3},{2,0},{3,1},{4,6},{5,7},{6,4},{7,5},{8,10},{9,11},{10,... | collective-permute-start | bytes 147464 | tf_op jit(solution)/shard_map/ppermute | solution.py:62
  137.9 19.5 %collective-permute-start.20 = (f32[48,256]{1,0:T(8,128)}, f32[48,256]{1,0:T(8,128)S(1)}, u32[]{:S(2)}, u32[]{:S(2)}) collective-permute-start(f32[48,256]{1,0:T(8,128)} %shard_map.157.p0), channel_id=1, source_target_pairs={{0,1},{1,0},{2,3},{3,2},{4,5},{5,4},{6,7},{7,6},{8,9},{9,8},{10,11... | collective-permute-start | bytes 147464 | tf_op jit(solution)/shard_map/ppermute | solution.py:62
  139.1 1.1 copy-start.43
  154.9 4.4 %copy-start.36 = (s32[4,16]{1,0:T(4,128)S(1)}, s32[4,16]{1,0:T(4,128)}, u32[]{:S(2)}) copy-start(s32[4,16]{1,0:T(4,128)} %lists_ref.17) | copy-start | bytes 772
  154.9 4.4 %copy-start.41 = (s32[4]{0:T(128)S(1)}, s32[4]{0:T(128)}, u32[]{:S(2)}) copy-start(s32[4]{0:T(128)} %counts_ref.17) | copy-start | bytes 52
  157.4 7.1 %copy-start.53 = (f32[48,256]{1,0:T(8,128)}, f32[48,256]{1,0:T(8,128)S(1)}, u32[]{:S(2)}) copy-start(f32[48,256]{1,0:T(8,128)S(1)} %collective-permute-done.22.p3) | copy-start | bytes 147460
  157.4 7.1 %copy-start.54 = (f32[48,256]{1,0:T(8,128)}, f32[48,256]{1,0:T(8,128)S(1)}, u32[]{:S(2)}) copy-start(f32[48,256]{1,0:T(8,128)S(1)} %collective-permute-done.21.p2) | copy-start | bytes 147460
  157.4 7.0 %copy-start.55 = (f32[48,256]{1,0:T(8,128)}, f32[48,256]{1,0:T(8,128)S(1)}, u32[]{:S(2)}) copy-start(f32[48,256]{1,0:T(8,128)S(1)} %collective-permute-done.20.p1) | copy-start | bytes 147460
  157.4 21.3 %collective-permute-start.23 = (bf16[2,192,1024]{2,1,0:T(8,128)(2,1)}, bf16[2,192,1024]{2,1,0:T(8,128)(2,1)}, u32[]{:S(2)}, u32[]{:S(2)}) collective-permute-start(bf16[2,192,1024]{2,1,0:T(8,128)(2,1)} %add_add_fusion), channel_id=1, source_target_pairs={{8,0},{12,4},{16,8},{20,12},{24,16},{28,20},{9,1},{13,5},{17,9},{2... | collective-permute-start | bytes 2359304 | tf_op jit(solution)/shard_map/ppermute | solution.py:41
  (18 other events, 13.7 us)

commit v4 on v3

--- a/solution.py
+++ b/solution.py
@@ -113,8 +113,30 @@
     )(place, *pieces)
 
 
-def live_items(lists_ref, counts_ref, place_ref, regions, blocks, first, items_ref, together):
-    row = place_ref[0]
+class Table:
+    def __init__(self, ref, blocks):
+        self.ref, self.blocks = ref, blocks
+
+    def entry(self, b, j):
+        return self.ref[b * LIST + j]
+
+    def count(self, b):
+        return self.ref[self.blocks * LIST + b]
+
+    def row(self):
+        return self.ref[self.blocks * (LIST + 1)]
+
+    def col(self):
+        return self.ref[self.blocks * (LIST + 1) + 1]
+
+
+def packed(lists, counts, place):
+    flat = jnp.concatenate([lists.reshape(-1), counts, place])
+    return jnp.pad(flat, (0, -flat.shape[0] % 128))
+
+
+def live_items(table, regions, blocks, first, items_ref, together):
+    row = table.row()
     odd = lax.rem(row, 2)
     slots = len(regions) * blocks
     wanted = [jnp.where(odd == 1, region[1], region[0]) for region in regions]
@@ -123,7 +145,7 @@
     for b in range(blocks):
 
         def look(j, count, b=b):
-            block = lists_ref[b, j]
+            block = table.entry(b, j)
             distance = row - lax.div(block, blocks)
             slot, hit = b * slots, 0
             for r, want in enumerate(wanted):
@@ -134,13 +156,12 @@
             return count + hit
 
         start = total if together else b * LIST
-        total = lax.fori_loop(first, counts_ref[b], look, start)
+        total = lax.fori_loop(first, table.count(b), look, start)
         found.append(total - start)
     return total if together else found
 
 
-def staged(place_ref, regions, refs, raw, sems, act):
-    odd = lax.rem(place_ref[0], 2)
+def staged(parity_at, regions, refs, raw, sems, act):
     at = 0
     for r, region in enumerate(regions):
         if region[2] == "both":
@@ -150,12 +171,24 @@
         for parity in (0, 1):
             if region[parity] >= 0:
                 copy = pltpu.make_async_copy(refs[at], raw.at[r], sems.at[r])
-                pl.when(odd == parity)(lambda r=r, copy=copy: act(r, copy))
+                pl.when(parity_at() == parity)(lambda r=r, copy=copy: act(r, copy))
                 at += 1
 
 
 def begin(r, copy):
     copy.start()
+
+
+def started(pairs, sems):
+    copies = [pltpu.make_async_copy(a, b, sems.at[i]) for i, (a, b) in enumerate(pairs)]
+    for copy in copies:
+        copy.start()
+    return copies
+
+
+def finished(copies):
+    for copy in copies:
+        copy.wait()
 
 
 def region_inputs(regions):
@@ -172,33 +205,28 @@
     return slice(h * HEAD_DIM, (h + 1) * HEAD_DIM)
 
 
-def forward_kernel(regions, opening, closing, lists_ref, counts_ref, place_ref, q_ref, *refs):
+def forward_kernel(regions, opening, closing, table_ref, q_ref, *refs):
     heads = q_ref.shape[0] // HEAD_DIM
     blocks = q_ref.shape[1] // BLOCK
     slots = len(regions) * blocks
     refs = list(refs)
     slabs = [refs.pop(0) for _ in range(region_inputs(regions))]
-    if not opening:
-        acc_in, stat_in = refs.pop(0), refs.pop(0)
-    if closing:
-        att_ref, lse_ref = refs.pop(0), refs.pop(0)
-    else:
-        acc_out, stat_out = refs.pop(0), refs.pop(0)
-    (key_rows, value_cols, scaled, items, found_ref, acc_ref, stat_ref, raw, q_vmem, sems,
-     q_sem) = refs
-    if not closing:
-        acc_ref, stat_ref = acc_out, stat_out
-
-    q_copy = pltpu.make_async_copy(q_ref, q_vmem, q_sem)
-    q_copy.start()
-    staged(place_ref, regions, slabs, raw, sems, begin)
-    for b, found in enumerate(live_items(
-            lists_ref, counts_ref, place_ref, regions, blocks, int(opening), items, False)):
+    given = [] if opening else [refs.pop(0), refs.pop(0)]
+    outs = [refs.pop(0), refs.pop(0)]
+    (key_rows, value_cols, scaled, items, found_ref, acc_ref, stat_ref, raw, q_vmem, table_smem,
+     att_ref, lse_ref, sems, in_sems, out_sems) = refs
+    table = Table(table_smem, blocks)
+    copies = started([(table_ref, table_smem), (q_ref, q_vmem)]
+                     + list(zip(given, (acc_ref, stat_ref))), in_sems)
+    copies[0].wait()
+
+    def parity():
+        return lax.rem(table.row(), 2)
+
+    staged(parity, regions, slabs, raw, sems, begin)
+    for b, found in enumerate(live_items(table, regions, blocks, int(opening), items, False)):
         found_ref[b] = found
-    if not opening:
-        acc_ref[...] = acc_in[...]
-        stat_ref[...] = stat_in[...]
-    q_copy.wait()
+    finished(copies[1:])
     for b in range(blocks):
         scaled[b] = q_vmem[:, b * BLOCK:(b + 1) * BLOCK] * BF16(SCALE)
 
@@ -210,7 +238,7 @@
             for h in range(heads):
                 key_rows[slot, h] = raw[r, 0, head_rows(h), cols].T
 
-    staged(place_ref, regions, slabs, raw, sems, spread)
+    staged(parity, regions, slabs, raw, sems, spread)
 
     def entries(b, chosen, masked=False):
         scores = [[dot(key_rows[slot, h], scaled[b, head_rows(h)]) for slot in chosen]
@@ -228,17 +256,18 @@
             if masked:
                 newest, total, acc = peak, 0.0, 0.0
             else:
-                newest = jnp.maximum(stat_ref[b, 2 * h], peak)
-                fade = jnp.exp(stat_ref[b, 2 * h] - newest)
-                total = stat_ref[b, 2 * h + 1] * fade
+                top = stat_ref[b, 2 * h:2 * h + 1]
+                newest = jnp.maximum(top, peak)
+                fade = jnp.exp(top - newest)
+                total = stat_ref[b, 2 * h + 1:2 * h + 2] * fade
                 acc = acc_ref[b, rows] * fade
             for slot, tile in zip(chosen, tiles):
                 weights = jnp.exp(tile - newest)
                 total = total + jnp.sum(weights, axis=0, keepdims=True)
                 acc = acc + dot(value_cols[slot, rows], weights.astype(BF16))
             acc_ref[b, rows] = acc
-            stat_ref[b, 2 * h] = newest
-            stat_ref[b, 2 * h + 1] = total
+            stat_ref[b, 2 * h:2 * h + 1] = newest
+            stat_ref[b, 2 * h + 1:2 * h + 2] = total
 
     def one_block(b, carry):
         found = found_ref[b]
@@ -258,47 +287,56 @@
 
         return carry
 
+    if opening:
+        stat_ref[...] = jnp.zeros_like(stat_ref)
     lax.fori_loop(0, blocks, one_block, 0)
-    if closing:
-        for b in range(blocks):
-            cols = slice(b * BLOCK, (b + 1) * BLOCK)
-            for h in range(heads):
-                top, total = stat_ref[b, 2 * h], stat_ref[b, 2 * h + 1]
-                att_ref[head_rows(h), cols] = (acc_ref[b, head_rows(h)] / total).astype(BF16)
-                lse_ref[b, h] = top + jnp.log(total)
+    if not closing:
+        finished(started(list(zip((acc_ref, stat_ref), outs)), out_sems))
+        return
+    lse_ref[...] = jnp.zeros_like(lse_ref)
+    for b in range(blocks):
+        cols = slice(b * BLOCK, (b + 1) * BLOCK)
+        for h in range(heads):
+            top, total = stat_ref[b, 2 * h:2 * h + 1], stat_ref[b, 2 * h + 1:2 * h + 2]
+            att_ref[head_rows(h), cols] = (acc_ref[b, head_rows(h)] / total).astype(BF16)
+            lse_ref[b, h:h + 1] = top + jnp.log(total)
+    finished(started(list(zip((att_ref, lse_ref), outs)), out_sems))
 
 
 def forward(tables, queries, regions, slabs, state=None, closing=False, pairs=1):
     width, tokens = queries.shape
     heads, blocks = width // HEAD_DIM, tokens // BLOCK
     slots = len(regions) * blocks
-    acc, stat = (blocks, width, BLOCK), (blocks, 2 * heads, 1, BLOCK)
-    result = (jax.ShapeDtypeStruct((width, tokens), BF16),
-              jax.ShapeDtypeStruct((blocks, heads, 1, BLOCK), F32))
+    acc, stat = (blocks, width, BLOCK), (blocks, 8, BLOCK)
+    result = (jax.ShapeDtypeStruct((width, tokens), BF16), jax.ShapeDtypeStruct(stat, F32))
     state = () if state is None else state
     return pl.pallas_call(
         functools.partial(forward_kernel, regions, not state, closing),
         out_shape=result if closing else tuple(
             jax.ShapeDtypeStruct(shape, F32) for shape in (acc, stat)),
-        in_specs=smem(3) + anywhere(1 + len(slabs)) + vmem(len(state)),
-        out_specs=tuple(vmem(2)),
+        in_specs=anywhere(2 + len(slabs) + len(state)),
+        out_specs=tuple(anywhere(2)),
         scratch_shapes=[
             pltpu.VMEM((slots, heads, BLOCK, HEAD_DIM), BF16),
             pltpu.VMEM((slots, width, BLOCK), BF16),
             pltpu.VMEM((blocks, width, BLOCK), BF16),
             pltpu.SMEM((blocks * LIST,), jnp.int32),
             pltpu.SMEM((blocks,), jnp.int32),
-            pltpu.VMEM(acc if closing else (8, BLOCK), F32),
-            pltpu.VMEM(stat if closing else (8, BLOCK), F32),
+            pltpu.VMEM(acc, F32),
+            pltpu.VMEM(stat, F32),
             pltpu.VMEM((len(regions), 2, width, tokens), BF16),
             pltpu.VMEM((width, tokens), BF16),
+            pltpu.SMEM(tables.shape, jnp.int32),
+            pltpu.VMEM((width, tokens), BF16),
+            pltpu.VMEM(stat, F32),
             pltpu.SemaphoreType.DMA((len(regions),)),
-            pltpu.SemaphoreType.DMA,
+            pltpu.SemaphoreType.DMA((4,)),
+            pltpu.SemaphoreType.DMA((2,)),
         ],
         compiler_params=pltpu.CompilerParams(vmem_limit_bytes=48 << 20),
         cost_estimate=pl.CostEstimate(
             flops=pairs * 10 ** 9, bytes_accessed=6 << 20, transcendentals=pairs * 10 ** 5),
-    )(*tables, queries, *slabs, *state)
+    )(tables, queries, *slabs, *state)
 
 
 def flow_kernel(place_ref, a0, a1, a2, a3, w0, w1, w2, w3, stream_ref, gain_ref, head_ref,
@@ -343,33 +381,39 @@
     )(place, *parts, *weights, stream, gain, head_proj, patches, grad)
 
 
-def backward_kernel(regions, diagonal, last, lists_ref, counts_ref, place_ref, q_ref, att_ref,
-                    lse_ref, g0, g1, g2, g3, *refs):
+def backward_kernel(regions, diagonal, last, first, table_ref, q_ref, att_ref, lse_any,
+                    g0, g1, g2, g3, *refs):
     heads = q_ref.shape[0] // HEAD_DIM
     blocks = q_ref.shape[1] // BLOCK
     slots = len(regions) * blocks
     refs = list(refs)
     slabs = [refs.pop(0) for _ in range(region_inputs(regions))]
-    dq_in = None if len(refs) < 17 + len(regions) else refs.pop(0)
-    dq_ref = refs.pop(0)
+    dq_in = None if first else refs.pop(0)
+    dq_out = refs.pop(0)
     outs = [refs.pop(0) for _ in regions]
     (key_rows, value_rows, key_cols, grad_cols, scaled, sums, grad_keys, grad_values, items,
-     acc_ref, raw, q_vmem, att_vmem, sems, more_sems) = refs
-    q_copy = pltpu.make_async_copy(q_ref, q_vmem, more_sems.at[0])
-    att_copy = pltpu.make_async_copy(att_ref, att_vmem, more_sems.at[1])
-    q_copy.start()
-    att_copy.start()
-    staged(place_ref, regions, slabs, raw, sems, begin)
-    me = place_ref[1]
+     acc_ref, raw, q_vmem, att_vmem, lse_ref, table_smem, dq_vmem, leaving, sems, in_sems,
+     out_sems) = refs
+    table = Table(table_smem, blocks)
+    copies = started([(table_ref, table_smem), (q_ref, q_vmem), (att_ref, att_vmem),
+                      (lse_any, lse_ref)] + ([] if first else [(dq_in, acc_ref)]), in_sems)
+    copies[0].wait()
+    me = table.col()
     for k, ref in enumerate((g0, g1, g2, g3)):
-        grad_cols[jnp.bitwise_xor(me, k)] = ref[...]
+        copies.append(pltpu.make_async_copy(
+            ref, grad_cols.at[jnp.bitwise_xor(me, k)], in_sems.at[5 + k]))
+        copies[-1].start()
+
+    def parity():
+        return lax.rem(table.row(), 2)
+
+    staged(parity, regions, slabs, raw, sems, begin)
     grad_keys[...] = jnp.zeros_like(grad_keys)
     grad_values[...] = jnp.zeros_like(grad_values)
-    found = live_items(
-        lists_ref, counts_ref, place_ref, regions, blocks, int(diagonal), items, True)
-    acc_ref[...] = jnp.zeros_like(acc_ref) if dq_in is None else dq_in[...]
-    q_copy.wait()
-    att_copy.wait()
+    if first:
+        acc_ref[...] = jnp.zeros_like(acc_ref)
+    found = live_items(table, regions, blocks, int(diagonal), items, True)
+    finished(copies[1:])
     for b in range(blocks):
         cols = slice(b * BLOCK, (b + 1) * BLOCK)
         scaled[b] = q_vmem[:, cols] * BF16(SCALE)
@@ -388,7 +432,7 @@
                 key_rows[slot, h] = raw[r, 0, head_rows(h), cols].T
                 value_rows[slot, h] = raw[r, 1, head_rows(h), cols].T
 
-    staged(place_ref, regions, slabs, raw, sems, spread)
+    staged(parity, regions, slabs, raw, sems, spread)
 
     def entries(chosen, masked=False):
         tiles = [(b, slot, h, head_rows(h)) for b, slot in chosen for h in range(heads)]
@@ -397,7 +441,7 @@
             keep = causal()
             scores = [jnp.where(keep, tile, NEG) for tile in scores]
         grads = [dot(value_rows[slot, h], grad_cols[b, rows]) for b, slot, h, rows in tiles]
-        probs = [jnp.exp(tile - lse_ref[b, h]) for tile, (b, _, h, _) in zip(scores, tiles)]
+        probs = [jnp.exp(tile - lse_ref[b, h:h + 1]) for tile, (b, _, h, _) in zip(scores, tiles)]
         grads = [(p * (g - sums[b, h])).astype(BF16)
                  for p, g, (b, _, h, _) in zip(probs, grads, tiles)]
         probs = [p.astype(BF16) for p in probs]
@@ -425,14 +469,16 @@
 
     if last:
         for b in range(blocks):
-            dq_ref[:, b * BLOCK:(b + 1) * BLOCK] = (acc_ref[b] * SCALE).astype(BF16)
-    else:
-        dq_ref[...] = acc_ref[...]
+            dq_vmem[:, b * BLOCK:(b + 1) * BLOCK] = (acc_ref[b] * SCALE).astype(BF16)
+    going = started([(dq_vmem if last else acc_ref, dq_out)], out_sems)
     for r, ref in enumerate(outs):
         for b in range(blocks):
             cols = slice(b * BLOCK, (b + 1) * BLOCK)
-            ref[0, :, cols] = grad_keys[r * blocks + b].astype(ref.dtype)
-            ref[1, :, cols] = grad_values[r * blocks + b].astype(ref.dtype)
+            leaving[r, 0, :, cols] = grad_keys[r * blocks + b].astype(ref.dtype)
+            leaving[r, 1, :, cols] = grad_values[r * blocks + b].astype(ref.dtype)
+        going.append(pltpu.make_async_copy(leaving.at[r], ref, out_sems.at[1 + r]))
+        going[-1].start()
+    finished(going)
 
 
 def backward(tables, queries, attended, lse, grads, regions, slabs, dq=None, last=False, pairs=1):
@@ -442,12 +488,12 @@
     diagonal = regions[0][0] == 0
     given = () if dq is None else (dq,)
     return pl.pallas_call(
-        functools.partial(backward_kernel, regions, diagonal, last),
+        functools.partial(backward_kernel, regions, diagonal, last, dq is None),
         out_shape=(jax.ShapeDtypeStruct((width, tokens), BF16) if last else
                    jax.ShapeDtypeStruct((blocks, width, BLOCK), F32),)
         + (jax.ShapeDtypeStruct((2, width, tokens), F32 if diagonal else BF16),) * len(regions),
-        in_specs=smem(3) + anywhere(2) + vmem(5) + anywhere(len(slabs)) + vmem(len(given)),
-        out_specs=tuple(vmem(1 + len(regions))),
+        in_specs=anywhere(8 + len(slabs) + len(given)),
+        out_specs=tuple(anywhere(1 + len(regions))),
         scratch_shapes=[
             pltpu.VMEM((slots, heads, BLOCK, HEAD_DIM), BF16),
             pltpu.VMEM((slots, heads, BLOCK, HEAD_DIM), BF16),
@@ -462,13 +508,18 @@
             pltpu.VMEM((len(regions), 2, width, tokens), BF16),
             pltpu.VMEM((width, tokens), BF16),
             pltpu.VMEM((width, tokens), BF16),
+            pltpu.VMEM((blocks, 8, BLOCK), F32),
+            pltpu.SMEM(tables.shape, jnp.int32),
+            pltpu.VMEM((width, tokens), BF16),
+            pltpu.VMEM((len(regions), 2, width, tokens), F32 if diagonal else BF16),
             pltpu.SemaphoreType.DMA((len(regions),)),
-            pltpu.SemaphoreType.DMA((2,)),
+            pltpu.SemaphoreType.DMA((9,)),
+            pltpu.SemaphoreType.DMA((3,)),
         ],
         compiler_params=pltpu.CompilerParams(vmem_limit_bytes=48 << 20),
         cost_estimate=pl.CostEstimate(
             flops=pairs * 10 ** 9, bytes_accessed=8 << 20, transcendentals=pairs * 10 ** 5),
-    )(*tables, queries, attended, lse, *grads, *slabs, *given)
+    )(tables, queries, attended, lse, *grads, *slabs, *given)
 
 
 def on_device(queries, key_rows, values, block_lists, counts, out_proj, stream, norm_gain,
@@ -479,29 +530,26 @@
     odd = row % 2 == 1
     place = jnp.stack([row, col]).astype(jnp.int32)
 
-    tables = (block_lists, counts, place)
+    tables = packed(block_lists, counts, place)
     tie = lax.optimization_barrier
     own = jnp.stack([key_rows, values])
     slab2 = hop(own, 2)
     state = forward(tables, queries, [(0, 0, "both")], [own])
-    *state, out_proj, own_again = tie([*state, out_proj, own])
-    order = token_order.reshape(1, tokens)
-    landed = permuted(scatter_kernel, place, order, cotangent.T)
-    weights = [across(out_proj, k) for k in range(1, cols)]
-    up1 = upward(own_again)
-    *state, slab2, landed, out_proj, w1, w2, w3 = tie(
-        [*state, slab2, landed, out_proj, *weights])
-    weights = [out_proj, w1, w2, w3]
+    *state, slab2 = tie([*state, slab2])
     slab4 = hop(slab2, 2)
+    up1 = upward(own)
     down1 = downward(slab2)
     up2 = upward(slab2)
     state = forward(tables, queries, [(2, 2, "both")], [slab2], tuple(state))
-    *state, slab4, landed = tie([*state, slab4, landed])
+    *state, slab4, cotangent, out_proj = tie([*state, slab4, cotangent, out_proj])
     down2 = downward(slab4)
-    grad_latent = mirror(landed)
+    order = token_order.reshape(1, tokens)
+    grad_latent = mirror(permuted(scatter_kernel, place, order, cotangent.T))
+    weights = [across(out_proj, k) for k in range(1, cols)]
     state = forward(tables, queries, [(1, 1, "each")], [down1, up1], tuple(state))
     state = forward(tables, queries, [(4, 4, "both"), (-1, 3, "one")], [slab4, up2], state)
-    *state, grad_latent = tie([*state, grad_latent])
+    *state, grad_latent, out_proj, w1, w2, w3 = tie([*state, grad_latent, out_proj, *weights])
+    weights = [out_proj, w1, w2, w3]
     attended, lse = forward(tables, queries, [(3, -1, "one")], [down2], tuple(state), True)
 
     def block_of(array, b):

time: 185 us -> 182 us (0.984)
  the two profiles are of different devices: /device:TPU:8 before, /device:TPU:0 now
where the time goes in v4:
time: 182 us; the launch traced here: 179 us
  waiting for transfers between devices  59.5 us (33%)
  starting transfers between devices  56.8 us (31%)
  Pallas kernels  40.8 us (22%)
  local copies, waits for them, and re-layouts  13.3 us (7%)
  other arithmetic  7.05 us (4%)
    ppermute x4, waiting for transfers between devices, hop(): return lax.ppermute(array, 'row', pairs)  29.2 us
    pallas_call x4, Pallas kernels, backward(): pl.pallas_call(functools.partial(backward_kernel, regions, diagonal, last...  19.6 us
    ppermute x2, starting transfers between devices, mirror(): return lax.ppermute(array, 'row', [(i, size - 1 - i) for i in range(size)])  14.3 us
    pallas_call x5, Pallas kernels, forward(): pl.pallas_call(functools.partial(forward_kernel, regions, not state, clos...  13.1 us
    ppermute x4, starting transfers between devices, hop(): return lax.ppermute(array, 'row', pairs)  13 us
    unnamed x80, local copies, waits for them, and re-layouts  12.2 us
    ppermute x2, starting transfers between devices, mate(): lax.ppermute(array, 'row', [(i, i ^ 1) for i in range(lax.axis_size('row'...  10.7 us
    ppermute x12, waiting for transfers between devices, across(): lax.ppermute(array, 'col', [(i, i ^ bits) for i in range(lax.axis_size('c...  10.3 us
  transfers between devices with their start and end apart: 24, of which 13 were waited for; matrix products, arithmetic and copies ran while one was open for 2% of the time, Pallas kernels for 18%

profile of v4, /device:TPU:0, one launch (start us, length us, event | category | flops | bytes accessed | tf_op | source)
XLA Modules:
  0.0 178.6 jit_solution(4386617854324186377)
XLA Ops:
  0.7 1.2 pad_maximum_fusion.refs_0_
  1.9 5.9 %collective-permute-start = (bf16[2,192,1024]{2,1,0:T(8,128)(2,1)S(1)}, bf16[2,192,1024]{2,1,0:T(8,128)(2,1)}, u32[]{:S(2)}, u32[]{:S(2)}) collective-permute-start(bf16[2,192,1024]{2,1,0:T(8,128)(2,1)S(1)} %pad_maximum_fusion.refs_0_), channel_id=1, source_target_pairs={{0,8},{4,12},{8,16},{12,20},{16,24},{20,28},{1,9},{5,13},{9,17},{1... | collective-permute-start | bytes 2359304 | tf_op jit(solution)/shard_map/ppermute | solution.py:41
  7.9 5.7 %shard_map.147 = (f32[4,192,256]{2,1,0:T(8,128)S(1)}, f32[4,8,256]{2,1,0:T(8,128)S(1)}) custom-call(s32[128]{0:T(128)S(1)} %pad.4.table_ref, bf16[192,1024]{1,0:T(8,128)(2,1)S(1)} %copy-done.2, bf16[2,192,1024]{2,1,0:T(8,128)(2,1)S(1)} %pad_maximum_fusion.refs_0_), custom_call_target="tpu_custom_call" | custom-call | flops 1000000000 | bytes 6291456 | tf_op jit(solution)/shard_map/pallas_call | solution.py:313
  13.7 9.9 %collective-permute-done.refs_0_ = bf16[2,192,1024]{2,1,0:T(8,128)(2,1)} collective-permute-done((bf16[2,192,1024]{2,1,0:T(8,128)(2,1)S(1)}, bf16[2,192,1024]{2,1,0:T(8,128)(2,1)}, u32[]{:S(2)}, u32[]{:S(2)}) %collective-permute-start) | collective-permute-done | bytes 786464 | tf_op jit(solution)/shard_map/ppermute | solution.py:41
  23.6 4.5 %collective-permute-start.1 = (bf16[2,192,1024]{2,1,0:T(8,128)(2,1)}, bf16[2,192,1024]{2,1,0:T(8,128)(2,1)S(1)}, u32[]{:S(2)}, u32[]{:S(2)}) collective-permute-start(bf16[2,192,1024]{2,1,0:T(8,128)(2,1)} %collective-permute-done.refs_0_), channel_id=1, source_target_pairs={{0,8},{4,12},{8,16},{12,20},{16,24},{20,28},{1,9},{5,13},{9,17},{1... | collective-permute-start | bytes 2359304 | tf_op jit(solution)/shard_map/ppermute | solution.py:41
  28.2 3.5 %collective-permute-start.5 = (bf16[2,192,1024]{2,1,0:T(8,128)(2,1)S(1)}, bf16[2,192,1024]{2,1,0:T(8,128)(2,1)S(1)}, u32[]{:S(2)}, u32[]{:S(2)}) collective-permute-start(bf16[2,192,1024]{2,1,0:T(8,128)(2,1)S(1)} %pad_maximum_fusion.refs_0_), channel_id=1, source_target_pairs={{0,4},{8,12},{16,20},{24,28},{1,5},{9,13},{17,21},{25,29},{2,6},{1... | collective-permute-start | bytes 2359304 | tf_op jit(solution)/shard_map/ppermute | solution.py:49
  31.6 1.3 collective-permute-start.4
  32.9 5.5 %collective-permute-start.3 = (bf16[2,192,1024]{2,1,0:T(8,128)(2,1)}, bf16[2,192,1024]{2,1,0:T(8,128)(2,1)}, u32[]{:S(2)}, u32[]{:S(2)}) collective-permute-start(bf16[2,192,1024]{2,1,0:T(8,128)(2,1)} %collective-permute-done.refs_0_), channel_id=1, source_target_pairs={{0,4},{8,12},{16,20},{24,28},{1,5},{9,13},{17,21},{25,29},{2,6},{1... | collective-permute-start | bytes 2359304 | tf_op jit(solution)/shard_map/ppermute | solution.py:49
  38.4 2.2 %shard_map.148 = (f32[4,192,256]{2,1,0:T(8,128)S(1)}, f32[4,8,256]{2,1,0:T(8,128)S(1)}) custom-call(s32[128]{0:T(128)S(1)} %pad.4.table_ref, bf16[192,1024]{1,0:T(8,128)(2,1)S(1)} %copy-done.2, bf16[2,192,1024]{2,1,0:T(8,128)(2,1)} %collective-permute-done.refs_0_, f32[4,192,256]{2,1,0:T(8,128)S(1)} %get-tuple-element.61.refs_1_, ...), custom_call_target="tpu_custom_call" | custom-call | flops 1000000000 | bytes 6291456 | tf_op jit(solution)/shard_map/pallas_call | solution.py:313
  40.7 0.9 copy-done.28
  41.6 0.6 copy-done.30
  42.2 2.2 %collective-permute-done.1.refs_0_ = bf16[2,192,1024]{2,1,0:T(8,128)(2,1)S(1)} collective-permute-done((bf16[2,192,1024]{2,1,0:T(8,128)(2,1)}, bf16[2,192,1024]{2,1,0:T(8,128)(2,1)S(1)}, u32[]{:S(2)}, u32[]{:S(2)}) %collective-permute-start.1) | collective-permute-done | bytes 786464 | tf_op jit(solution)/shard_map/ppermute | solution.py:41
  44.3 1.3 collective-permute-start.2
  45.7 3.8 %collective-permute-done.5.refs_1_.refs_2_ = bf16[2,192,1024]{2,1,0:T(8,128)(2,1)S(1)} collective-permute-done((bf16[2,192,1024]{2,1,0:T(8,128)(2,1)S(1)}, bf16[2,192,1024]{2,1,0:T(8,128)(2,1)S(1)}, u32[]{:S(2)}, u32[]{:S(2)}) %collective-permute-start.5) | collective-permute-done | bytes 786464 | tf_op jit(solution)/shard_map/ppermute | solution.py:49
  49.6 1.5 collective-permute-start.8
  51.1 3.2 %collective-permute-done.4.refs_0_.refs_1_ = bf16[2,192,1024]{2,1,0:T(8,128)(2,1)S(1)} collective-permute-done((bf16[2,192,1024]{2,1,0:T(8,128)(2,1)}, bf16[2,192,1024]{2,1,0:T(8,128)(2,1)S(1)}, u32[]{:S(2)}, u32[]{:S(2)}) %collective-permute-start.4) | collective-permute-done | bytes 786464 | tf_op jit(solution)/shard_map/ppermute | solution.py:53
  54.2 0.6 pad_add_fusion.place_ref
  54.8 1.8 %shard_map.151 = f32[48,256]{1,0:T(8,128)} custom-call(s32[2]{0:T(128)} %pad_add_fusion.place_ref, s32[1,1024]{1,0:T(1,128)} %bitcast.17, f32[48,1024]{1,0:T(8,128)} %bitcast.16), custom_call_target="tpu_custom_call" | custom-call | tf_op jit(solution)/shard_map/pallas_call | solution.py:92
  56.7 1.1 copy-done.29
  57.8 0.8 copy-done.31
  58.5 1.3 shard_map.149
  59.9 4.3 %collective-permute-done.3.refs_1_ = bf16[2,192,1024]{2,1,0:T(8,128)(2,1)} collective-permute-done((bf16[2,192,1024]{2,1,0:T(8,128)(2,1)}, bf16[2,192,1024]{2,1,0:T(8,128)(2,1)}, u32[]{:S(2)}, u32[]{:S(2)}) %collective-permute-start.3) | collective-permute-done | bytes 786464 | tf_op jit(solution)/shard_map/ppermute | solution.py:49
  64.2 3.6 %collective-permute-start.6 = (f32[48,256]{1,0:T(8,128)S(1)}, f32[48,256]{1,0:T(8,128)S(1)}, u32[]{:S(2)}, u32[]{:S(2)}) collective-permute-start(f32[48,256]{1,0:T(8,128)S(1)} %copy-done.36), channel_id=1, source_target_pairs={{0,28},{4,24},{8,20},{12,16},{16,12},{20,8},{24,4},{28,0},{1,29},{... | collective-permute-start | bytes 147464 | tf_op jit(solution)/shard_map/ppermute | solution.py:58
  67.7 1.3 shard_map.150
  69.1 2.0 %collective-permute-done.6.grad_ref = f32[48,256]{1,0:T(8,128)S(1)} collective-permute-done((f32[48,256]{1,0:T(8,128)S(1)}, f32[48,256]{1,0:T(8,128)S(1)}, u32[]{:S(2)}, u32[]{:S(2)}) %collective-permute-start.6) | collective-permute-done | bytes 49184 | tf_op jit(solution)/shard_map/ppermute | solution.py:58
  71.2 2.5 %shard_map.152 = (bf16[192,1024]{1,0:T(8,128)(2,1)S(1)}, f32[4,8,256]{2,1,0:T(8,128)S(1)}) custom-call(s32[128]{0:T(128)S(1)} %pad.4.table_ref, bf16[192,1024]{1,0:T(8,128)(2,1)S(1)} %copy-done.3, bf16[2,192,1024]{2,1,0:T(8,128)(2,1)} %collective-permute-done.2.refs_0_, f32[4,192,256]{2,1,0:T(8,128)S(1)} %get-tuple-element.74.refs_1_, ...), custom_call_target="tpu_custom_call" | custom-call | flops 1000000000 | bytes 6291456 | tf_op jit(solution)/shard_map/pallas_call | solution.py:313
  73.8 1.6 collective-permute-start.11
  75.7 3.2 %collective-permute-done.12.a3 = bf16[192,256]{1,0:T(8,128)(2,1)S(1)} collective-permute-done((bf16[192,256]{1,0:T(8,128)(2,1)S(1)}, bf16[192,256]{1,0:T(8,128)(2,1)S(1)}, u32[]{:S(2)}, u32[]{:S(2)}) %collective-permute-start.12) | collective-permute-done | bytes 98336 | tf_op jit(solution)/shard_map/ppermute | solution.py:62
  78.9 2.2 %collective-permute-done.11.a2 = bf16[192,256]{1,0:T(8,128)(2,1)S(1)} collective-permute-done((bf16[192,256]{1,0:T(8,128)(2,1)S(1)}, bf16[192,256]{1,0:T(8,128)(2,1)S(1)}, u32[]{:S(2)}, u32[]{:S(2)}) %collective-permute-start.11) | collective-permute-done | bytes 98336 | tf_op jit(solution)/shard_map/ppermute | solution.py:62
  81.0 3.0 %shard_map.153 = (f32[48,256]{1,0:T(8,128)S(1)}, bf16[192,256]{1,0:T(8,128)(2,1)S(1)}, bf16[192,256]{1,0:T(8,128)(2,1)S(1)}, bf16[192,256]{1,0:T(8,128)(2,1)S(1)}, bf16[192,256]{1,0:T(8,128)(2,1)S(1)}) custom-call(s32[2]{0:T(128)S(1)} %copy-done.24, bf16[192,256]{1,0:T(8,128)(2,1)S(1)} %get-tuple-element.117.a0, ...), custom_call_target="tpu_custom_call" | custom-call | tf_op jit(solution)/shard_map/pallas_call | solution.py:372
  84.6 1.5 collective-permute-start.15
  86.1 3.8 %collective-permute-done.14.g2 = bf16[192,256]{1,0:T(8,128)(2,1)S(1)} collective-permute-done((bf16[192,256]{1,0:T(8,128)(2,1)S(1)}, bf16[192,256]{1,0:T(8,128)(2,1)S(1)}, u32[]{:S(2)}, u32[]{:S(2)}) %collective-permute-start.14) | collective-permute-done | bytes 98336 | tf_op jit(solution)/shard_map/ppermute | solution.py:62
  89.9 1.2 collective-permute-done.15.g3
  91.1 3.9 %shard_map.154 = (f32[4,192,256]{2,1,0:T(8,128)S(1)}, bf16[2,192,1024]{2,1,0:T(8,128)(2,1)}) custom-call(s32[128]{0:T(128)S(1)} %pad.4.table_ref, bf16[192,1024]{1,0:T(8,128)(2,1)S(1)} %copy-done.3, bf16[192,1024]{1,0:T(8,128)(2,1)S(1)} %get-tuple-element.76.att_ref, f32[4,8,256]{2,1,0:T(8,128)S(1)} %get-tuple-element.77.lse_any, ...), custom_call_target="tpu_custom_call" | custom-call | flops 1000000000 | bytes 8388608 | tf_op jit(solution)/shard_map/pallas_call | solution.py:490
  95.0 0.9 copy-done.1
  95.9 1.2 collective-permute-start.16
  97.1 10.8 %collective-permute-start.17 = (f32[48,256]{1,0:T(8,128)}, f32[48,256]{1,0:T(8,128)S(1)}, u32[]{:S(2)}, u32[]{:S(2)}) collective-permute-start(f32[48,256]{1,0:T(8,128)} %copy-done.27), channel_id=1, source_target_pairs={{0,28},{4,24},{8,20},{12,16},{16,12},{20,8},{24,4},{28,0},{1,29},{... | collective-permute-start | bytes 147464 | tf_op jit(solution)/shard_map/ppermute | solution.py:58
  107.9 1.0 copy-done.4
  108.9 0.9 copy-done.10
  109.8 0.9 copy-done.13
  110.7 0.9 copy-done.16
  111.6 0.9 copy-done.19
  112.5 0.8 copy-done.22
  113.2 4.0 %shard_map.155 = (f32[4,192,256]{2,1,0:T(8,128)S(1)}, bf16[2,192,1024]{2,1,0:T(8,128)(2,1)S(1)}, bf16[2,192,1024]{2,1,0:T(8,128)(2,1)}) custom-call(s32[128]{0:T(128)S(1)} %pad.4.table_ref, bf16[192,1024]{1,0:T(8,128)(2,1)S(1)} %copy-done.4, bf16[192,1024]{1,0:T(8,128)(2,1)S(1)} %get-tuple-element.76.att_ref, f32[4,8,256]{2,1,0:T(8,128)S(1)} %copy-done.22, ...), custom_call_target="tpu_custom_call" | custom-call | flops 1000000000 | bytes 8388608 | tf_op jit(solution)/shard_map/pallas_call | solution.py:490
  117.4 9.4 %collective-permute-start.18 = (bf16[2,192,1024]{2,1,0:T(8,128)(2,1)}, bf16[2,192,1024]{2,1,0:T(8,128)(2,1)}, u32[]{:S(2)}, u32[]{:S(2)}) collective-permute-start(bf16[2,192,1024]{2,1,0:T(8,128)(2,1)} %get-tuple-element.96), channel_id=1, source_target_pairs={{0,4},{4,0},{8,12},{12,8},{16,20},{20,16},{24,28},{28,24},{1,5},{5... | collective-permute-start | bytes 2359304 | tf_op jit(solution)/shard_map/ppermute | solution.py:45
  126.8 1.0 select_add_fusion
  127.8 0.6 copy-done.35
  128.4 1.3 collective-permute-start.19
  129.7 1.7 shard_map.157.p0
  131.3 0.5 collective-permute-start.22
  131.9 0.8 collective-permute-start.21
  132.7 0.5 collective-permute-start.20
  133.2 0.7 copy-done.23
  134.0 1.1 copy-done.26
  135.1 3.0 %shard_map.156 = (f32[4,192,256]{2,1,0:T(8,128)S(1)}, bf16[2,192,1024]{2,1,0:T(8,128)(2,1)S(1)}) custom-call(s32[128]{0:T(128)S(1)} %pad.4.table_ref, bf16[192,1024]{1,0:T(8,128)(2,1)S(1)} %copy-done.5, bf16[192,1024]{1,0:T(8,128)(2,1)S(1)} %get-tuple-element.76.att_ref, f32[4,8,256]{2,1,0:T(8,128)S(1)} %copy-done.23, bf16[192,256]{1,0:T(8,128)(2,1)S(1)} %copy-done.11, ...), custom_call_target="tpu_custom_call" | custom-call | flops 1000000000 | bytes 8388608 | tf_op jit(solution)/shard_map/pallas_call | solution.py:490
  138.1 6.7 %collective-permute-done.18 = bf16[2,192,1024]{2,1,0:T(8,128)(2,1)} collective-permute-done((bf16[2,192,1024]{2,1,0:T(8,128)(2,1)}, bf16[2,192,1024]{2,1,0:T(8,128)(2,1)}, u32[]{:S(2)}, u32[]{:S(2)}) %collective-permute-start.18) | collective-permute-done | bytes 786464 | tf_op jit(solution)/shard_map/ppermute | solution.py:45
  144.8 5.3 %collective-permute-done.19 = bf16[2,192,1024]{2,1,0:T(8,128)(2,1)} collective-permute-done((bf16[2,192,1024]{2,1,0:T(8,128)(2,1)}, bf16[2,192,1024]{2,1,0:T(8,128)(2,1)}, u32[]{:S(2)}, u32[]{:S(2)}) %collective-permute-start.19) | collective-permute-done | bytes 786464 | tf_op jit(solution)/shard_map/ppermute | solution.py:41
  150.1 2.4 %add_add_fusion = bf16[2,192,1024]{2,1,0:T(8,128)(2,1)} fusion(bf16[2,192,1024]{2,1,0:T(8,128)(2,1)} %collective-permute-done.19, bf16[2,192,1024]{2,1,0:T(8,128)(2,1)S(1)} %get-tuple-element.95, bf16[2,192,1024]{2,1,0:T(8,128)(2,1)} %collective-permute-done.18, bf16[2,192,1024]{2,1,0:T(8,128)(2,1)} %collective-permute-done.16, pred[]{:T(512)S(6)} %eq.5), kind=kLoop, calls=%fused_computation.2 | loop fusion | flops 1179648 | bytes 3932161 | tf_op jit(solution)/shard_map/add | solution.py:580
  152.6 1.3 collective-permute-start.23
  153.9 8.6 %shard_map.158 = (bf16[192,1024]{1,0:T(8,128)(2,1)}, f32[2,192,1024]{2,1,0:T(8,128)S(1)}) custom-call(s32[128]{0:T(128)S(1)} %pad.4.table_ref, bf16[192,1024]{1,0:T(8,128)(2,1)S(1)} %copy-done.5, bf16[192,1024]{1,0:T(8,128)(2,1)S(1)} %get-tuple-element.76.att_ref, f32[4,8,256]{2,1,0:T(8,128)S(1)} %copy-done.23, bf16[192,256]{1,0:T(8,128)(2,1)S(1)} %copy-done.11, ...), custom_call_target="tpu_custom_call" | custom-call | flops 1000000000 | bytes 8388608 | tf_op jit(solution)/shard_map/pallas_call | solution.py:490
  162.6 1.6 shard_map.159
  164.2 11.7 %collective-permute-done.23 = bf16[2,192,1024]{2,1,0:T(8,128)(2,1)} collective-permute-done((bf16[2,192,1024]{2,1,0:T(8,128)(2,1)}, bf16[2,192,1024]{2,1,0:T(8,128)(2,1)}, u32[]{:S(2)}, u32[]{:S(2)}) %collective-permute-start.23) | collective-permute-done | bytes 786464 | tf_op jit(solution)/shard_map/ppermute | solution.py:41
  175.9 1.7 add_convert_fusion
  177.7 0.9 slice_bitcast_fusion
  (88 shorter events, 1.3 us)
Async XLA Ops:
  0.6 7.1 %copy-start.38 = (s32[4,16]{1,0:T(4,128)S(1)}, s32[4,16]{1,0:T(4,128)}, u32[]{:S(2)}) copy-start(s32[4,16]{1,0:T(4,128)} %param.15) | copy-start | bytes 772
  0.6 7.2 %copy-start.39 = (s32[4]{0:T(128)S(1)}, s32[4]{0:T(128)}, u32[]{:S(2)}) copy-start(s32[4]{0:T(128)} %param.16) | copy-start | bytes 52
  0.7 7.3 %copy-start.2 = (bf16[192,1024]{1,0:T(8,128)(2,1)S(1)}, bf16[192,1024]{1,0:T(8,128)(2,1)}, u32[]{:S(2)}) copy-start(bf16[192,1024]{1,0:T(8,128)(2,1)} %q_ref.17) | copy-start | bytes 1179652
  1.9 21.7 %collective-permute-start = (bf16[2,192,1024]{2,1,0:T(8,128)(2,1)S(1)}, bf16[2,192,1024]{2,1,0:T(8,128)(2,1)}, u32[]{:S(2)}, u32[]{:S(2)}) collective-permute-start(bf16[2,192,1024]{2,1,0:T(8,128)(2,1)S(1)} %pad_maximum_fusion.refs_0_), channel_id=1, source_target_pairs={{0,8},{4,12},{8,16},{12,20},{16,24},{20,28},{1,9},{5,13},{9,17},{1... | collective-permute-start | bytes 2359304 | tf_op jit(solution)/shard_map/ppermute | solution.py:41
  23.6 20.7 %collective-permute-start.1 = (bf16[2,192,1024]{2,1,0:T(8,128)(2,1)}, bf16[2,192,1024]{2,1,0:T(8,128)(2,1)S(1)}, u32[]{:S(2)}, u32[]{:S(2)}) collective-permute-start(bf16[2,192,1024]{2,1,0:T(8,128)(2,1)} %collective-permute-done.refs_0_), channel_id=1, source_target_pairs={{0,8},{4,12},{8,16},{12,20},{16,24},{20,28},{1,9},{5,13},{9,17},{1... | collective-permute-start | bytes 2359304 | tf_op jit(solution)/shard_map/ppermute | solution.py:41
  28.2 21.4 %collective-permute-start.5 = (bf16[2,192,1024]{2,1,0:T(8,128)(2,1)S(1)}, bf16[2,192,1024]{2,1,0:T(8,128)(2,1)S(1)}, u32[]{:S(2)}, u32[]{:S(2)}) collective-permute-start(bf16[2,192,1024]{2,1,0:T(8,128)(2,1)S(1)} %pad_maximum_fusion.refs_0_), channel_id=1, source_target_pairs={{0,4},{8,12},{16,20},{24,28},{1,5},{9,13},{17,21},{25,29},{2,6},{1... | collective-permute-start | bytes 2359304 | tf_op jit(solution)/shard_map/ppermute | solution.py:49
  31.6 22.6 %collective-permute-start.4 = (bf16[2,192,1024]{2,1,0:T(8,128)(2,1)}, bf16[2,192,1024]{2,1,0:T(8,128)(2,1)S(1)}, u32[]{:S(2)}, u32[]{:S(2)}) collective-permute-start(bf16[2,192,1024]{2,1,0:T(8,128)(2,1)} %collective-permute-done.refs_0_), channel_id=1, source_target_pairs={{4,0},{12,8},{20,16},{28,24},{5,1},{13,9},{21,17},{29,25},{6,2},{1... | collective-permute-start | bytes 2359304 | tf_op jit(solution)/shard_map/ppermute | solution.py:53
  32.9 31.2 %collective-permute-start.3 = (bf16[2,192,1024]{2,1,0:T(8,128)(2,1)}, bf16[2,192,1024]{2,1,0:T(8,128)(2,1)}, u32[]{:S(2)}, u32[]{:S(2)}) collective-permute-start(bf16[2,192,1024]{2,1,0:T(8,128)(2,1)} %collective-permute-done.refs_0_), channel_id=1, source_target_pairs={{0,4},{8,12},{16,20},{24,28},{1,5},{9,13},{17,21},{25,29},{2,6},{1... | collective-permute-start | bytes 2359304 | tf_op jit(solution)/shard_map/ppermute | solution.py:49
  40.7 0.9 copy-start.28
  41.6 0.6 copy-start.30
  44.3 26.8 %collective-permute-start.2 = (bf16[2,192,1024]{2,1,0:T(8,128)(2,1)S(1)}, bf16[2,192,1024]{2,1,0:T(8,128)(2,1)}, u32[]{:S(2)}, u32[]{:S(2)}) collective-permute-start(bf16[2,192,1024]{2,1,0:T(8,128)(2,1)S(1)} %collective-permute-done.1.refs_0_), channel_id=1, source_target_pairs={{4,0},{12,8},{20,16},{28,24},{5,1},{13,9},{21,17},{29,25},{6,2},{1... | collective-permute-start | bytes 2359304 | tf_op jit(solution)/shard_map/ppermute | solution.py:53
  45.6 25.4 %collective-permute-start.9 = (bf16[192,768]{1,0:T(8,128)(2,1)}, bf16[192,768]{1,0:T(8,128)(2,1)}, u32[]{:S(2)}, u32[]{:S(2)}) collective-permute-start(bf16[192,768]{1,0:T(8,128)(2,1)} %w0), channel_id=1, source_target_pairs={{0,3},{1,2},{2,1},{3,0},{4,7},{5,6},{6,5},{7,4},{8,11},{9,10},{10,... | collective-permute-start | bytes 884744 | tf_op jit(solution)/shard_map/ppermute | solution.py:62
  49.6 21.5 %collective-permute-start.8 = (bf16[192,768]{1,0:T(8,128)(2,1)}, bf16[192,768]{1,0:T(8,128)(2,1)}, u32[]{:S(2)}, u32[]{:S(2)}) collective-permute-start(bf16[192,768]{1,0:T(8,128)(2,1)} %w0), channel_id=1, source_target_pairs={{0,2},{1,3},{2,0},{3,1},{4,6},{5,7},{6,4},{7,5},{8,10},{9,11},{10,... | collective-permute-start | bytes 884744 | tf_op jit(solution)/shard_map/ppermute | solution.py:62
  54.2 16.9 %collective-permute-start.7 = (bf16[192,768]{1,0:T(8,128)(2,1)}, bf16[192,768]{1,0:T(8,128)(2,1)}, u32[]{:S(2)}, u32[]{:S(2)}) collective-permute-start(bf16[192,768]{1,0:T(8,128)(2,1)} %w0), channel_id=1, source_target_pairs={{0,1},{1,0},{2,3},{3,2},{4,5},{5,4},{6,7},{7,6},{8,9},{9,8},{10,11... | collective-permute-start | bytes 884744 | tf_op jit(solution)/shard_map/ppermute | solution.py:62
  56.7 1.1 copy-start.29
  57.8 0.8 copy-start.31
  58.5 5.6 %copy-start.36 = (f32[48,256]{1,0:T(8,128)S(1)}, f32[48,256]{1,0:T(8,128)}, u32[]{:S(2)}) copy-start(f32[48,256]{1,0:T(8,128)} %shard_map.151) | copy-start | bytes 147460
  64.2 6.9 %collective-permute-start.6 = (f32[48,256]{1,0:T(8,128)S(1)}, f32[48,256]{1,0:T(8,128)S(1)}, u32[]{:S(2)}, u32[]{:S(2)}) collective-permute-start(f32[48,256]{1,0:T(8,128)S(1)} %copy-done.36), channel_id=1, source_target_pairs={{0,28},{4,24},{8,20},{12,16},{16,12},{20,8},{24,4},{28,0},{1,29},{... | collective-permute-start | bytes 147464 | tf_op jit(solution)/shard_map/ppermute | solution.py:58
  67.7 3.4 %copy-start.3 = (bf16[192,1024]{1,0:T(8,128)(2,1)S(1)}, bf16[192,1024]{1,0:T(8,128)(2,1)}, u32[]{:S(2)}) copy-start(bf16[192,1024]{1,0:T(8,128)(2,1)} %q_ref.17) | copy-start | bytes 1179652
  71.1 4.6 %copy-start.37 = (f32[768]{0:T(1024)S(1)}, f32[768]{0:T(1024)}, u32[]{:S(2)}) copy-start(f32[768]{0:T(1024)} %param.19) | copy-start | bytes 9220
  71.1 9.9 %copy-start = (bf16[1024,768]{1,0:T(8,128)(2,1)S(1)}, bf16[1024,768]{1,0:T(8,128)(2,1)}, u32[]{:S(2)}) copy-start(bf16[1024,768]{1,0:T(8,128)(2,1)} %stream_ref.1) | copy-start | bytes 4718596
  71.1 9.9 %copy-start.6 = (bf16[192,768]{1,0:T(8,128)(2,1)S(1)}, bf16[192,768]{1,0:T(8,128)(2,1)}, u32[]{:S(2)}) copy-start(bf16[192,768]{1,0:T(8,128)(2,1)} %w0) | copy-start | bytes 884740
  71.1 9.9 %copy-start.7 = (f32[1024,48]{0,1:T(8,128)S(1)}, f32[1024,48]{0,1:T(8,128)}, u32[]{:S(2)}) copy-start(f32[1024,48]{0,1:T(8,128)} %param.21) | copy-start | bytes 589828
  71.1 9.9 %copy-start.8 = (bf16[96,768]{1,0:T(8,128)(2,1)S(1)}, bf16[96,768]{1,0:T(8,128)(2,1)}, u32[]{:S(2)}) copy-start(bf16[96,768]{1,0:T(8,128)(2,1)} %head_ref.1) | copy-start | bytes 442372
  71.1 9.9 %copy-start.24 = (s32[2]{0:T(128)S(1)}, s32[2]{0:T(128)}, u32[]{:S(2)}) copy-start(s32[2]{0:T(128)} %pad_add_fusion.place_ref) | copy-start | bytes 28
  73.7 17.4 %copy-start.21 = (f32[4,8,256]{2,1,0:T(8,128)}, f32[4,8,256]{2,1,0:T(8,128)S(1)}, u32[]{:S(2)}) copy-start(f32[4,8,256]{2,1,0:T(8,128)S(1)} %get-tuple-element.77.lse_any) | copy-start | bytes 98308
  73.7 5.1 %collective-permute-start.12 = (bf16[192,256]{1,0:T(8,128)(2,1)S(1)}, bf16[192,256]{1,0:T(8,128)(2,1)S(1)}, u32[]{:S(2)}, u32[]{:S(2)}) collective-permute-start(bf16[192,256]{1,0:T(8,128)(2,1)S(1)} %get-tuple-element.114), channel_id=1, source_target_pairs={{0,3},{1,2},{2,1},{3,0},{4,7},{5,6},{6,5},{7,4},{8,11},{9,10},{10,... | collective-permute-start | bytes 294920 | tf_op jit(solution)/shard_map/ppermute | solution.py:62
  73.8 7.2 %collective-permute-start.11 = (bf16[192,256]{1,0:T(8,128)(2,1)S(1)}, bf16[192,256]{1,0:T(8,128)(2,1)S(1)}, u32[]{:S(2)}, u32[]{:S(2)}) collective-permute-start(bf16[192,256]{1,0:T(8,128)(2,1)S(1)} %get-tuple-element.115), channel_id=1, source_target_pairs={{0,2},{1,3},{2,0},{3,1},{4,6},{5,7},{6,4},{7,5},{8,10},{9,11},{10,... | collective-permute-start | bytes 294920 | tf_op jit(solution)/shard_map/ppermute | solution.py:62
  75.4 5.6 %collective-permute-start.10 = (bf16[192,256]{1,0:T(8,128)(2,1)S(1)}, bf16[192,256]{1,0:T(8,128)(2,1)S(1)}, u32[]{:S(2)}, u32[]{:S(2)}) collective-permute-start(bf16[192,256]{1,0:T(8,128)(2,1)S(1)} %get-tuple-element.116), channel_id=1, source_target_pairs={{0,1},{1,0},{2,3},{3,2},{4,5},{5,4},{6,7},{7,6},{8,9},{9,8},{10,11... | collective-permute-start | bytes 294920 | tf_op jit(solution)/shard_map/ppermute | solution.py:62
  84.1 10.9 %copy-start.9 = (bf16[192,256]{1,0:T(8,128)(2,1)}, bf16[192,256]{1,0:T(8,128)(2,1)S(1)}, u32[]{:S(2)}) copy-start(bf16[192,256]{1,0:T(8,128)(2,1)S(1)} %get-tuple-element.83.g0) | copy-start | bytes 294916
  84.1 11.8 %copy-start.27 = (f32[48,256]{1,0:T(8,128)}, f32[48,256]{1,0:T(8,128)S(1)}, u32[]{:S(2)}) copy-start(f32[48,256]{1,0:T(8,128)S(1)} %get-tuple-element.92) | copy-start | bytes 147460
  84.1 1.9 %collective-permute-start.13 = (bf16[192,256]{1,0:T(8,128)(2,1)S(1)}, bf16[192,256]{1,0:T(8,128)(2,1)S(1)}, u32[]{:S(2)}, u32[]{:S(2)}) collective-permute-start(bf16[192,256]{1,0:T(8,128)(2,1)S(1)} %get-tuple-element.84), channel_id=1, source_target_pairs={{0,1},{1,0},{2,3},{3,2},{4,5},{5,4},{6,7},{7,6},{8,9},{9,8},{10,11... | collective-permute-start | bytes 294920 | tf_op jit(solution)/shard_map/ppermute | solution.py:62
  84.3 5.6 %collective-permute-start.14 = (bf16[192,256]{1,0:T(8,128)(2,1)S(1)}, bf16[192,256]{1,0:T(8,128)(2,1)S(1)}, u32[]{:S(2)}, u32[]{:S(2)}) collective-permute-start(bf16[192,256]{1,0:T(8,128)(2,1)S(1)} %get-tuple-element.85), channel_id=1, source_target_pairs={{0,2},{1,3},{2,0},{3,1},{4,6},{5,7},{6,4},{7,5},{8,10},{9,11},{10,... | collective-permute-start | bytes 294920 | tf_op jit(solution)/shard_map/ppermute | solution.py:62
  84.6 6.5 %collective-permute-start.15 = (bf16[192,256]{1,0:T(8,128)(2,1)S(1)}, bf16[192,256]{1,0:T(8,128)(2,1)S(1)}, u32[]{:S(2)}, u32[]{:S(2)}) collective-permute-start(bf16[192,256]{1,0:T(8,128)(2,1)S(1)} %get-tuple-element.86), channel_id=1, source_target_pairs={{0,3},{1,2},{2,1},{3,0},{4,7},{5,6},{6,5},{7,4},{8,11},{9,10},{10,... | collective-permute-start | bytes 294920 | tf_op jit(solution)/shard_map/ppermute | solution.py:62
  86.1 8.9 %copy-start.12 = (bf16[192,256]{1,0:T(8,128)(2,1)}, bf16[192,256]{1,0:T(8,128)(2,1)S(1)}, u32[]{:S(2)}) copy-start(bf16[192,256]{1,0:T(8,128)(2,1)S(1)} %collective-permute-done.13.g1) | copy-start | bytes 294916
  89.9 5.1 %copy-start.15 = (bf16[192,256]{1,0:T(8,128)(2,1)}, bf16[192,256]{1,0:T(8,128)(2,1)S(1)}, u32[]{:S(2)}) copy-start(bf16[192,256]{1,0:T(8,128)(2,1)S(1)} %collective-permute-done.14.g2) | copy-start | bytes 294916
  91.1 3.9 %copy-start.18 = (bf16[192,256]{1,0:T(8,128)(2,1)}, bf16[192,256]{1,0:T(8,128)(2,1)S(1)}, u32[]{:S(2)}) copy-start(bf16[192,256]{1,0:T(8,128)(2,1)S(1)} %collective-permute-done.15.g3) | copy-start | bytes 294916
  95.0 0.9 copy-start.1
  95.9 30.9 %collective-permute-start.16 = (bf16[2,192,1024]{2,1,0:T(8,128)(2,1)}, bf16[2,192,1024]{2,1,0:T(8,128)(2,1)}, u32[]{:S(2)}, u32[]{:S(2)}) collective-permute-start(bf16[2,192,1024]{2,1,0:T(8,128)(2,1)} %get-tuple-element.90), channel_id=1, source_target_pairs={{0,4},{4,0},{8,12},{12,8},{16,20},{20,16},{24,28},{28,24},{1,5},{5... | collective-permute-start | bytes 2359304 | tf_op jit(solution)/shard_map/ppermute | solution.py:45
  97.1 30.6 %collective-permute-start.17 = (f32[48,256]{1,0:T(8,128)}, f32[48,256]{1,0:T(8,128)S(1)}, u32[]{:S(2)}, u32[]{:S(2)}) collective-permute-start(f32[48,256]{1,0:T(8,128)} %copy-done.27), channel_id=1, source_target_pairs={{0,28},{4,24},{8,20},{12,16},{16,12},{20,8},{24,4},{28,0},{1,29},{... | collective-permute-start | bytes 147464 | tf_op jit(solution)/shard_map/ppermute | solution.py:58
  107.9 1.0 copy-start.4
  108.9 0.9 copy-start.10
  109.8 0.9 copy-start.13
  110.7 0.9 copy-start.16
  111.6 0.9 copy-start.19
  112.5 0.8 copy-start.22
  117.3 10.5 %copy-start.25 = (f32[4,192,256]{2,1,0:T(8,128)}, f32[4,192,256]{2,1,0:T(8,128)S(1)}, u32[]{:S(2)}) copy-start(f32[4,192,256]{2,1,0:T(8,128)S(1)} %get-tuple-element.93.refs_1_) | copy-start | bytes 2359300
  117.3 15.9 %copy-start.5 = (bf16[192,1024]{1,0:T(8,128)(2,1)S(1)}, bf16[192,1024]{1,0:T(8,128)(2,1)}, u32[]{:S(2)}) copy-start(bf16[192,1024]{1,0:T(8,128)(2,1)} %q_ref.17) | copy-start | bytes 1179652
  117.3 15.9 %copy-start.11 = (bf16[192,256]{1,0:T(8,128)(2,1)S(1)}, bf16[192,256]{1,0:T(8,128)(2,1)}, u32[]{:S(2)}) copy-start(bf16[192,256]{1,0:T(8,128)(2,1)} %copy-done.9) | copy-start | bytes 294916
  117.3 15.9 %copy-start.14 = (bf16[192,256]{1,0:T(8,128)(2,1)S(1)}, bf16[192,256]{1,0:T(8,128)(2,1)}, u32[]{:S(2)}) copy-start(bf16[192,256]{1,0:T(8,128)(2,1)} %copy-done.12) | copy-start | bytes 294916
  117.3 15.8 %copy-start.17 = (bf16[192,256]{1,0:T(8,128)(2,1)S(1)}, bf16[192,256]{1,0:T(8,128)(2,1)}, u32[]{:S(2)}) copy-start(bf16[192,256]{1,0:T(8,128)(2,1)} %copy-done.15) | copy-start | bytes 294916
  117.4 15.8 %copy-start.20 = (bf16[192,256]{1,0:T(8,128)(2,1)S(1)}, bf16[192,256]{1,0:T(8,128)(2,1)}, u32[]{:S(2)}) copy-start(bf16[192,256]{1,0:T(8,128)(2,1)} %copy-done.18) | copy-start | bytes 294916
  117.4 27.4 %collective-permute-start.18 = (bf16[2,192,1024]{2,1,0:T(8,128)(2,1)}, bf16[2,192,1024]{2,1,0:T(8,128)(2,1)}, u32[]{:S(2)}, u32[]{:S(2)}) collective-permute-start(bf16[2,192,1024]{2,1,0:T(8,128)(2,1)} %get-tuple-element.96), channel_id=1, source_target_pairs={{0,4},{4,0},{8,12},{12,8},{16,20},{20,16},{24,28},{28,24},{1,5},{5... | collective-permute-start | bytes 2359304 | tf_op jit(solution)/shard_map/ppermute | solution.py:45
  127.8 0.6 copy-start.35
  128.4 21.8 %collective-permute-start.19 = (bf16[2,192,1024]{2,1,0:T(8,128)(2,1)}, bf16[2,192,1024]{2,1,0:T(8,128)(2,1)}, u32[]{:S(2)}, u32[]{:S(2)}) collective-permute-start(bf16[2,192,1024]{2,1,0:T(8,128)(2,1)} %select_add_fusion), channel_id=1, source_target_pairs={{8,0},{12,4},{16,8},{20,12},{24,16},{28,20},{9,1},{13,5},{17,9},{2... | collective-permute-start | bytes 2359304 | tf_op jit(solution)/shard_map/ppermute | solution.py:41
  131.3 21.3 %collective-permute-start.22 = (f32[48,256]{1,0:T(8,128)}, f32[48,256]{1,0:T(8,128)S(1)}, u32[]{:S(2)}, u32[]{:S(2)}) collective-permute-start(f32[48,256]{1,0:T(8,128)} %shard_map.157.p0), channel_id=1, source_target_pairs={{0,3},{1,2},{2,1},{3,0},{4,7},{5,6},{6,5},{7,4},{8,11},{9,10},{10,... | collective-permute-start | bytes 147464 | tf_op jit(solution)/shard_map/ppermute | solution.py:62
  131.9 20.7 %collective-permute-start.21 = (f32[48,256]{1,0:T(8,128)}, f32[48,256]{1,0:T(8,128)S(1)}, u32[]{:S(2)}, u32[]{:S(2)}) collective-permute-start(f32[48,256]{1,0:T(8,128)} %shard_map.157.p0), channel_id=1, source_target_pairs={{0,2},{1,3},{2,0},{3,1},{4,6},{5,7},{6,4},{7,5},{8,10},{9,11},{10,... | collective-permute-start | bytes 147464 | tf_op jit(solution)/shard_map/ppermute | solution.py:62
  132.7 20.0 %collective-permute-start.20 = (f32[48,256]{1,0:T(8,128)}, f32[48,256]{1,0:T(8,128)S(1)}, u32[]{:S(2)}, u32[]{:S(2)}) collective-permute-start(f32[48,256]{1,0:T(8,128)} %shard_map.157.p0), channel_id=1, source_target_pairs={{0,1},{1,0},{2,3},{3,2},{4,5},{5,4},{6,7},{7,6},{8,9},{9,8},{10,11... | collective-permute-start | bytes 147464 | tf_op jit(solution)/shard_map/ppermute | solution.py:62
  133.2 0.8 copy-start.23
  134.0 1.1 copy-start.26
  152.6 10.0 %copy-start.32 = (f32[48,256]{1,0:T(8,128)}, f32[48,256]{1,0:T(8,128)S(1)}, u32[]{:S(2)}) copy-start(f32[48,256]{1,0:T(8,128)S(1)} %collective-permute-done.22.p3) | copy-start | bytes 147460
  152.6 10.0 %copy-start.33 = (f32[48,256]{1,0:T(8,128)}, f32[48,256]{1,0:T(8,128)S(1)}, u32[]{:S(2)}) copy-start(f32[48,256]{1,0:T(8,128)S(1)} %collective-permute-done.21.p2) | copy-start | bytes 147460
  152.6 10.0 %copy-start.34 = (f32[48,256]{1,0:T(8,128)}, f32[48,256]{1,0:T(8,128)S(1)}, u32[]{:S(2)}) copy-start(f32[48,256]{1,0:T(8,128)S(1)} %collective-permute-done.20.p1) | copy-start | bytes 147460
  152.6 23.3 %collective-permute-start.23 = (bf16[2,192,1024]{2,1,0:T(8,128)(2,1)}, bf16[2,192,1024]{2,1,0:T(8,128)(2,1)}, u32[]{:S(2)}, u32[]{:S(2)}) collective-permute-start(bf16[2,192,1024]{2,1,0:T(8,128)(2,1)} %add_add_fusion), channel_id=1, source_target_pairs={{8,0},{12,4},{16,8},{20,12},{24,16},{28,20},{9,1},{13,5},{17,9},{2... | collective-permute-start | bytes 2359304 | tf_op jit(solution)/shard_map/ppermute | solution.py:41

commit v5 on v4

--- a/solution.py
+++ b/solution.py
@@ -11,6 +11,7 @@
 BLOCK = 256
 LIST = 16
 REACH = 4
+VMEM_GRANT = 63 << 20
 
 NEG = -1e30
 EPS = 1e-05
@@ -333,7 +334,7 @@
             pltpu.SemaphoreType.DMA((4,)),
             pltpu.SemaphoreType.DMA((2,)),
         ],
-        compiler_params=pltpu.CompilerParams(vmem_limit_bytes=48 << 20),
+        compiler_params=pltpu.CompilerParams(vmem_limit_bytes=VMEM_GRANT),
         cost_estimate=pl.CostEstimate(
             flops=pairs * 10 ** 9, bytes_accessed=6 << 20, transcendentals=pairs * 10 ** 5),
     )(tables, queries, *slabs, *state)
@@ -516,7 +517,7 @@
             pltpu.SemaphoreType.DMA((9,)),
             pltpu.SemaphoreType.DMA((3,)),
         ],
-        compiler_params=pltpu.CompilerParams(vmem_limit_bytes=48 << 20),
+        compiler_params=pltpu.CompilerParams(vmem_limit_bytes=VMEM_GRANT),
         cost_estimate=pl.CostEstimate(
             flops=pairs * 10 ** 9, bytes_accessed=8 << 20, transcendentals=pairs * 10 ** 5),
     )(tables, queries, attended, lse, *grads, *slabs, *given)
@@ -561,12 +562,13 @@
         place, parts, weights, stream, norm_gain.reshape(1, -1), head_proj, patches.T,
         grad_latent)
     grads = [grads[0]] + [across(grads[k], k) for k in range(1, cols)]
+    *grads, latent = tie([*grads, latent])
+    mirrored = mirror(latent)
 
     shared = (tables, queries, attended, lse, grads)
     grad_queries, part3 = backward(*shared, [(3, 3, "each")], [down2, up2])
+    part3, mirrored = tie([part3, mirrored])
     from3 = mate(part3)
-    part3, latent = tie([part3, latent])
-    mirrored = mirror(latent)
     grad_queries, part4, part1 = backward(
         *shared, [(4, 4, "both"), (1, 1, "each")], [slab4, down1, up1], grad_queries)
     from1 = mate(part1)
@@ -583,9 +585,10 @@
     grad_queries, own_grad = backward(*shared, [(0, 0, "both")], [own], grad_queries, True)
     own_grad, *pieces = tie([own_grad] + pieces)
     latent_out = assembled(place, pieces, tokens).T
-    own_grad = own_grad + jnp.where(odd, zero, from1).astype(F32) + near.astype(F32)
-    own_grad = own_grad.astype(BF16)
-    return (latent_out, grad_queries, own_grad[0], own_grad[1])
+    grad_keys, grad_values = (
+        (own_grad[i] + jnp.where(odd, zero[i], from1[i]).astype(F32) + near[i].astype(F32))
+        .astype(BF16) for i in range(2))
+    return (latent_out, grad_queries, grad_keys, grad_values)
 
 
 def solution(mesh):

time: 182 us -> 186 us (1.022)
  the two profiles are of different devices: /device:TPU:0 before, /device:TPU:8 now
where the time goes in v5:
time: 186 us; the launch traced here: 184 us
  waiting for transfers between devices  62.5 us (34%)
  Pallas kernels  53.7 us (29%)
  starting transfers between devices  50.7 us (27%)
  other arithmetic  9.3 us (5%)
  local copies, waits for them, and re-layouts  6.25 us (3%)
    ppermute x4, waiting for transfers between devices, hop(): return lax.ppermute(array, 'row', pairs)  33.4 us
    pallas_call x4, Pallas kernels, backward(): pl.pallas_call(functools.partial(backward_kernel, regions, diagonal, last...  23.9 us
    pallas_call x5, Pallas kernels, forward(): pl.pallas_call(functools.partial(forward_kernel, regions, not state, clos...  21.8 us
    ppermute x4, starting transfers between devices, hop(): return lax.ppermute(array, 'row', pairs)  20 us
    ppermute x2, waiting for transfers between devices, mate(): lax.ppermute(array, 'row', [(i, i ^ 1) for i in range(lax.axis_size('row'...  10.7 us
    ppermute x2, starting transfers between devices, upward(): lax.ppermute(array, 'row', [(i, i + 1) for i in range(0, lax.axis_size('r...  10.6 us
    ppermute x12, waiting for transfers between devices, across(): lax.ppermute(array, 'col', [(i, i ^ bits) for i in range(lax.axis_size('c...  10.3 us
    ppermute x2, starting transfers between devices, mirror(): return lax.ppermute(array, 'row', [(i, size - 1 - i) for i in range(size)])  7.6 us
  transfers between devices with their start and end apart: 24, of which 12 were waited for; matrix products, arithmetic and copies ran while one was open for 3% of the time, Pallas kernels for 26%

profile of v5, /device:TPU:8, one launch (start us, length us, event | category | flops | bytes accessed | tf_op | source)
XLA Modules:
  0.0 183.5 jit_solution(11064712071704821779)
XLA Ops:
  0.7 1.2 pad_maximum_fusion.refs_0_
  1.9 3.5 %collective-permute-start = (bf16[2,192,1024]{2,1,0:T(8,128)(2,1)S(1)}, bf16[2,192,1024]{2,1,0:T(8,128)(2,1)}, u32[]{:S(2)}, u32[]{:S(2)}) collective-permute-start(bf16[2,192,1024]{2,1,0:T(8,128)(2,1)S(1)} %pad_maximum_fusion.refs_0_), channel_id=1, source_target_pairs={{0,8},{4,12},{8,16},{12,20},{16,24},{20,28},{1,9},{5,13},{9,17},{1... | collective-permute-start | bytes 2359304 | tf_op jit(solution)/shard_map/ppermute | solution.py:42
  5.4 0.1 reshape.33
  5.5 0.1 pad_add_fusion.1
  5.5 0.5 pad.4.table_ref
  6.1 6.5 %shard_map.147 = (f32[4,192,256]{2,1,0:T(8,128)}, f32[4,8,256]{2,1,0:T(8,128)}) custom-call(s32[128]{0:T(128)} %pad.4.table_ref, bf16[192,1024]{1,0:T(8,128)(2,1)} %q_ref.17, bf16[2,192,1024]{2,1,0:T(8,128)(2,1)} %copy-done.6), custom_call_target="tpu_custom_call" | custom-call | flops 1000000000 | bytes 6291456 | tf_op jit(solution)/shard_map/pallas_call | solution.py:314
  12.6 10.5 %collective-permute-done.refs_0_ = bf16[2,192,1024]{2,1,0:T(8,128)(2,1)} collective-permute-done((bf16[2,192,1024]{2,1,0:T(8,128)(2,1)S(1)}, bf16[2,192,1024]{2,1,0:T(8,128)(2,1)}, u32[]{:S(2)}, u32[]{:S(2)}) %collective-permute-start) | collective-permute-done | bytes 786464 | tf_op jit(solution)/shard_map/ppermute | solution.py:42
  23.1 3.6 %collective-permute-start.1 = (bf16[2,192,1024]{2,1,0:T(8,128)(2,1)}, bf16[2,192,1024]{2,1,0:T(8,128)(2,1)}, u32[]{:S(2)}, u32[]{:S(2)}) collective-permute-start(bf16[2,192,1024]{2,1,0:T(8,128)(2,1)} %collective-permute-done.refs_0_), channel_id=1, source_target_pairs={{0,8},{4,12},{8,16},{12,20},{16,24},{20,28},{1,9},{5,13},{9,17},{1... | collective-permute-start | bytes 2359304 | tf_op jit(solution)/shard_map/ppermute | solution.py:42
  26.8 4.3 %collective-permute-start.5 = (bf16[2,192,1024]{2,1,0:T(8,128)(2,1)}, bf16[2,192,1024]{2,1,0:T(8,128)(2,1)}, u32[]{:S(2)}, u32[]{:S(2)}) collective-permute-start(bf16[2,192,1024]{2,1,0:T(8,128)(2,1)} %copy-done.6), channel_id=1, source_target_pairs={{0,4},{8,12},{16,20},{24,28},{1,5},{9,13},{17,21},{25,29},{2,6},{1... | collective-permute-start | bytes 2359304 | tf_op jit(solution)/shard_map/ppermute | solution.py:50
  31.1 1.3 collective-permute-start.4
  32.4 6.3 %collective-permute-start.3 = (bf16[2,192,1024]{2,1,0:T(8,128)(2,1)}, bf16[2,192,1024]{2,1,0:T(8,128)(2,1)}, u32[]{:S(2)}, u32[]{:S(2)}) collective-permute-start(bf16[2,192,1024]{2,1,0:T(8,128)(2,1)} %collective-permute-done.refs_0_), channel_id=1, source_target_pairs={{0,4},{8,12},{16,20},{24,28},{1,5},{9,13},{17,21},{25,29},{2,6},{1... | collective-permute-start | bytes 2359304 | tf_op jit(solution)/shard_map/ppermute | solution.py:50
  38.7 3.2 %shard_map.148 = (f32[4,192,256]{2,1,0:T(8,128)}, f32[4,8,256]{2,1,0:T(8,128)}) custom-call(s32[128]{0:T(128)} %pad.4.table_ref, bf16[192,1024]{1,0:T(8,128)(2,1)} %q_ref.17, bf16[2,192,1024]{2,1,0:T(8,128)(2,1)} %collective-permute-done.refs_0_, f32[4,192,256]{2,1,0:T(8,128)} %get-tuple-element.67.refs_1_, f32[4,8,256]{2,1,0:T(8,128)} %get-tuple-element.68.refs_2_), custom_call_target="tpu_custom_call" | custom-call | flops 1000000000 | bytes 6291456 | tf_op jit(solution)/shard_map/pallas_call | solution.py:314
  41.9 2.0 %collective-permute-done.1.refs_0_ = bf16[2,192,1024]{2,1,0:T(8,128)(2,1)} collective-permute-done((bf16[2,192,1024]{2,1,0:T(8,128)(2,1)}, bf16[2,192,1024]{2,1,0:T(8,128)(2,1)}, u32[]{:S(2)}, u32[]{:S(2)}) %collective-permute-start.1) | collective-permute-done | bytes 786464 | tf_op jit(solution)/shard_map/ppermute | solution.py:42
  43.9 1.3 collective-permute-start.2
  45.2 0.1 collective-permute-start.9
  45.3 3.2 %collective-permute-done.5.refs_1_.refs_2_ = bf16[2,192,1024]{2,1,0:T(8,128)(2,1)} collective-permute-done((bf16[2,192,1024]{2,1,0:T(8,128)(2,1)}, bf16[2,192,1024]{2,1,0:T(8,128)(2,1)}, u32[]{:S(2)}, u32[]{:S(2)}) %collective-permute-start.5) | collective-permute-done | bytes 786464 | tf_op jit(solution)/shard_map/ppermute | solution.py:50
  48.5 1.5 collective-permute-start.8
  50.0 3.8 %collective-permute-done.4.refs_0_.refs_1_ = bf16[2,192,1024]{2,1,0:T(8,128)(2,1)} collective-permute-done((bf16[2,192,1024]{2,1,0:T(8,128)(2,1)}, bf16[2,192,1024]{2,1,0:T(8,128)(2,1)}, u32[]{:S(2)}, u32[]{:S(2)}) %collective-permute-start.4) | collective-permute-done | bytes 786464 | tf_op jit(solution)/shard_map/ppermute | solution.py:54
  53.8 0.6 pad_add_fusion.place_ref
  54.4 1.8 %shard_map.151 = f32[48,256]{1,0:T(8,128)} custom-call(s32[2]{0:T(128)} %pad_add_fusion.place_ref, s32[1,1024]{1,0:T(1,128)} %bitcast.17, f32[48,1024]{1,0:T(8,128)} %bitcast.16), custom_call_target="tpu_custom_call" | custom-call | tf_op jit(solution)/shard_map/pallas_call | solution.py:93
  56.3 5.7 %shard_map.149 = (f32[4,192,256]{2,1,0:T(8,128)}, f32[4,8,256]{2,1,0:T(8,128)}) custom-call(s32[128]{0:T(128)} %pad.4.table_ref, bf16[192,1024]{1,0:T(8,128)(2,1)} %q_ref.17, bf16[2,192,1024]{2,1,0:T(8,128)(2,1)} %collective-permute-done.4.refs_0_.refs_1_, bf16[2,192,1024]{2,1,0:T(8,128)(2,1)} %collective-permute-done.5.refs_1_.refs_2_, ...), custom_call_target="tpu_custom_call" | custom-call | flops 1000000000 | bytes 6291456 | tf_op jit(solution)/shard_map/pallas_call | solution.py:314
  62.0 1.0 collective-permute-done.3.refs_1_
  63.0 3.5 %collective-permute-start.6 = (f32[48,256]{1,0:T(8,128)S(1)}, f32[48,256]{1,0:T(8,128)S(1)}, u32[]{:S(2)}, u32[]{:S(2)}) collective-permute-start(f32[48,256]{1,0:T(8,128)S(1)} %copy-done.14), channel_id=1, source_target_pairs={{0,28},{4,24},{8,20},{12,16},{16,12},{20,8},{24,4},{28,0},{1,29},{... | collective-permute-start | bytes 147464 | tf_op jit(solution)/shard_map/ppermute | solution.py:59
  66.5 3.2 %shard_map.150 = (f32[4,192,256]{2,1,0:T(8,128)}, f32[4,8,256]{2,1,0:T(8,128)}) custom-call(s32[128]{0:T(128)} %pad.4.table_ref, bf16[192,1024]{1,0:T(8,128)(2,1)} %q_ref.17, bf16[2,192,1024]{2,1,0:T(8,128)(2,1)} %collective-permute-done.1.refs_0_, bf16[2,192,1024]{2,1,0:T(8,128)(2,1)} %collective-permute-done.3.refs_1_, ...), custom_call_target="tpu_custom_call" | custom-call | flops 1000000000 | bytes 6291456 | tf_op jit(solution)/shard_map/pallas_call | solution.py:314
  69.7 0.0 collective-permute-done.9.w3
  69.8 0.0 copy-start.15
  69.8 3.2 %shard_map.152 = (bf16[192,1024]{1,0:T(8,128)(2,1)}, f32[4,8,256]{2,1,0:T(8,128)}) custom-call(s32[128]{0:T(128)} %pad.4.table_ref, bf16[192,1024]{1,0:T(8,128)(2,1)} %q_ref.17, bf16[2,192,1024]{2,1,0:T(8,128)(2,1)} %collective-permute-done.2.refs_0_, f32[4,192,256]{2,1,0:T(8,128)} %get-tuple-element.80.refs_1_, f32[4,8,256]{2,1,0:T(8,128)} %get-tuple-element.81.refs_2_), custom_call_target="tpu_custom_call" | custom-call | flops 1000000000 | bytes 6291456 | tf_op jit(solution)/shard_map/pallas_call | solution.py:314
  72.9 1.1 constant_dynamic-slice_fusion
  74.0 0.1 collective-permute-start.12
  74.1 1.6 collective-permute-start.11
  75.7 0.3 collective-permute-start.10
  76.0 3.2 %collective-permute-done.12.a3 = bf16[192,256]{1,0:T(8,128)(2,1)S(1)} collective-permute-done((bf16[192,256]{1,0:T(8,128)(2,1)S(1)}, bf16[192,256]{1,0:T(8,128)(2,1)S(1)}, u32[]{:S(2)}, u32[]{:S(2)}) %collective-permute-start.12) | collective-permute-done | bytes 98336 | tf_op jit(solution)/shard_map/ppermute | solution.py:63
  79.1 2.2 %collective-permute-done.11.a2 = bf16[192,256]{1,0:T(8,128)(2,1)S(1)} collective-permute-done((bf16[192,256]{1,0:T(8,128)(2,1)S(1)}, bf16[192,256]{1,0:T(8,128)(2,1)S(1)}, u32[]{:S(2)}, u32[]{:S(2)}) %collective-permute-start.11) | collective-permute-done | bytes 98336 | tf_op jit(solution)/shard_map/ppermute | solution.py:63
  81.3 1.4 copy-done
  82.7 0.9 copy-done.2
  83.6 0.9 copy-done.3
  84.6 2.9 %shard_map.153 = (f32[48,256]{1,0:T(8,128)}, bf16[192,256]{1,0:T(8,128)(2,1)S(1)}, bf16[192,256]{1,0:T(8,128)(2,1)S(1)}, bf16[192,256]{1,0:T(8,128)(2,1)S(1)}, bf16[192,256]{1,0:T(8,128)(2,1)S(1)}) custom-call(s32[2]{0:T(128)S(1)} %copy-done.5, bf16[192,256]{1,0:T(8,128)(2,1)S(1)} %get-tuple-element.129.a0, bf16[192,256]{1,0:T(8,128)(2,1)S(1)} %collective-permute-done.10.a1, ...), custom_call_target="tpu_custom_call" | custom-call | tf_op jit(solution)/shard_map/pallas_call | solution.py:373
  87.5 0.6 copy-done.4
  88.1 0.1 collective-permute-start.13
  88.2 0.3 collective-permute-start.14
  88.5 1.5 collective-permute-start.15
  90.0 3.8 %collective-permute-done.14.g2 = bf16[192,256]{1,0:T(8,128)(2,1)S(1)} collective-permute-done((bf16[192,256]{1,0:T(8,128)(2,1)S(1)}, bf16[192,256]{1,0:T(8,128)(2,1)S(1)}, u32[]{:S(2)}, u32[]{:S(2)}) %collective-permute-start.14) | collective-permute-done | bytes 98336 | tf_op jit(solution)/shard_map/ppermute | solution.py:63
  93.8 1.2 collective-permute-done.15.g3
  95.0 4.1 %collective-permute-start.16 = (f32[48,256]{1,0:T(8,128)}, f32[48,256]{1,0:T(8,128)S(1)}, u32[]{:S(2)}, u32[]{:S(2)}) collective-permute-start(f32[48,256]{1,0:T(8,128)} %get-tuple-element.102), channel_id=1, source_target_pairs={{0,28},{4,24},{8,20},{12,16},{16,12},{20,8},{24,4},{28,0},{1,29},{... | collective-permute-start | bytes 147464 | tf_op jit(solution)/shard_map/ppermute | solution.py:59
  99.1 4.0 %shard_map.154 = (f32[4,192,256]{2,1,0:T(8,128)}, bf16[2,192,1024]{2,1,0:T(8,128)(2,1)}) custom-call(s32[128]{0:T(128)} %pad.4.table_ref, bf16[192,1024]{1,0:T(8,128)(2,1)} %q_ref.17, bf16[192,1024]{1,0:T(8,128)(2,1)} %get-tuple-element.82.att_ref, f32[4,8,256]{2,1,0:T(8,128)} %get-tuple-element.83.lse_any, bf16[192,256]{1,0:T(8,128)(2,1)} %copy-done.4, ...), custom_call_target="tpu_custom_call" | custom-call | flops 1000000000 | bytes 8388608 | tf_op jit(solution)/shard_map/pallas_call | solution.py:491
  103.1 0.0 copy-start.13
  103.1 0.6 copy-done.13
  103.7 2.7 %collective-permute-start.17 = (bf16[2,192,1024]{2,1,0:T(8,128)(2,1)}, bf16[2,192,1024]{2,1,0:T(8,128)(2,1)S(1)}, u32[]{:S(2)}, u32[]{:S(2)}) collective-permute-start(bf16[2,192,1024]{2,1,0:T(8,128)(2,1)} %get-tuple-element.103), channel_id=1, source_target_pairs={{0,4},{4,0},{8,12},{12,8},{16,20},{20,16},{24,28},{28,24},{1,5},{5... | collective-permute-start | bytes 2359304 | tf_op jit(solution)/shard_map/ppermute | solution.py:46
  106.4 7.7 %shard_map.155 = (f32[4,192,256]{2,1,0:T(8,128)}, bf16[2,192,1024]{2,1,0:T(8,128)(2,1)}, bf16[2,192,1024]{2,1,0:T(8,128)(2,1)}) custom-call(s32[128]{0:T(128)} %pad.4.table_ref, bf16[192,1024]{1,0:T(8,128)(2,1)} %q_ref.17, bf16[192,1024]{1,0:T(8,128)(2,1)} %get-tuple-element.82.att_ref, f32[4,8,256]{2,1,0:T(8,128)} %get-tuple-element.83.lse_any, ...), custom_call_target="tpu_custom_call" | custom-call | flops 1000000000 | bytes 8388608 | tf_op jit(solution)/shard_map/pallas_call | solution.py:491
  114.2 0.1 collective-permute-start.18
  114.2 10.7 %collective-permute-done.17 = bf16[2,192,1024]{2,1,0:T(8,128)(2,1)S(1)} collective-permute-done((bf16[2,192,1024]{2,1,0:T(8,128)(2,1)}, bf16[2,192,1024]{2,1,0:T(8,128)(2,1)S(1)}, u32[]{:S(2)}, u32[]{:S(2)}) %collective-permute-start.17) | collective-permute-done | bytes 786464 | tf_op jit(solution)/shard_map/ppermute | solution.py:46
  125.0 2.1 %select_add_fusion = bf16[2,192,1024]{2,1,0:T(8,128)(2,1)} fusion(bf16[2,192,1024]{2,1,0:T(8,128)(2,1)} %get-tuple-element.100, bf16[2,192,1024]{2,1,0:T(8,128)(2,1)S(1)} %collective-permute-done.17, pred[]{:T(512)S(6)} %eq.5), kind=kLoop, calls=%fused_computation.4 | loop fusion | flops 786432 | bytes 2359297 | tf_op jit(solution)/shard_map/add | solution.py:576
  127.1 8.5 %collective-permute-start.19 = (bf16[2,192,1024]{2,1,0:T(8,128)(2,1)}, bf16[2,192,1024]{2,1,0:T(8,128)(2,1)}, u32[]{:S(2)}, u32[]{:S(2)}) collective-permute-start(bf16[2,192,1024]{2,1,0:T(8,128)(2,1)} %select_add_fusion), channel_id=1, source_target_pairs={{8,0},{12,4},{16,8},{20,12},{24,16},{28,20},{9,1},{13,5},{17,9},{2... | collective-permute-start | bytes 2359304 | tf_op jit(solution)/shard_map/ppermute | solution.py:42
  135.6 1.7 shard_map.157.p0
  137.2 0.3 collective-permute-start.21
  137.6 1.5 collective-permute-start.20
  139.1 3.9 %shard_map.156 = (f32[4,192,256]{2,1,0:T(8,128)}, bf16[2,192,1024]{2,1,0:T(8,128)(2,1)}) custom-call(s32[128]{0:T(128)} %pad.4.table_ref, bf16[192,1024]{1,0:T(8,128)(2,1)} %q_ref.17, bf16[192,1024]{1,0:T(8,128)(2,1)} %get-tuple-element.82.att_ref, f32[4,8,256]{2,1,0:T(8,128)} %get-tuple-element.83.lse_any, bf16[192,256]{1,0:T(8,128)(2,1)} %copy-done.4, ...), custom_call_target="tpu_custom_call" | custom-call | flops 1000000000 | bytes 8388608 | tf_op jit(solution)/shard_map/pallas_call | solution.py:491
  143.0 8.6 %collective-permute-done.19 = bf16[2,192,1024]{2,1,0:T(8,128)(2,1)} collective-permute-done((bf16[2,192,1024]{2,1,0:T(8,128)(2,1)}, bf16[2,192,1024]{2,1,0:T(8,128)(2,1)}, u32[]{:S(2)}, u32[]{:S(2)}) %collective-permute-start.19) | collective-permute-done | bytes 786464 | tf_op jit(solution)/shard_map/ppermute | solution.py:42
  151.6 2.4 %add_add_fusion = bf16[2,192,1024]{2,1,0:T(8,128)(2,1)} fusion(bf16[2,192,1024]{2,1,0:T(8,128)(2,1)} %collective-permute-done.19, bf16[2,192,1024]{2,1,0:T(8,128)(2,1)} %get-tuple-element.107, bf16[2,192,1024]{2,1,0:T(8,128)(2,1)} %collective-permute-done.18, bf16[2,192,1024]{2,1,0:T(8,128)(2,1)S(1)} %collective-permute-done.17, pred[]{:T(512)S(6)} %eq.5), kind=kLoop, calls=%fused_computation.3 | loop fusion | flops 1179648 | bytes 3932161 | tf_op jit(solution)/shard_map/add | solution.py:582
  154.1 4.4 %collective-permute-start.23 = (bf16[2,192,1024]{2,1,0:T(8,128)(2,1)}, bf16[2,192,1024]{2,1,0:T(8,128)(2,1)S(1)}, u32[]{:S(2)}, u32[]{:S(2)}) collective-permute-start(bf16[2,192,1024]{2,1,0:T(8,128)(2,1)} %add_add_fusion), channel_id=1, source_target_pairs={{8,0},{12,4},{16,8},{20,12},{24,16},{28,20},{9,1},{13,5},{17,9},{2... | collective-permute-start | bytes 2359304 | tf_op jit(solution)/shard_map/ppermute | solution.py:42
  158.5 8.3 %shard_map.158 = (bf16[192,1024]{1,0:T(8,128)(2,1)}, f32[2,192,1024]{2,1,0:T(8,128)}) custom-call(s32[128]{0:T(128)} %pad.4.table_ref, bf16[192,1024]{1,0:T(8,128)(2,1)} %q_ref.17, bf16[192,1024]{1,0:T(8,128)(2,1)} %get-tuple-element.82.att_ref, f32[4,8,256]{2,1,0:T(8,128)} %get-tuple-element.83.lse_any, bf16[192,256]{1,0:T(8,128)(2,1)} %copy-done.4, ...), custom_call_target="tpu_custom_call" | custom-call | flops 1000000000 | bytes 8388608 | tf_op jit(solution)/shard_map/pallas_call | solution.py:491
  166.8 1.6 shard_map.159
  168.4 12.3 %collective-permute-done.23 = bf16[2,192,1024]{2,1,0:T(8,128)(2,1)S(1)} collective-permute-done((bf16[2,192,1024]{2,1,0:T(8,128)(2,1)}, bf16[2,192,1024]{2,1,0:T(8,128)(2,1)S(1)}, u32[]{:S(2)}, u32[]{:S(2)}) %collective-permute-start.23) | collective-permute-done | bytes 786464 | tf_op jit(solution)/shard_map/ppermute | solution.py:42
  180.7 2.8 %fusion.1 = (bf16[192,1024]{1,0:T(8,128)(2,1)}, bf16[192,1024]{1,0:T(8,128)(2,1)}) fusion(f32[2,192,1024]{2,1,0:T(8,128)} %get-tuple-element.122, bf16[2,192,1024]{2,1,0:T(8,128)(2,1)S(1)} %collective-permute-done.23, bf16[2,192,1024]{2,1,0:T(8,128)(2,1)} %collective-permute-done.18, pred[]{:T(512)S(6)} %eq.5), kind=kLoop, calls=%fused_computation.6 | loop fusion | flops 2359296 | bytes 3932161 | tf_op jit(solution)/shard_map/add | solution.py:589
  (43 shorter events, 0.1 us)
Async XLA Ops:
  0.6 4.7 %copy-start.16 = (s32[4,16]{1,0:T(4,128)S(1)}, s32[4,16]{1,0:T(4,128)}, u32[]{:S(2)}) copy-start(s32[4,16]{1,0:T(4,128)} %param.15) | copy-start | bytes 772
  0.6 4.8 %copy-start.17 = (s32[4]{0:T(128)S(1)}, s32[4]{0:T(128)}, u32[]{:S(2)}) copy-start(s32[4]{0:T(128)} %param.16) | copy-start | bytes 52
  1.9 4.2 %copy-start.6 = (bf16[2,192,1024]{2,1,0:T(8,128)(2,1)}, bf16[2,192,1024]{2,1,0:T(8,128)(2,1)S(1)}, u32[]{:S(2)}) copy-start(bf16[2,192,1024]{2,1,0:T(8,128)(2,1)S(1)} %pad_maximum_fusion.refs_0_) | copy-start | bytes 2359300
  1.9 21.3 %collective-permute-start = (bf16[2,192,1024]{2,1,0:T(8,128)(2,1)S(1)}, bf16[2,192,1024]{2,1,0:T(8,128)(2,1)}, u32[]{:S(2)}, u32[]{:S(2)}) collective-permute-start(bf16[2,192,1024]{2,1,0:T(8,128)(2,1)S(1)} %pad_maximum_fusion.refs_0_), channel_id=1, source_target_pairs={{0,8},{4,12},{8,16},{12,20},{16,24},{20,28},{1,9},{5,13},{9,17},{1... | collective-permute-start | bytes 2359304 | tf_op jit(solution)/shard_map/ppermute | solution.py:42
  23.1 22.1 %copy-start.1 = (bf16[192,768]{1,0:T(8,128)(2,1)S(1)}, bf16[192,768]{1,0:T(8,128)(2,1)}, u32[]{:S(2)}) copy-start(bf16[192,768]{1,0:T(8,128)(2,1)} %w0) | copy-start | bytes 884740
  23.1 20.7 %collective-permute-start.1 = (bf16[2,192,1024]{2,1,0:T(8,128)(2,1)}, bf16[2,192,1024]{2,1,0:T(8,128)(2,1)}, u32[]{:S(2)}, u32[]{:S(2)}) collective-permute-start(bf16[2,192,1024]{2,1,0:T(8,128)(2,1)} %collective-permute-done.refs_0_), channel_id=1, source_target_pairs={{0,8},{4,12},{8,16},{12,20},{16,24},{20,28},{1,9},{5,13},{9,17},{1... | collective-permute-start | bytes 2359304 | tf_op jit(solution)/shard_map/ppermute | solution.py:42
  26.8 21.7 %collective-permute-start.5 = (bf16[2,192,1024]{2,1,0:T(8,128)(2,1)}, bf16[2,192,1024]{2,1,0:T(8,128)(2,1)}, u32[]{:S(2)}, u32[]{:S(2)}) collective-permute-start(bf16[2,192,1024]{2,1,0:T(8,128)(2,1)} %copy-done.6), channel_id=1, source_target_pairs={{0,4},{8,12},{16,20},{24,28},{1,5},{9,13},{17,21},{25,29},{2,6},{1... | collective-permute-start | bytes 2359304 | tf_op jit(solution)/shard_map/ppermute | solution.py:50
  31.1 22.7 %collective-permute-start.4 = (bf16[2,192,1024]{2,1,0:T(8,128)(2,1)}, bf16[2,192,1024]{2,1,0:T(8,128)(2,1)}, u32[]{:S(2)}, u32[]{:S(2)}) collective-permute-start(bf16[2,192,1024]{2,1,0:T(8,128)(2,1)} %collective-permute-done.refs_0_), channel_id=1, source_target_pairs={{4,0},{12,8},{20,16},{28,24},{5,1},{13,9},{21,17},{29,25},{6,2},{1... | collective-permute-start | bytes 2359304 | tf_op jit(solution)/shard_map/ppermute | solution.py:54
  32.4 30.6 %collective-permute-start.3 = (bf16[2,192,1024]{2,1,0:T(8,128)(2,1)}, bf16[2,192,1024]{2,1,0:T(8,128)(2,1)}, u32[]{:S(2)}, u32[]{:S(2)}) collective-permute-start(bf16[2,192,1024]{2,1,0:T(8,128)(2,1)} %collective-permute-done.refs_0_), channel_id=1, source_target_pairs={{0,4},{8,12},{16,20},{24,28},{1,5},{9,13},{17,21},{25,29},{2,6},{1... | collective-permute-start | bytes 2359304 | tf_op jit(solution)/shard_map/ppermute | solution.py:50
  43.9 25.9 %collective-permute-start.2 = (bf16[2,192,1024]{2,1,0:T(8,128)(2,1)}, bf16[2,192,1024]{2,1,0:T(8,128)(2,1)}, u32[]{:S(2)}, u32[]{:S(2)}) collective-permute-start(bf16[2,192,1024]{2,1,0:T(8,128)(2,1)} %collective-permute-done.1.refs_0_), channel_id=1, source_target_pairs={{4,0},{12,8},{20,16},{28,24},{5,1},{13,9},{21,17},{29,25},{6,2},{1... | collective-permute-start | bytes 2359304 | tf_op jit(solution)/shard_map/ppermute | solution.py:54
  45.2 24.5 %collective-permute-start.9 = (bf16[192,768]{1,0:T(8,128)(2,1)S(1)}, bf16[192,768]{1,0:T(8,128)(2,1)S(1)}, u32[]{:S(2)}, u32[]{:S(2)}) collective-permute-start(bf16[192,768]{1,0:T(8,128)(2,1)S(1)} %copy-done.1), channel_id=1, source_target_pairs={{0,3},{1,2},{2,1},{3,0},{4,7},{5,6},{6,5},{7,4},{8,11},{9,10},{10,... | collective-permute-start | bytes 884744 | tf_op jit(solution)/shard_map/ppermute | solution.py:63
  48.5 21.2 %collective-permute-start.8 = (bf16[192,768]{1,0:T(8,128)(2,1)S(1)}, bf16[192,768]{1,0:T(8,128)(2,1)S(1)}, u32[]{:S(2)}, u32[]{:S(2)}) collective-permute-start(bf16[192,768]{1,0:T(8,128)(2,1)S(1)} %copy-done.1), channel_id=1, source_target_pairs={{0,2},{1,3},{2,0},{3,1},{4,6},{5,7},{6,4},{7,5},{8,10},{9,11},{10,... | collective-permute-start | bytes 884744 | tf_op jit(solution)/shard_map/ppermute | solution.py:63
  53.8 16.0 %collective-permute-start.7 = (bf16[192,768]{1,0:T(8,128)(2,1)S(1)}, bf16[192,768]{1,0:T(8,128)(2,1)}, u32[]{:S(2)}, u32[]{:S(2)}) collective-permute-start(bf16[192,768]{1,0:T(8,128)(2,1)S(1)} %copy-done.1), channel_id=1, source_target_pairs={{0,1},{1,0},{2,3},{3,2},{4,5},{5,4},{6,7},{7,6},{8,9},{9,8},{10,11... | collective-permute-start | bytes 884744 | tf_op jit(solution)/shard_map/ppermute | solution.py:63
  56.3 6.7 %copy-start.14 = (f32[48,256]{1,0:T(8,128)S(1)}, f32[48,256]{1,0:T(8,128)}, u32[]{:S(2)}) copy-start(f32[48,256]{1,0:T(8,128)} %shard_map.151) | copy-start | bytes 147460
  63.0 6.7 %collective-permute-start.6 = (f32[48,256]{1,0:T(8,128)S(1)}, f32[48,256]{1,0:T(8,128)S(1)}, u32[]{:S(2)}, u32[]{:S(2)}) collective-permute-start(f32[48,256]{1,0:T(8,128)S(1)} %copy-done.14), channel_id=1, source_target_pairs={{0,28},{4,24},{8,20},{12,16},{16,12},{20,8},{24,4},{28,0},{1,29},{... | collective-permute-start | bytes 147464 | tf_op jit(solution)/shard_map/ppermute | solution.py:59
  69.8 6.2 %copy-start.15 = (f32[768]{0:T(1024)S(1)}, f32[768]{0:T(1024)}, u32[]{:S(2)}) copy-start(f32[768]{0:T(1024)} %param.19) | copy-start | bytes 9220
  69.8 11.5 %copy-start.5 = (s32[2]{0:T(128)S(1)}, s32[2]{0:T(128)}, u32[]{:S(2)}) copy-start(s32[2]{0:T(128)} %pad_add_fusion.place_ref) | copy-start | bytes 28
  74.0 5.1 %collective-permute-start.12 = (bf16[192,256]{1,0:T(8,128)(2,1)S(1)}, bf16[192,256]{1,0:T(8,128)(2,1)S(1)}, u32[]{:S(2)}, u32[]{:S(2)}) collective-permute-start(bf16[192,256]{1,0:T(8,128)(2,1)S(1)} %get-tuple-element.126), channel_id=1, source_target_pairs={{0,3},{1,2},{2,1},{3,0},{4,7},{5,6},{6,5},{7,4},{8,11},{9,10},{10,... | collective-permute-start | bytes 294920 | tf_op jit(solution)/shard_map/ppermute | solution.py:63
  74.1 7.2 %collective-permute-start.11 = (bf16[192,256]{1,0:T(8,128)(2,1)S(1)}, bf16[192,256]{1,0:T(8,128)(2,1)S(1)}, u32[]{:S(2)}, u32[]{:S(2)}) collective-permute-start(bf16[192,256]{1,0:T(8,128)(2,1)S(1)} %get-tuple-element.127), channel_id=1, source_target_pairs={{0,2},{1,3},{2,0},{3,1},{4,6},{5,7},{6,4},{7,5},{8,10},{9,11},{10,... | collective-permute-start | bytes 294920 | tf_op jit(solution)/shard_map/ppermute | solution.py:63
  75.7 5.6 %collective-permute-start.10 = (bf16[192,256]{1,0:T(8,128)(2,1)S(1)}, bf16[192,256]{1,0:T(8,128)(2,1)S(1)}, u32[]{:S(2)}, u32[]{:S(2)}) collective-permute-start(bf16[192,256]{1,0:T(8,128)(2,1)S(1)} %get-tuple-element.128), channel_id=1, source_target_pairs={{0,1},{1,0},{2,3},{3,2},{4,5},{5,4},{6,7},{7,6},{8,9},{9,8},{10,11... | collective-permute-start | bytes 294920 | tf_op jit(solution)/shard_map/ppermute | solution.py:63
  81.3 1.4 copy-start
  82.7 0.9 copy-start.2
  83.6 0.9 copy-start.3
  87.5 0.6 copy-start.4
  88.1 1.9 %collective-permute-start.13 = (bf16[192,256]{1,0:T(8,128)(2,1)S(1)}, bf16[192,256]{1,0:T(8,128)(2,1)S(1)}, u32[]{:S(2)}, u32[]{:S(2)}) collective-permute-start(bf16[192,256]{1,0:T(8,128)(2,1)S(1)} %get-tuple-element.90), channel_id=1, source_target_pairs={{0,1},{1,0},{2,3},{3,2},{4,5},{5,4},{6,7},{7,6},{8,9},{9,8},{10,11... | collective-permute-start | bytes 294920 | tf_op jit(solution)/shard_map/ppermute | solution.py:63
  88.2 5.6 %collective-permute-start.14 = (bf16[192,256]{1,0:T(8,128)(2,1)S(1)}, bf16[192,256]{1,0:T(8,128)(2,1)S(1)}, u32[]{:S(2)}, u32[]{:S(2)}) collective-permute-start(bf16[192,256]{1,0:T(8,128)(2,1)S(1)} %get-tuple-element.91), channel_id=1, source_target_pairs={{0,2},{1,3},{2,0},{3,1},{4,6},{5,7},{6,4},{7,5},{8,10},{9,11},{10,... | collective-permute-start | bytes 294920 | tf_op jit(solution)/shard_map/ppermute | solution.py:63
  88.5 6.4 %collective-permute-start.15 = (bf16[192,256]{1,0:T(8,128)(2,1)S(1)}, bf16[192,256]{1,0:T(8,128)(2,1)S(1)}, u32[]{:S(2)}, u32[]{:S(2)}) collective-permute-start(bf16[192,256]{1,0:T(8,128)(2,1)S(1)} %get-tuple-element.92), channel_id=1, source_target_pairs={{0,3},{1,2},{2,1},{3,0},{4,7},{5,6},{6,5},{7,4},{8,11},{9,10},{10,... | collective-permute-start | bytes 294920 | tf_op jit(solution)/shard_map/ppermute | solution.py:63
  90.0 9.1 %copy-start.7 = (bf16[192,256]{1,0:T(8,128)(2,1)}, bf16[192,256]{1,0:T(8,128)(2,1)S(1)}, u32[]{:S(2)}) copy-start(bf16[192,256]{1,0:T(8,128)(2,1)S(1)} %collective-permute-done.13.g1) | copy-start | bytes 294916
  93.8 5.3 %copy-start.8 = (bf16[192,256]{1,0:T(8,128)(2,1)}, bf16[192,256]{1,0:T(8,128)(2,1)S(1)}, u32[]{:S(2)}) copy-start(bf16[192,256]{1,0:T(8,128)(2,1)S(1)} %collective-permute-done.14.g2) | copy-start | bytes 294916
  95.0 4.1 %copy-start.9 = (bf16[192,256]{1,0:T(8,128)(2,1)}, bf16[192,256]{1,0:T(8,128)(2,1)S(1)}, u32[]{:S(2)}) copy-start(bf16[192,256]{1,0:T(8,128)(2,1)S(1)} %collective-permute-done.15.g3) | copy-start | bytes 294916
  95.0 8.1 %collective-permute-start.16 = (f32[48,256]{1,0:T(8,128)}, f32[48,256]{1,0:T(8,128)S(1)}, u32[]{:S(2)}, u32[]{:S(2)}) collective-permute-start(f32[48,256]{1,0:T(8,128)} %get-tuple-element.102), channel_id=1, source_target_pairs={{0,28},{4,24},{8,20},{12,16},{16,12},{20,8},{24,4},{28,0},{1,29},{... | collective-permute-start | bytes 147464 | tf_op jit(solution)/shard_map/ppermute | solution.py:59
  103.1 0.6 copy-start.13
  103.7 21.3 %collective-permute-start.17 = (bf16[2,192,1024]{2,1,0:T(8,128)(2,1)}, bf16[2,192,1024]{2,1,0:T(8,128)(2,1)S(1)}, u32[]{:S(2)}, u32[]{:S(2)}) collective-permute-start(bf16[2,192,1024]{2,1,0:T(8,128)(2,1)} %get-tuple-element.103), channel_id=1, source_target_pairs={{0,4},{4,0},{8,12},{12,8},{16,20},{20,16},{24,28},{28,24},{1,5},{5... | collective-permute-start | bytes 2359304 | tf_op jit(solution)/shard_map/ppermute | solution.py:46
  114.2 28.9 %collective-permute-start.18 = (bf16[2,192,1024]{2,1,0:T(8,128)(2,1)}, bf16[2,192,1024]{2,1,0:T(8,128)(2,1)}, u32[]{:S(2)}, u32[]{:S(2)}) collective-permute-start(bf16[2,192,1024]{2,1,0:T(8,128)(2,1)} %get-tuple-element.108), channel_id=1, source_target_pairs={{0,4},{4,0},{8,12},{12,8},{16,20},{20,16},{24,28},{28,24},{1,5},{5... | collective-permute-start | bytes 2359304 | tf_op jit(solution)/shard_map/ppermute | solution.py:46
  127.1 24.5 %collective-permute-start.19 = (bf16[2,192,1024]{2,1,0:T(8,128)(2,1)}, bf16[2,192,1024]{2,1,0:T(8,128)(2,1)}, u32[]{:S(2)}, u32[]{:S(2)}) collective-permute-start(bf16[2,192,1024]{2,1,0:T(8,128)(2,1)} %select_add_fusion), channel_id=1, source_target_pairs={{8,0},{12,4},{16,8},{20,12},{24,16},{28,20},{9,1},{13,5},{17,9},{2... | collective-permute-start | bytes 2359304 | tf_op jit(solution)/shard_map/ppermute | solution.py:42
  137.2 16.8 %collective-permute-start.22 = (f32[48,256]{1,0:T(8,128)}, f32[48,256]{1,0:T(8,128)S(1)}, u32[]{:S(2)}, u32[]{:S(2)}) collective-permute-start(f32[48,256]{1,0:T(8,128)} %shard_map.157.p0), channel_id=1, source_target_pairs={{0,3},{1,2},{2,1},{3,0},{4,7},{5,6},{6,5},{7,4},{8,11},{9,10},{10,... | collective-permute-start | bytes 147464 | tf_op jit(solution)/shard_map/ppermute | solution.py:63
  137.2 16.8 %collective-permute-start.21 = (f32[48,256]{1,0:T(8,128)}, f32[48,256]{1,0:T(8,128)S(1)}, u32[]{:S(2)}, u32[]{:S(2)}) collective-permute-start(f32[48,256]{1,0:T(8,128)} %shard_map.157.p0), channel_id=1, source_target_pairs={{0,2},{1,3},{2,0},{3,1},{4,6},{5,7},{6,4},{7,5},{8,10},{9,11},{10,... | collective-permute-start | bytes 147464 | tf_op jit(solution)/shard_map/ppermute | solution.py:63
  137.6 16.5 %collective-permute-start.20 = (f32[48,256]{1,0:T(8,128)}, f32[48,256]{1,0:T(8,128)S(1)}, u32[]{:S(2)}, u32[]{:S(2)}) collective-permute-start(f32[48,256]{1,0:T(8,128)} %shard_map.157.p0), channel_id=1, source_target_pairs={{0,1},{1,0},{2,3},{3,2},{4,5},{5,4},{6,7},{7,6},{8,9},{9,8},{10,11... | collective-permute-start | bytes 147464 | tf_op jit(solution)/shard_map/ppermute | solution.py:63
  154.0 12.7 %copy-start.10 = (f32[48,256]{1,0:T(8,128)}, f32[48,256]{1,0:T(8,128)S(1)}, u32[]{:S(2)}) copy-start(f32[48,256]{1,0:T(8,128)S(1)} %collective-permute-done.22.p3) | copy-start | bytes 147460
  154.1 12.7 %copy-start.11 = (f32[48,256]{1,0:T(8,128)}, f32[48,256]{1,0:T(8,128)S(1)}, u32[]{:S(2)}) copy-start(f32[48,256]{1,0:T(8,128)S(1)} %collective-permute-done.21.p2) | copy-start | bytes 147460
  154.1 12.7 %copy-start.12 = (f32[48,256]{1,0:T(8,128)}, f32[48,256]{1,0:T(8,128)S(1)}, u32[]{:S(2)}) copy-start(f32[48,256]{1,0:T(8,128)S(1)} %collective-permute-done.20.p1) | copy-start | bytes 147460
  154.1 26.6 %collective-permute-start.23 = (bf16[2,192,1024]{2,1,0:T(8,128)(2,1)}, bf16[2,192,1024]{2,1,0:T(8,128)(2,1)S(1)}, u32[]{:S(2)}, u32[]{:S(2)}) collective-permute-start(bf16[2,192,1024]{2,1,0:T(8,128)(2,1)} %add_add_fusion), channel_id=1, source_target_pairs={{8,0},{12,4},{16,8},{20,12},{24,16},{28,20},{9,1},{13,5},{17,9},{2... | collective-permute-start | bytes 2359304 | tf_op jit(solution)/shard_map/ppermute | solution.py:42
